TPU v7x, 32 devices: a whole 2x2x4 slice. The times are simulated.
32 devices in a mesh: fsdp: 4 (over x, core), expert: 8 (over z, y).
Axes of the slice: x: 2, y: 2, z: 4, core: 2. Of those that a mesh axis runs over, the one named last changes fastest.
Arguments:
- tokens: bfloat16 [4096, 768], P(('fsdp', 'expert')), may hold values from -6 to 6
- cotangent: bfloat16 [4096, 768], P(('fsdp', 'expert')), may hold values from -6 to 6
- project_in: bfloat16 [768, 2304], P(('fsdp', 'expert')), may hold values from -0.21875 to 0.21875
- project_out: bfloat16 [768, 768], P(('fsdp', 'expert')), may hold values from -0.875 to 0.875
- router: bfloat16 [768, 8], P(('fsdp', 'expert')), may hold values from -0.14941406 to 0.14941406
- first_gain: bfloat16 [768], P(('fsdp', 'expert')), may hold values from 0.5 to 1.5
- second_gain: bfloat16 [768], P(('fsdp', 'expert')), may hold values from 0.5 to 1.5
- bias_table: float32 [32, 12], replicated, may hold values from -4 to 4
- expert_up: bfloat16 [8, 768, 3072], P('expert', None, 'fsdp'), may hold values from -0.21875 to 0.21875
- expert_down: bfloat16 [8, 3072, 768], P('expert', 'fsdp'), may hold values from -0.109375 to 0.109375
- positions: int32 [4096], P(('fsdp', 'expert')), may hold values from 0 to 127, as said below
- buckets: int32 [128], replicated, may hold values from 0 to 31, as said below
- routes: int32 [4096, 2], P(('fsdp', 'expert')), may hold values from 0 to 7, as said below
- slots: int32 [4096, 2], P(('fsdp', 'expert')), may hold values from 0 to 47, as said below
Outputs:
- mixed: bfloat16 [4096, 768], P(('fsdp', 'expert'))
- grad_tokens: bfloat16 [4096, 768], P(('fsdp', 'expert'))
- grad_project_in: float32 [768, 2304], P(('fsdp', 'expert'))
- grad_project_out: float32 [768, 768], P(('fsdp', 'expert'))
- grad_router: float32 [768, 8], P(('fsdp', 'expert'))
- grad_first_gain: float32 [768], P(('fsdp', 'expert'))
- grad_second_gain: float32 [768], P(('fsdp', 'expert'))
- grad_bias_table: float32 [32, 12], replicated
- grad_expert_up: float32 [8, 768, 3072], P('expert', None, 'fsdp')
- grad_expert_down: float32 [8, 3072, 768], P('expert', 'fsdp')
Inputs may be any that keep to these rules, and one draw needn't show every extreme that they name: `positions`: each device's tokens hold whole sequences in order: a position is 0 at a sequence's first token and rises by one along it. `buckets`: 0 at distance 0, never falling with the distance. `routes`: the two experts of a token differ; the tokens of one device name no expert more than 48 times. routes of one device to one expert have different slots.
All inputs are finite; a program needn't handle non-finite values.
Results may differ from a plain program's by a relative error of at most 0.015.
Values may be sent and summed in bfloat16 or wider, within the bound.
No kernel may reach another device: no remote copies, remote signals or barrier semaphores. Data moves between devices by JAX's collectives and lax.ppermute only.
A program may use at most 128 MiB of HBM per device.

v0:
```python
import jax
import jax.numpy as jnp
from jax import lax
from jax.sharding import PartitionSpec as P

HEADS = 12
HEAD = 64
BUCKETS = 32


def rms_scale(value, gain):
    return value * lax.rsqrt(jnp.mean(value * value, axis=-1, keepdims=True) + 1e-06) * gain


def contract_rows(left, right):
    return lax.dot_general(
        left, right, (((0,), (0,)), ((), ())), preferred_element_type=jnp.float32
    )


def contract_cols(left, right):
    return lax.dot_general(
        left, right, (((1,), (1,)), ((), ())), preferred_element_type=jnp.float32
    )


def on_device(
    tokens,
    cotangent,
    project_in,
    project_out,
    router,
    first_gain,
    second_gain,
    bias_table,
    expert_up,
    expert_down,
    positions,
    buckets,
    routes,
    slots,
):
    highest = lax.Precision.HIGHEST
    count, width = tokens.shape
    experts = lax.axis_size("expert")
    capacity = 3 * count // experts
    rows_here = experts * capacity
    gathered = (
        lax.all_gather(project_in, ("fsdp", "expert"), axis=0, tiled=True),
        lax.all_gather(project_out, ("fsdp", "expert"), axis=0, tiled=True),
        lax.all_gather(router, ("fsdp", "expert"), axis=0, tiled=True),
        lax.all_gather(first_gain, ("fsdp", "expert"), axis=0, tiled=True),
        lax.all_gather(second_gain, ("fsdp", "expert"), axis=0, tiled=True),
    )
    triple_weight, output_weight, router_matrix = (gathered[0], gathered[1], gathered[2])
    gain_first = gathered[3].astype(jnp.float32)
    gain_second = gathered[4].astype(jnp.float32)
    inputs = tokens.astype(jnp.float32)
    normed_low = rms_scale(inputs, gain_first).astype(jnp.bfloat16)
    joint = jnp.dot(normed_low, triple_weight, preferred_element_type=jnp.float32).astype(
        jnp.bfloat16
    )
    query = joint[:, :width].reshape(count, HEADS, HEAD)
    keys_low = joint[:, width : 2 * width].reshape(count, HEADS, HEAD)
    values_low = joint[:, 2 * width :].reshape(count, HEADS, HEAD)
    places = jnp.arange(count, dtype=jnp.int32)
    distance = places[:, None] - places[None, :]
    valid = (distance >= 0) & (distance <= positions[:, None])
    bucket_pair = jnp.take(buckets, jnp.clip(distance, 0, count - 1))
    bucket_hot = (bucket_pair[:, :, None] == jnp.arange(BUCKETS, dtype=jnp.int32)).astype(
        jnp.float32
    )
    bias = jnp.einsum("qkb,bh->hqk", bucket_hot, bias_table, precision=highest)

    def scores_of():
        raw = jnp.einsum("qhd,khd->hqk", query, keys_low, preferred_element_type=jnp.float32)
        return jnp.where(valid[None], raw * 0.125 + bias, -1e30)

    scores = scores_of()
    top = jnp.max(scores, axis=-1, keepdims=True)
    log_total = top + jnp.log(jnp.sum(jnp.exp(scores - top), axis=-1, keepdims=True))
    probs_low = jnp.exp(scores - log_total).astype(jnp.bfloat16)
    attended = (
        jnp.einsum("hqk,khd->qhd", probs_low, values_low, preferred_element_type=jnp.float32)
        .astype(jnp.bfloat16)
        .reshape(count, width)
    )
    first = inputs + jnp.dot(attended, output_weight, preferred_element_type=jnp.float32)
    second_low = rms_scale(first, gain_second).astype(jnp.bfloat16)
    logits = jnp.dot(second_low, router_matrix, preferred_element_type=jnp.float32)
    route_hot = (routes[:, :, None] == jnp.arange(experts, dtype=jnp.int32)).astype(jnp.float32)
    chosen = jnp.sum(logits[:, None, :] * route_hot, axis=-1)
    gates = jax.nn.softmax(chosen, axis=1)
    target = routes * capacity + slots
    place_hot = (jnp.arange(rows_here, dtype=jnp.int32)[:, None, None] == target[None]).astype(
        jnp.bfloat16
    )
    outgoing = jnp.einsum(
        "stc,td->sd", place_hot, second_low, preferred_element_type=jnp.float32
    ).astype(jnp.bfloat16)
    received = lax.all_to_all(
        outgoing.reshape(experts, capacity, width),
        "expert",
        split_axis=0,
        concat_axis=0,
        tiled=True,
    ).reshape(rows_here, width)
    piece = lax.all_gather(received, "fsdp", axis=0, tiled=True)
    inner = jnp.dot(piece, expert_up[0], preferred_element_type=jnp.float32)
    rows_all = piece
    inner_all = inner
    active_all = jax.nn.gelu(inner).astype(jnp.bfloat16)
    results = lax.psum_scatter(
        jnp.dot(active_all, expert_down[0], preferred_element_type=jnp.float32).astype(
            jnp.bfloat16
        ),
        "fsdp",
        scatter_dimension=0,
        tiled=True,
    )
    returned = lax.all_to_all(
        results.reshape(experts, capacity, width), "expert", split_axis=0, concat_axis=0, tiled=True
    ).reshape(rows_here, width)
    routed = jnp.einsum("stc,sd->tcd", place_hot, returned, preferred_element_type=jnp.float32)
    mixed = (first + jnp.sum(gates[:, :, None] * routed, axis=1)).astype(jnp.bfloat16)
    upstream = cotangent.astype(jnp.float32)
    gate_grad = jnp.sum(upstream[:, None, :] * routed, axis=-1)
    route_grad = (gates[:, :, None] * upstream[:, None, :]).astype(jnp.bfloat16)
    result_grad = jnp.einsum(
        "stc,tcd->sd", place_hot, route_grad, preferred_element_type=jnp.float32
    ).astype(jnp.bfloat16)
    arrived = lax.all_to_all(
        result_grad.reshape(experts, capacity, width),
        "expert",
        split_axis=0,
        concat_axis=0,
        tiled=True,
    ).reshape(rows_here, width)
    piece = lax.all_gather(arrived, "fsdp", axis=0, tiled=True)
    inner = inner_all
    active_grad = contract_cols(piece, expert_down[0])
    inner_grad = jax.vjp(jax.nn.gelu, inner)[1](active_grad)[0]
    inner_grad_all = inner_grad.astype(jnp.bfloat16)
    grad_up = contract_rows(rows_all, inner_grad_all)
    grad_down = contract_rows(active_all, piece)
    row_grad = lax.psum_scatter(
        contract_cols(inner_grad_all, expert_up[0]).astype(jnp.bfloat16),
        "fsdp",
        scatter_dimension=0,
        tiled=True,
    )
    home_grad = lax.all_to_all(
        row_grad.reshape(experts, capacity, width),
        "expert",
        split_axis=0,
        concat_axis=0,
        tiled=True,
    ).reshape(rows_here, width)
    chosen_grad = gates * (gate_grad - jnp.sum(gates * gate_grad, axis=1, keepdims=True))
    logit_grad = jnp.sum(route_hot * chosen_grad[:, :, None], axis=1).astype(jnp.bfloat16)
    again = (
        lax.all_gather(project_in, ("fsdp", "expert"), axis=0, tiled=True),
        lax.all_gather(project_out, ("fsdp", "expert"), axis=0, tiled=True),
        lax.all_gather(router, ("fsdp", "expert"), axis=0, tiled=True),
    )
    triple_weight, output_weight, router_matrix = (again[0], again[1], again[2])
    second_grad = jnp.einsum(
        "stc,sd->td", place_hot, home_grad, preferred_element_type=jnp.float32
    ) + contract_cols(logit_grad, router_matrix)
    grad_router = contract_rows(second_low, logit_grad)
    branch_grad, gain_second_grad = jax.vjp(rms_scale, first, gain_second)[1](second_grad)
    first_grad = upstream + branch_grad
    first_low = first_grad.astype(jnp.bfloat16)
    grad_output = contract_rows(attended, first_low)
    attended_grad = (
        contract_cols(first_low, output_weight).astype(jnp.bfloat16).reshape(count, HEADS, HEAD)
    )
    probs = jnp.exp(scores_of() - log_total)
    prob_grad = jnp.einsum(
        "qhd,khd->hqk", attended_grad, values_low, preferred_element_type=jnp.float32
    )
    score_grad = probs * (prob_grad - jnp.sum(probs * prob_grad, axis=-1, keepdims=True))
    table_grad = jnp.einsum("qkb,hqk->bh", bucket_hot, score_grad, precision=highest)
    pair_grad = (score_grad * 0.125).astype(jnp.bfloat16)
    query_grad = jnp.einsum("hqk,khd->qhd", pair_grad, keys_low, preferred_element_type=jnp.float32)
    key_grad = jnp.einsum("hqk,qhd->khd", pair_grad, query, preferred_element_type=jnp.float32)
    value_grad = jnp.einsum(
        "hqk,qhd->khd", probs_low, attended_grad, preferred_element_type=jnp.float32
    )
    joint_grad = jnp.concatenate(
        [
            query_grad.reshape(count, width),
            key_grad.reshape(count, width),
            value_grad.reshape(count, width),
        ],
        axis=1,
    ).astype(jnp.bfloat16)
    grad_triple = contract_rows(normed_low, joint_grad)
    normed_grad = contract_cols(joint_grad, triple_weight)
    input_grad, gain_first_grad = jax.vjp(rms_scale, inputs, gain_first)[1](normed_grad)
    token_grad = (first_grad + input_grad).astype(jnp.bfloat16)
    sharded = (
        lax.psum_scatter(grad_triple, ("fsdp", "expert"), scatter_dimension=0, tiled=True),
        lax.psum_scatter(grad_output, ("fsdp", "expert"), scatter_dimension=0, tiled=True),
        lax.psum_scatter(grad_router, ("fsdp", "expert"), scatter_dimension=0, tiled=True),
        lax.psum_scatter(gain_first_grad, ("fsdp", "expert"), scatter_dimension=0, tiled=True),
        lax.psum_scatter(gain_second_grad, ("fsdp", "expert"), scatter_dimension=0, tiled=True),
    )
    table_total = lax.psum(table_grad, ("fsdp", "expert"))
    return (
        mixed,
        token_grad,
        sharded[0],
        sharded[1],
        sharded[2],
        sharded[3],
        sharded[4],
        table_total,
        grad_up[None],
        grad_down[None],
    )


def solution(mesh):
    return jax.shard_map(
        on_device,
        mesh=mesh,
        in_specs=(
            P(("fsdp", "expert"), None),
            P(("fsdp", "expert"), None),
            P(("fsdp", "expert"), None),
            P(("fsdp", "expert"), None),
            P(("fsdp", "expert"), None),
            P(("fsdp", "expert")),
            P(("fsdp", "expert")),
            P(),
            P("expert", None, "fsdp"),
            P("expert", "fsdp", None),
            P(("fsdp", "expert")),
            P(),
            P(("fsdp", "expert"), None),
            P(("fsdp", "expert"), None),
        ),
        out_specs=(
            P(("fsdp", "expert"), None),
            P(("fsdp", "expert"), None),
            P(("fsdp", "expert"), None),
            P(("fsdp", "expert"), None),
            P(("fsdp", "expert"), None),
            P(("fsdp", "expert")),
            P(("fsdp", "expert")),
            P(),
            P("expert", None, "fsdp"),
            P("expert", "fsdp", None),
        ),
        check_vma=False,
    )
```

profile of v0, /device:TPU:0, one launch (start us, length us, event | category | flops | bytes accessed | tf_op | source)
XLA Modules:
  0.0 619.8 jit_solution(18164552652386921137)
XLA Ops:
  9.6 97.2 %gather_fusion = s32[16384]{0:T(1024)S(1)} fusion(s32[128]{0:T(128)S(1)} %copy-done.1, s32[16384]{0:T(1024)S(1)} %fusion.48), kind=kCustom, calls=%fused_computation | custom fusion | bytes 196608 | tf_op jit(solution)/shard_map/jit(_take)/gather | solution.py:69
  107.4 42.0 %all-reduce.6 = (bf16[768]{0:T(1024)(128)(2,1)S(1)}, bf16[768]{0:T(1024)(128)(2,1)S(1)}) all-reduce(bf16[768]{0:T(1024)(128)(2,1)S(1)} %dynamic-update-slice, bf16[768]{0:T(1024)(128)(2,1)S(1)} %dynamic-update-slice.1), channel_id=1, replica_groups=mesh['fsdp'=4,'expert'=8] {'fsdp','expert'}, use_global_device_ids=true, to_apply=%add | all-reduce | flops 1536 | bytes 6144
  150.7 2.7 convolution_convert_fusion
  155.2 1.8 copy.80
  157.9 1.5 fusion.70
  159.8 1.8 multiply_reduce_fusion.5
  162.0 20.0 %all_to_all.20 = bf16[8,48,768]{2,1,0:T(8,128)(2,1)} all-to-all(bf16[8,48,768]{2,1,0:T(8,128)(2,1)S(1)} %bitcast.98), channel_id=1, replica_groups=mesh['fsdp'=4,'expert'=8] {'expert'}, dimensions={0} | all-to-all | bytes 1179648 | tf_op jit(solution)/shard_map/all_to_all | solution.py:101
  182.1 65.5 %all-gather = bf16[32,24,8]{1,2,0:T(8,128)(2,1)S(1)} all-gather(bf16[1,24,8]{1,2,0:T(8,128)(2,1)S(1)} %bitcast.119), channel_id=1, replica_groups=mesh['fsdp'=4,'expert'=8] {'fsdp','expert'}, dimensions={0}, use_global_device_ids=true | all-gather | bytes 12672 | tf_op jit(solution)/shard_map/all_gather | solution.py:51
  247.8 1.7 convert_element_type.94
  251.2 17.6 %all_to_all.21 = bf16[8,48,768]{2,1,0:T(8,128)(2,1)} all-to-all(bf16[8,48,768]{2,1,0:T(8,128)(2,1)S(1)} %bitcast.99), channel_id=1, replica_groups=mesh['fsdp'=4,'expert'=8] {'expert'}, dimensions={0} | all-to-all | bytes 1179648 | tf_op jit(solution)/shard_map/all_to_all | solution.py:132
  268.9 4.0 fusion.18
  272.9 2.2 copy-done.39
  275.1 4.4 convolution_convert_fusion.2
  279.8 10.9 %all-gather.12.cloned.1.call-done = bf16[1536,768]{1,0:T(8,128)(2,1)} async-done(((bf16[384,768]{1,0:T(8,128)(2,1)}), bf16[1536,768]{1,0:T(8,128)(2,1)}) %all-gather.12.cloned.1.call-update) | async-done | bytes 2359312 | tf_op jit(solution)/shard_map/all_gather | solution.py:139
  290.7 8.8 %fusion.6 = bf16[1536,768]{1,0:T(8,128)(2,1)} fusion(f32[1536,768]{1,0:T(8,128)} %copy-done.39, bf16[1536,768]{1,0:T(8,128)(2,1)} %all-gather.12.cloned.1.call-done, bf16[1,768,768]{2,1,0:T(8,128)(2,1)S(1)} %copy-done), kind=kOutput, calls=%fused_computation.9 | convolution fusion | flops 1835532288 | bytes 10616832 | tf_op jit(solution)/shard_map/dot_general | solution.py:22
  299.4 5.4 convolution_convert_fusion.1
  304.9 21.2 %reduce-scatter.6.cloned.1.call-done = bf16[384,768]{1,0:T(8,128)(2,1)} async-done(((bf16[1536,768]{1,0:T(8,128)(2,1)}), bf16[384,768]{1,0:T(8,128)(2,1)}) %reduce-scatter.6.cloned.1.call-update) | async-done | bytes 589840 | tf_op jit(solution)/shard_map/reduce_scatter | solution.py:113
  326.1 5.5 all-to-all-start.1
  331.7 30.7 %reduce-scatter.8.cloned.1.call-done = bf16[384,768]{1,0:T(8,128)(2,1)} async-done(((bf16[1536,768]{1,0:T(8,128)(2,1)}), bf16[384,768]{1,0:T(8,128)(2,1)}) %reduce-scatter.8.cloned.1.call-update) | async-done | bytes 589840 | tf_op jit(solution)/shard_map/reduce_scatter | solution.py:146
  363.2 5.5 all-to-all-start.3
  368.7 2.5 multiply_reduce_fusion.1
  371.2 13.3 %all-to-all-done.3 = bf16[8,48,768]{2,1,0:T(8,128)(2,1)S(1)} async-done(((bf16[8,48,768]{2,1,0:T(8,128)(2,1)}), bf16[8,48,768]{2,1,0:T(8,128)(2,1)S(1)}, u32[]{:S(2)}, u32[]{:S(2)}) %all-to-all-start.3) | async-done | bytes 589856 | tf_op jit(solution)/shard_map/all_to_all | solution.py:152
  385.8 1.4 fusion.29
  387.2 2.9 fusion.44
  390.1 1.8 convolution_convert_fusion.7
  394.9 4.1 fusion.38
  399.1 6.0 convolution_bitcast_fusion.1
  405.1 6.5 %convolution_bitcast_fusion = f32[1,768,768]{2,1,0:T(8,128)} fusion(bf16[1536,768]{1,0:T(8,128)(2,1)S(1)} %copy-done.35, f32[1536,768]{1,0:T(8,128)} %copy-done.39), kind=kOutput, calls=%fused_computation.17 | convolution fusion | flops 1822556160 | bytes 9437184 | tf_op jit(solution)/shard_map/dot_general | solution.py:16
  413.2 1.4 fusion.28
  414.7 39.9 %all-reduce.5 = (f32[768,8]{0,1:T(8,128)S(1)}, f32[768]{0:T(1024)S(1)}, f32[768]{0:T(1024)S(1)}, f32[32,12]{0,1:T(8,128)}) all-reduce(f32[768,8]{0,1:T(8,128)S(1)} %fusion.74, f32[768]{0:T(1024)S(1)} %get-tuple-element.14, f32[768]{0:T(1024)S(1)} %copy-done.25, ...), channel_id=6, replica_groups=mesh['fsdp'=4,'expert'=8] {'fsdp','expert'}, use_global_device_ids=true, to_apply=%region_19.20.clone | all-reduce | flops 8064 | bytes 64512
  457.2 30.3 %reduce-scatter.12.cloned.1.call-done = f32[24,768]{1,0:T(8,128)} async-done(((f32[768,768]{1,0:T(8,128)}), f32[24,768]{1,0:T(8,128)}) %reduce-scatter.12.cloned.1.call-update) | async-done | bytes 73744 | tf_op jit(solution)/shard_map/reduce_scatter | solution.py:204
  487.5 125.4 %reduce-scatter.10.cloned.1.call-done = f32[24,2304]{1,0:T(8,128)} async-done(((f32[768,2304]{1,0:T(8,128)}), f32[24,2304]{1,0:T(8,128)}) %reduce-scatter.10.cloned.1.call-update) | async-done | bytes 221200 | tf_op jit(solution)/shard_map/reduce_scatter | solution.py:203
  (151 shorter events, 18.9 us)
Async XLA Ops:
  7.2 268.0 %copy-start = (bf16[1,768,768]{2,1,0:T(8,128)(2,1)S(1)}, bf16[1,768,768]{2,1,0:T(8,128)(2,1)}, u32[]{:S(2)}) copy-start(bf16[1,768,768]{2,1,0:T(8,128)(2,1)} %param.23) | copy-start | bytes 3538948
  7.2 2.3 copy-start.1
  7.2 143.5 %all-gather.6.cloned.1.call-start = ((), (), s32[]{:S(2)}) async-start(), calls=%async_computation.8 | async-start | bytes 3649536 | tf_op jit(solution)/shard_map/all_gather | solution.py:49
  7.9 151.9 %all-gather.8.cloned.1.call-start = ((), (), s32[]{:S(2)}) async-start(), calls=%async_computation.9 | async-start | bytes 1216512 | tf_op jit(solution)/shard_map/all_gather | solution.py:50
  8.7 260.2 %all-gather.10.cloned.1.call-start = ((), (), s32[]{:S(2)}) async-start(), calls=%async_computation.10 | async-start | bytes 2949120 | tf_op jit(solution)/shard_map/all_gather | solution.py:108
  9.5 97.3 %copy-start.26 = (s32[128,2]{0,1:T(2,128)S(1)}, s32[128,2]{0,1:T(2,128)}, u32[]{:S(2)}) copy-start(s32[128,2]{0,1:T(2,128)} %param.26) | copy-start | bytes 3076
  9.5 97.3 %copy-start.32 = (s32[128,2]{0,1:T(2,128)S(1)}, s32[128,2]{0,1:T(2,128)}, u32[]{:S(2)}) copy-start(s32[128,2]{0,1:T(2,128)} %param.27) | copy-start | bytes 3076
  9.6 97.4 %copy-start.37 = (bf16[24]{0:T(256)(128)(2,1)S(1)}, bf16[24]{0:T(256)(128)(2,1)}, u32[]{:S(2)}) copy-start(bf16[24]{0:T(256)(128)(2,1)} %param.19) | copy-start | bytes 148
  9.6 97.6 %copy-start.38 = (bf16[24]{0:T(256)(128)(2,1)S(1)}, bf16[24]{0:T(256)(128)(2,1)}, u32[]{:S(2)}) copy-start(bf16[24]{0:T(256)(128)(2,1)} %param.20) | copy-start | bytes 148
  9.6 140.1 %copy-start.2 = (bf16[128,768]{1,0:T(8,128)(2,1)S(1)}, bf16[128,768]{1,0:T(8,128)(2,1)}, u32[]{:S(2)}) copy-start(bf16[128,768]{1,0:T(8,128)(2,1)} %param.14) | copy-start | bytes 589828
  9.6 140.3 %copy-start.27 = (f32[32,12]{0,1:T(8,128)S(1)}, f32[32,12]{0,1:T(8,128)}, u32[]{:S(2)}) copy-start(f32[32,12]{0,1:T(8,128)} %param.21) | copy-start | bytes 4612
  149.8 3.5 copy-start.33
  155.2 4.5 copy-start.5
  159.8 22.3 %copy-start.31 = (bf16[24,8]{0,1:T(8,128)(2,1)S(1)}, bf16[24,8]{0,1:T(8,128)(2,1)}, u32[]{:S(2)}) copy-start(bf16[24,8]{0,1:T(8,128)(2,1)} %param.18) | copy-start | bytes 1156
  161.6 223.3 %copy-start.30 = (f32[128]{0:T(128)}, f32[128]{0:T(128)S(1)}, u32[]{:S(2)}) copy-start(f32[128]{0:T(128)S(1)} %fusion.64) | copy-start | bytes 1540
  182.1 108.6 %all-gather.12.cloned.1.call-start = ((), (), s32[]{:S(2)}) async-start(), calls=%async_computation.12 | async-start | bytes 2949120 | tf_op jit(solution)/shard_map/all_gather | solution.py:139
  268.8 57.3 %reduce-scatter.6.cloned.1.call-start = ((), (), s32[]{:S(2)}) async-start(), calls=%async_computation.11 | async-start | bytes 2949120 | tf_op jit(solution)/shard_map/reduce_scatter | solution.py:113
  279.5 82.8 %reduce-scatter.8.cloned.1.call-start = ((), (), s32[]{:S(2)}) async-start(), calls=%async_computation.13 | async-start | bytes 2949120 | tf_op jit(solution)/shard_map/reduce_scatter | solution.py:146
  290.7 8.8 %copy-start.36 = (bf16[1,768,768]{2,1,0:T(8,128)(2,1)S(1)}, bf16[1,768,768]{2,1,0:T(8,128)(2,1)}, u32[]{:S(2)}) copy-start(bf16[1,768,768]{2,1,0:T(8,128)(2,1)} %param.22) | copy-start | bytes 3538948
  326.1 36.2 %all-to-all-start.1 = ((bf16[8,48,768]{2,1,0:T(8,128)(2,1)}), bf16[8,48,768]{2,1,0:T(8,128)(2,1)S(1)}, u32[]{:S(2)}, u32[]{:S(2)}) async-start(bf16[8,48,768]{2,1,0:T(8,128)(2,1)} %bitcast.117), calls=%async_computation.2 | async-start | bytes 1179648 | tf_op jit(solution)/shard_map/all_to_all | solution.py:121
  363.2 21.4 %all-to-all-start.3 = ((bf16[8,48,768]{2,1,0:T(8,128)(2,1)}), bf16[8,48,768]{2,1,0:T(8,128)(2,1)S(1)}, u32[]{:S(2)}, u32[]{:S(2)}) async-start(bf16[8,48,768]{2,1,0:T(8,128)(2,1)} %bitcast.116), calls=%async_computation.5 | async-start | bytes 1179648 | tf_op jit(solution)/shard_map/all_to_all | solution.py:152
  368.7 118.8 %reduce-scatter.12.cloned.1.call-start = ((), (), s32[]{:S(2)}) async-start(), calls=%async_computation.15 | async-start | bytes 2433024 | tf_op jit(solution)/shard_map/reduce_scatter | solution.py:204
  371.2 14.6 %copy-start.23 = (bf16[128,8]{0,1:T(8,128)(2,1)}, bf16[128,8]{0,1:T(8,128)(2,1)S(1)}, u32[]{:S(2)}) copy-start(bf16[128,8]{0,1:T(8,128)(2,1)S(1)} %select_reduce_fusion) | copy-start | bytes 6148
  390.1 222.8 %reduce-scatter.10.cloned.1.call-start = ((), (), s32[]{:S(2)}) async-start(), calls=%async_computation.14 | async-start | bytes 7299072 | tf_op jit(solution)/shard_map/reduce_scatter | solution.py:203
  399.0 6.1 copy-start.35
  405.1 6.5 %copy-start.20 = (s32[128,128]{0,1:T(8,128)S(1)}, s32[128,128]{0,1:T(8,128)}, u32[]{:S(2)}) copy-start(s32[128,128]{0,1:T(8,128)} %copy-done.19) | copy-start | bytes 196612
  405.1 7.9 %copy-start.24 = (bf16[128,8]{0,1:T(8,128)(2,1)S(1)}, bf16[128,8]{0,1:T(8,128)(2,1)}, u32[]{:S(2)}) copy-start(bf16[128,8]{0,1:T(8,128)(2,1)} %copy-done.23) | copy-start | bytes 6148
  405.1 8.1 %copy-start.3 = (bf16[768,2304]{1,0:T(8,128)(2,1)S(1)}, bf16[768,2304]{1,0:T(8,128)(2,1)}, u32[]{:S(2)}) copy-start(bf16[768,2304]{1,0:T(8,128)(2,1)} %all-gather.6.cloned.1.call-done) | copy-start | bytes 10616836
  405.1 8.1 %copy-start.14 = (bf16[12,64,128]{2,1,0:T(8,128)(2,1)S(1)}, bf16[12,64,128]{2,1,0:T(8,128)(2,1)}, u32[]{:S(2)}) copy-start(bf16[12,64,128]{2,1,0:T(8,128)(2,1)} %copy-done.13) | copy-start | bytes 589828
  405.1 8.1 %copy-start.16 = (bf16[12,64,128]{2,1,0:T(8,128)(2,1)S(1)}, bf16[12,64,128]{2,1,0:T(8,128)(2,1)}, u32[]{:S(2)}) copy-start(bf16[12,64,128]{2,1,0:T(8,128)(2,1)} %copy-done.15) | copy-start | bytes 589828
  405.1 8.1 %copy-start.18 = (bf16[12,64,128]{2,1,0:T(8,128)(2,1)S(1)}, bf16[12,64,128]{2,1,0:T(8,128)(2,1)}, u32[]{:S(2)}) copy-start(bf16[12,64,128]{2,1,0:T(8,128)(2,1)} %copy-done.17) | copy-start | bytes 589828
  413.2 43.1 %copy-start.34 = (f32[128]{0:T(128)S(1)}, f32[128]{0:T(128)}, u32[]{:S(2)}) copy-start(f32[128]{0:T(128)} %copy-done.33) | copy-start | bytes 1540
  (18 other events, 22.1 us)
Sparse Core Ops, SparseCore 0:
  10.9 62.8 all-gather.5
  76.8 52.9 all-gather.7
  182.2 22.4 all-gather.9
  269.0 21.6 all-gather.11
  293.0 33.0 reduce-scatter.5
  329.3 33.0 reduce-scatter.7
  390.2 97.2 reduce-scatter.11
  494.7 118.1 reduce-scatter.9
where the time goes:
time: 621 us; the launch traced here: 620 us
  waiting for transfers between devices  233 us (38%)
  blocking collectives  185 us (30%)
  local copies, waits for them, and re-layouts  109 us (18%)
  matrix products  60.6 us (10%)
  between operations  14.8 us (2%)
  starting transfers between devices  11.5 us (2%)
    reduce_scatter x1, waiting for transfers between devices, on_device(): lax.psum_scatter(grad_triple, ('fsdp', 'expert'), scatter_dimension=0, ti...  125 us
    gather x1, local copies, waits for them, and re-layouts, on_device(): bucket_pair = jnp.take(buckets, jnp.clip(distance, 0, count - 1))  97.2 us
    unnamed x2, blocking collectives  81.9 us
    all_gather x1, blocking collectives, on_device(): lax.all_gather(router, ('fsdp', 'expert'), axis=0, tiled=True)  65.5 us
    reduce_scatter x1, waiting for transfers between devices, on_device(): lax.psum_scatter(contract_cols(inner_grad_all, expert_up[0]).astype(jnp.b...  30.7 us
    reduce_scatter x1, waiting for transfers between devices, on_device(): lax.psum_scatter(grad_output, ('fsdp', 'expert'), scatter_dimension=0, ti...  30.3 us
    reduce_scatter x1, waiting for transfers between devices, on_device(): lax.psum_scatter(jnp.dot(active_all, expert_down[0], preferred_element_ty...  21.2 us
    all_to_all x1, blocking collectives, on_device(): lax.all_to_all(outgoing.reshape(experts, capacity, width), 'expert', spli...  20 us
  transfers between devices with their start and end apart: 10, of which 6 were waited for; matrix products, arithmetic and copies ran while one was open for 26% of the time, Pallas kernels for 0%

commit v1 on v0

v1 whole, which is shorter than its diff:
```python
import functools
import math

import jax
import jax.numpy as jnp
import numpy as np
from jax import lax
from jax.experimental import pallas as pl
from jax.experimental.pallas import tpu as pltpu
from jax.sharding import PartitionSpec as P

HEADS = 12
HEAD = 64
BUCKETS = 32
LANES = 128
BF = jnp.bfloat16
F32 = jnp.float32


def rms_scale(value, gain):
    return value * lax.rsqrt(jnp.mean(value * value, axis=-1, keepdims=True) + 1e-06) * gain


def contract_rows(left, right):
    return lax.dot_general(left, right, (((0,), (0,)), ((), ())), preferred_element_type=F32)


def contract_cols(left, right):
    return lax.dot_general(left, right, (((1,), (1,)), ((), ())), preferred_element_type=F32)


def matmul(left, right):
    return jnp.dot(left, right, preferred_element_type=F32)


AXES = ("fsdp", "expert")


def sizes():
    return lax.axis_size("fsdp"), lax.axis_size("expert")


def core_mask():
    return sizes()[1]


def xy_masks():
    columns, experts = sizes()
    return [2 * experts * x + y for y in range(2) for x in range(columns // 2)]


def chip_masks():
    columns, experts = sizes()
    return [2 * experts * x for x in range(columns // 2)]


def z_masks():
    return [2 * z for z in range(sizes()[1] // 2)]


def block_masks():
    return [c + xy + z for c in (0, core_mask()) for xy in xy_masks() for z in z_masks()]


def swap(value, mask):
    columns, experts = sizes()
    return lax.ppermute(value, AXES, [(i, i ^ mask) for i in range(columns * experts)])


def tied(value, other):
    return lax.optimization_barrier((value, other))[0]


def fan(value, masks):
    return [value] + [swap(value, mask) for mask in masks[1:]]


def fan_sum(parts, masks):
    arrived = [swap(part, mask) for part, mask in zip(parts[1:], masks[1:])]
    total = parts[0].astype(F32)
    for part in arrived:
        total = total + part.astype(F32)
    return total


def stack(parts):
    return jnp.concatenate(parts, axis=0)


def after(value, *others):
    return pl.pallas_call(
        lambda *refs: None,
        out_shape=jax.ShapeDtypeStruct(value.shape, value.dtype),
        in_specs=[pl.BlockSpec(memory_space=pl.ANY)] * (1 + len(others)),
        out_specs=pl.BlockSpec(memory_space=pl.ANY),
        input_output_aliases={0: 0},
    )(value, *others)


def gather_blocks(value, beside):
    value = stack(fan(value, z_masks()))
    value = stack(fan(after(value, beside), xy_masks()))
    return value, swap(value, core_mask())


def add_low(own, arrived):
    return (own.astype(F32) + arrived.astype(F32)).astype(BF)


def scatter_blocks(value):
    xy, z = xy_masks(), z_masks()
    value = value.reshape(len(xy), -1, value.shape[1])
    arrived = [swap(value[i], xy[i]) for i in range(1, len(xy))]
    value = sum((part.astype(F32) for part in arrived), value[0].astype(F32)).astype(BF)
    value = value.reshape(len(z), -1, value.shape[1])
    return [value[0]] + [swap(value[i], z[i]) for i in range(1, len(z))], arrived[0]


def exchange(value):
    experts = lax.axis_size("expert")
    blocks = value.reshape(experts, value.shape[0] // experts, value.shape[1])
    moved = lax.all_to_all(blocks, "expert", split_axis=0, concat_axis=0, tiled=True)
    return moved.reshape(value.shape)


def lanes_of(value, place):
    high = value.astype(BF)
    rest = (value - high.astype(F32)).astype(BF)
    lane = lax.broadcasted_iota(jnp.int32, (value.shape[0], LANES), 1)
    nothing = jnp.zeros((), BF)
    return jnp.where(lane == place, high, jnp.where(lane == place + 1, rest, nothing))


def nt(left, right):
    return contract_cols(left, right)


def tn(left, right):
    return contract_rows(left, right)


class Incoming:
    def __init__(self, ref, copy):
        self.ref, self.copy = ref, copy
        self.shape, self.dtype = ref.shape, ref.dtype
        copy.start()

    def wait(self):
        if self.copy is not None:
            self.copy.wait()
            self.copy = None

    def __getitem__(self, index):
        self.wait()
        return self.ref[index]


def kernel_call(body, outs, flops, *operands, fetch=(), scratch=16):
    moved = sum(math.prod(v.shape) * v.dtype.itemsize for v in operands)
    moved += sum(math.prod(shape) * jnp.dtype(kind).itemsize for shape, kind in outs)
    taken = len(operands) + len(outs)

    def kernel(*refs):
        refs, buffers = list(refs[:taken]), refs[taken:]
        for i, number in enumerate(fetch):
            copy = pltpu.make_async_copy(refs[number], buffers[i], buffers[-1].at[i])
            refs[number] = Incoming(buffers[i], copy)
        body(*refs)
        for number in fetch:
            refs[number].wait()

    whole, left = pl.BlockSpec(memory_space=pltpu.VMEM), pl.BlockSpec(memory_space=pl.ANY)
    buffers = [pltpu.VMEM(operands[i].shape, operands[i].dtype) for i in fetch]
    if fetch:
        buffers.append(pltpu.SemaphoreType.DMA((len(fetch),)))
    return pl.pallas_call(
        kernel,
        out_shape=[jax.ShapeDtypeStruct(shape, kind) for shape, kind in outs],
        in_specs=[left if i in fetch else whole for i in range(len(operands))],
        out_specs=[whole] * len(outs),
        scratch_shapes=buffers,
        compiler_params=pltpu.CompilerParams(vmem_limit_bytes=scratch * 1024 * 1024),
        cost_estimate=pl.CostEstimate(flops=flops, bytes_accessed=moved, transcendentals=0),
    )(*operands)


def pick_heads(first_head, second_head):
    lane = lax.broadcasted_iota(jnp.int32, first_head.shape, 1)
    return jnp.where(lane < HEAD, first_head, second_head)


def one_head(pair, side):
    lane = lax.broadcasted_iota(jnp.int32, pair.shape, 1)
    return jnp.where((lane < HEAD) == (side == 0), pair, jnp.zeros((), pair.dtype))


def pair_of(value, number):
    return value[:, number * LANES : (number + 1) * LANES]


def inverse_rms(value):
    return lax.rsqrt(jnp.mean(value * value, axis=-1, keepdims=True) + 1e-06)


def shuffle_of(place_of):
    width = place_of.shape[1]
    return (lax.broadcasted_iota(jnp.int32, (width, width), 0) == place_of[...]).astype(BF)


def small_of(near, far, shuffle):
    lanes = near.shape[1] - 4 * shuffle.shape[0]
    rows = jnp.concatenate([near[:, :lanes], far[:, :lanes]], axis=0)
    return jnp.transpose(matmul(shuffle, rows)).astype(BF)


def pack_kernel(router_rows, first_gain, second_gain, project_in, project_out, packed_ref):
    share, columns = project_in.shape
    experts = router_rows.shape[0]
    at = packed_ref.shape[1] - columns - project_out.shape[1]
    eye = lax.broadcasted_iota(jnp.int32, (share, share), 0)
    eye = (eye == lax.broadcasted_iota(jnp.int32, (share, share), 1)).astype(BF)
    rows = jnp.concatenate(
        [router_rows[...], first_gain[...], second_gain[...], jnp.zeros((at - experts - 2, share), BF)],
        axis=0,
    )
    packed_ref[:, :at] = nt(eye, rows).astype(BF)
    packed_ref[:, at : at + columns] = project_in[...]
    packed_ref[:, at + columns :] = project_out[...]


def forward_kernel(
    experts,
    tokens,
    place_of,
    near,
    far,
    bias_rows,
    positions,
    routes,
    target_rows,
    low_ref,
    high_ref,
    outgoing_ref,
):
    count, width = tokens.shape
    at_probs = width + LANES
    shuffle = shuffle_of(place_of)
    small = small_of(near, far, shuffle)
    half = width // 2
    inputs = tokens[...].astype(F32)
    gain_first = small[experts : experts + 1].astype(F32)
    gain_second = small[experts + 1 : experts + 2].astype(F32)
    normed = (inputs * inverse_rms(inputs) * gain_first).astype(BF)
    normed = matmul(normed, shuffle).astype(BF)
    low_ref[:, 3 * width : 4 * width] = normed
    at = near.shape[1] - 4 * width
    joint = matmul(normed[:, :half], near[:, at : at + 3 * width])
    joint = joint + matmul(normed[:, half:], far[:, at : at + 3 * width])
    low_ref[:, : 3 * width] = joint.astype(BF)
    row = lax.broadcasted_iota(jnp.int32, (count, count), 0)
    distance = row - lax.broadcasted_iota(jnp.int32, (count, count), 1)
    valid = (distance >= 0) & (distance <= positions[...])
    pairs = width // LANES
    attended = []
    for number in range(pairs):
        query, keys, values = (
            low_ref[:, i * width + number * LANES : i * width + (number + 1) * LANES] for i in range(3)
        )
        outs = []
        for side in range(2):
            head = 2 * number + side
            bias = jnp.broadcast_to(bias_rows[head : head + 1], (count, count))
            bias = pltpu.roll(bias, 0, 1, stride=1, stride_axis=0)
            scores = jnp.where(valid, nt(one_head(query, side), keys) * 0.125 + bias, -1e30)
            expo = jnp.exp(scores - jnp.max(scores, axis=-1, keepdims=True))
            probs = expo / jnp.sum(expo, axis=-1, keepdims=True)
            high_ref[:, at_probs + head * count : at_probs + (head + 1) * count] = probs
            outs.append(matmul(probs.astype(BF), values))
        attended.append(pick_heads(*outs).astype(BF))
    attended = matmul(jnp.concatenate(attended, axis=1), shuffle).astype(BF)
    low_ref[:, 4 * width : 5 * width] = attended
    first = inputs + matmul(attended[:, :half], near[:, at + 3 * width :])
    first = first + matmul(attended[:, half:], far[:, at + 3 * width :])
    high_ref[:, :width] = first
    second = (first * inverse_rms(first) * gain_second).astype(BF)
    low_ref[:, 5 * width :] = second
    logits = nt(second, small[:LANES])
    lane = lax.broadcasted_iota(jnp.int32, logits.shape, 1)
    chosen = [
        jnp.sum(jnp.where(lane == routes[:, c : c + 1], logits, 0.0), axis=-1, keepdims=True)
        for c in range(2)
    ]
    top = jnp.maximum(chosen[0], chosen[1])
    expo = [jnp.exp(value - top) for value in chosen]
    gates = [value / (expo[0] + expo[1]) for value in expo]
    high_ref[:, width:at_probs] = jnp.where(lane == 0, gates[0], jnp.where(lane == 1, gates[1], 0.0))
    slot = lax.broadcasted_iota(jnp.int32, (outgoing_ref.shape[0], count), 0)
    rows = jnp.zeros(outgoing_ref.shape, F32)
    for c in range(2):
        hot = (slot == target_rows[c : c + 1]).astype(BF)
        rows = rows + matmul(hot, jnp.concatenate([second, lanes_of(gates[c], 0)], axis=1))
    outgoing_ref[...] = rows.astype(BF)


def expert_forward(rows, up):
    inner = nt(rows, up)
    square = inner * inner
    bend = jnp.tanh(0.7978845608028654 * inner * (1.0 + 0.044715 * square))
    slope = 0.5 * (1.0 + bend) + 0.5 * inner * (1.0 - bend * bend) * (
        0.7978845608028654 * (1.0 + 0.134145 * square)
    )
    return (0.5 * inner * (1.0 + bend)).astype(BF), slope


def gate_of(packed, width):
    return packed[:, width : width + 1].astype(F32) + packed[:, width + 1 : width + 2].astype(F32)


def expert_kernel(chips, column, *refs):
    rows, grads, weights, refs = refs[:2], refs[2:4], refs[4 : 4 + chips], refs[4 + chips :]
    row_refs, result_ref, kept_ref = refs[:2], refs[2], refs[3]
    count, width = grads[0].shape
    hidden = weights[0].shape[0] // 2
    for core in range(2):
        packed, grad = rows[core], grads[core][...]
        gate = gate_of(packed, width)
        block = slice(core * count, (core + 1) * count)
        result, row_grad = jnp.zeros((count, width), F32), jnp.zeros((count, width), F32)
        for i in range(chips):
            up, down = weights[i][:hidden], weights[i][hidden:]
            active, slope = expert_forward(packed[:, :width], up)
            inner_grad = nt(grad, down) * slope
            if i == 0:
                kept_ref[block, :hidden] = active
                kept_ref[block, hidden : 2 * hidden] = (inner_grad * gate).astype(BF)
            result = result + matmul(active, down)
            row_grad = row_grad + matmul(inner_grad.astype(BF), up)
        grad = grad.astype(F32)
        kept_ref[block, 2 * hidden :] = (grad * gate).astype(BF)
        result_ref[block] = result.astype(BF)
        dots = jnp.sum(result * grad, axis=-1, keepdims=True)
        row_refs[core][...] = jnp.concatenate(
            [row_grad.astype(BF), lanes_of(dots, 2 * column[0, 0])], axis=1
        )


def weight_grad_kernel(others, weights, kept, far, near, *refs):
    packed_far, grads_far, (up_ref, down_ref) = refs[:others], refs[others : 2 * others], refs[2 * others :]
    width = up_ref.shape[0]
    hidden = up_ref.shape[1]
    count = near.shape[0]
    up, down = weights[:hidden], weights[hidden:]
    for i, rows in enumerate((far, near)):
        block = slice(i * count, (i + 1) * count)
        scaled = kept[block, 2 * hidden :]
        parts = (
            tn(rows[:, :width], kept[block, hidden : 2 * hidden]),
            tn(kept[block, :hidden], scaled),
        )
        if i == 0:
            up_ref[...], down_ref[...] = parts
        else:
            up_ref[...] += parts[0]
            down_ref[...] += parts[1]
    for packed, grad_ref in zip(packed_far, grads_far):
        gate = gate_of(packed, width)
        grad = grad_ref[...]
        active, slope = expert_forward(packed[:, :width], up)
        inner_grad = (nt(grad, down) * slope * gate).astype(BF)
        up_ref[...] += tn(packed[:, :width], inner_grad)
        down_ref[...] += tn(active, (grad.astype(F32) * gate).astype(BF))


def table_lanes(share):
    return BUCKETS * HEADS // share


def home_kernel(
    experts,
    share,
    home,
    routes,
    target,
    cotangent,
    place_of,
    low,
    high,
    near,
    far,
    flip_hot,
    keep_ref,
    send_ref,
    first_grad_ref,
    joint_grad_ref,
    distance_ref,
):
    count, width = cotangent.shape
    half = width // 2
    shuffle = shuffle_of(place_of)
    small_rows = small_of(near, far, shuffle)
    at_probs = width + LANES
    slot = lax.broadcasted_iota(jnp.int32, (count, home.shape[0]), 1)
    lane = lax.broadcasted_iota(jnp.int32, (count, LANES), 1)
    gates = [high[:, width + c : width + c + 1] for c in range(2)]
    routed = [matmul((slot == target[:, c : c + 1]).astype(BF), home[...]) for c in range(2)]
    dots = [jnp.sum(value[:, width:], axis=-1, keepdims=True) for value in routed]
    mean = gates[0] * dots[0] + gates[1] * dots[1]
    logit_grad = jnp.zeros((count, LANES), F32)
    for c in range(2):
        logit_grad = jnp.where(lane == routes[:, c : c + 1], gates[c] * (dots[c] - mean), logit_grad)
    logit_grad = logit_grad.astype(BF)
    second_grad = gates[0] * routed[0][:, :width] + gates[1] * routed[1][:, :width]
    second_grad = second_grad + matmul(logit_grad, small_rows[:LANES])
    gain = small_rows[experts + 1 : experts + 2].astype(F32)
    first = high[:, :width]
    inverse = inverse_rms(first)
    unit = first * inverse
    scaled = second_grad * gain
    first_grad = cotangent[...].astype(F32) + inverse * (
        scaled - unit * jnp.mean(unit * scaled, axis=-1, keepdims=True)
    )
    first_grad_ref[...] = first_grad
    first_low = first_grad.astype(BF)
    attended_grad = jnp.concatenate(
        [nt(first_low, part[:, part.shape[1] - width :]) for part in (near, far)], axis=1
    ).astype(BF)
    attended_grad = nt(attended_grad, shuffle).astype(BF)
    value_grad = []
    for number in range(width // LANES):
        outs = [
            tn(
                high[:, at_probs + head * count : at_probs + (head + 1) * count].astype(BF),
                pair_of(attended_grad, number),
            )
            for head in (2 * number, 2 * number + 1)
        ]
        value_grad.append(pick_heads(*outs).astype(BF))
    value_grad = jnp.concatenate(value_grad, axis=1)
    joint_grad_ref[:, 2 * width :] = value_grad
    gain_part = second_grad * unit
    gain_high = gain_part.astype(BF)
    gain_rest = (gain_part - gain_high.astype(F32)).astype(BF)
    ones = (lane == experts).astype(BF)
    left = jnp.concatenate([low[:, 5 * width :], gain_high, gain_rest], axis=0)
    left = matmul(left, shuffle).astype(BF)
    right = jnp.concatenate([logit_grad, ones, ones], axis=0)
    small = tn(left, right)
    row = lax.broadcasted_iota(jnp.int32, (count, count), 0)
    for number in range(width // LANES):
        span = slice(number * LANES, (number + 1) * LANES)
        query, keys, values = (
            low[:, i * width + number * LANES : i * width + (number + 1) * LANES] for i in range(3)
        )
        own_grad = attended_grad[:, span]
        query_grads, key_grads = [], []
        for side in range(2):
            head = 2 * number + side
            chance = high[:, at_probs + head * count : at_probs + (head + 1) * count]
            prob_grad = nt(one_head(own_grad, side), values)
            score_grad = chance * (prob_grad - jnp.sum(chance * prob_grad, axis=-1, keepdims=True))
            lined = score_grad
            step = 1
            while step < count:
                lined = jnp.where((row // step) % 2 == 1, pltpu.roll(lined, count - step, 1), lined)
                step *= 2
            distance_ref[head : head + 1] = jnp.sum(lined, axis=0, keepdims=True)
            pair_grad = (score_grad * 0.125).astype(BF)
            query_grads.append(matmul(pair_grad, keys))
            key_grads.append(tn(pair_grad, query))
        joint_grad_ref[:, span] = pick_heads(*query_grads).astype(BF)
        joint_grad_ref[:, width + number * LANES : width + (number + 1) * LANES] = pick_heads(
            *key_grads
        ).astype(BF)
    table = jnp.dot(
        distance_ref[...], flip_hot[...], precision=lax.Precision.HIGHEST, preferred_element_type=F32
    ).astype(BF)
    lanes = table_lanes(share)
    spread = keep_ref.shape[1] - 4 * width
    value_row = lax.broadcasted_iota(jnp.int32, (width, HEADS), 0) % share * lanes
    value_head = lax.broadcasted_iota(jnp.int32, (width, HEADS), 1)
    bucket = lax.broadcasted_iota(jnp.int32, (BUCKETS, spread), 0)
    lane = lax.broadcasted_iota(jnp.int32, (BUCKETS, spread), 1) - (experts + 1)
    small = jnp.pad(small, ((0, 0), (0, spread - LANES)))
    for start in range(0, max(lanes, BUCKETS), min(lanes, BUCKETS)):
        if lanes <= BUCKETS:
            picked = (value_row == value_head * BUCKETS + start).astype(BF)
            put = ((lane >= 0) & (lane < lanes) & (bucket == lane + start)).astype(BF)
        else:
            picked = (value_row + start == value_head * BUCKETS).astype(BF)
            put = (lane - start == bucket).astype(BF)
        small = small + matmul(picked, matmul(table, put).astype(BF))
    joint_grads = joint_grad_ref[...]
    for ref, at in ((keep_ref, 0), (send_ref, half)):
        attended, normed = (low[:, i * width + at : i * width + at + half] for i in (4, 3))
        ref[:, : 3 * width] = tn(normed, joint_grads).astype(BF)
        ref[:, 3 * width : 4 * width] = tn(attended, first_low).astype(BF)
        ref[:, 4 * width :] = small[at : at + half].astype(BF)


def finish_kernel(project_in, gain, *refs):
    parts, (grad_in_ref, sum_out_ref, small_ref, gain_ref) = refs[:-4], refs[-4:]
    sums = sum(part[...].astype(F32) for part in parts)
    width = sum_out_ref.shape[1]
    grad_in = sums[:, : 3 * width]
    grad_in_ref[...] = grad_in
    sum_out_ref[...] = sums[:, 3 * width : 4 * width]
    small_ref[...] = sums[:, 4 * width :]
    grads = grad_in * project_in[...].astype(F32)
    gain_ref[...] = jnp.sum(grads, axis=-1, keepdims=True) / gain[...].astype(F32)


def on_device(
    tokens,
    cotangent,
    project_in,
    project_out,
    router,
    first_gain,
    second_gain,
    bias_table,
    expert_up,
    expert_down,
    positions,
    buckets,
    routes,
    slots,
):
    highest = lax.Precision.HIGHEST
    count, width = tokens.shape
    experts = lax.axis_size("expert")
    capacity = 3 * count // experts
    rows_here = experts * capacity
    share = project_in.shape[0]
    column = lax.axis_index("fsdp")
    mine = column * experts + lax.axis_index("expert")
    small_lanes = -(-(experts + 2) // LANES) * LANES
    (packed,) = kernel_call(
        pack_kernel,
        [((share, small_lanes + 4 * width), BF)],
        0,
        router.T,
        first_gain[None],
        second_gain[None],
        project_in,
        project_out,
        fetch=range(5),
        scratch=56,
    )
    weights = stack([expert_up[0].T, expert_down[0]])
    halves = gather_blocks(packed, weights)
    weights = fan(after(weights, halves[0]), chip_masks())
    in_halves = [half[:, small_lanes : small_lanes + 3 * width] for half in halves]

    def times_back(value, parts):
        return jnp.concatenate([contract_cols(value, part) for part in parts], axis=1)

    feature = jnp.arange(width, dtype=jnp.int32)
    masks = jnp.asarray(np.repeat(np.array(block_masks(), np.int32), share))
    place_of = (masks ^ mine) * share + feature % share
    shuffle = (feature[:, None] == place_of[None, :]).astype(BF)

    inputs = tokens.astype(F32)
    inputs_rel = matmul(tokens, shuffle)

    target = routes * capacity + slots
    slot_index = jnp.arange(rows_here, dtype=jnp.int32)
    hot = (slot_index[None, None, :] == jnp.transpose(target)[:, :, None]).astype(BF)
    place_hot = hot[0] + hot[1]
    grad_rows = contract_rows(place_hot, cotangent).astype(BF)
    grad_own = exchange(grad_rows)
    grad_parts = (grad_own, swap(grad_own, core_mask()))

    places = jnp.arange(count, dtype=jnp.int32)
    bucket_hot = (buckets[:, None] == jnp.arange(BUCKETS, dtype=jnp.int32)).astype(F32)
    flip = ((places[:, None] + places[None, :]) % count == 0).astype(F32)
    flip_hot = jnp.dot(flip, bucket_hot, precision=highest)
    bias_rows = lax.dot_general(
        bias_table, flip_hot, (((0,), (1,)), ((), ())), precision=highest
    )
    low, high, outgoing = kernel_call(
        functools.partial(forward_kernel, experts),
        [
            ((count, 6 * width), BF),
            ((count, width + LANES + HEADS * count), F32),
            ((rows_here, width + LANES), BF),
        ],
        2 * count * width * 6 * width,
        tokens,
        place_of[None],
        *halves,
        bias_rows,
        positions[:, None],
        routes,
        jnp.transpose(target),
    )
    row_own = exchange(after(outgoing, grad_own))
    row_parts = (row_own, swap(row_own, core_mask()))

    chips = len(chip_masks())
    piece = expert_up.shape[2]
    wide = (rows_here, width + LANES)
    row_far, row_near, result, kept = kernel_call(
        functools.partial(expert_kernel, chips),
        [(wide, BF), (wide, BF), ((2 * rows_here, width), BF), ((2 * rows_here, 2 * piece + width), BF)],
        16 * rows_here * width * chips * piece,
        column.astype(jnp.int32).reshape(1, 1),
        row_parts[1],
        row_parts[0],
        grad_parts[1],
        grad_parts[0],
        *weights,
        fetch=range(5, 5 + len(weights)),
        scratch=56,
    )
    home = exchange(add_low(row_near, swap(row_far, core_mask())))
    result_own = add_low(result[rows_here:], swap(result[:rows_here], core_mask()))

    far = []
    for own in (row_own, grad_own):
        parts = [swap(after(own, *weights[1:]), mask) for mask in chip_masks()[1:]]
        far += [both for part in parts for both in (part, swap(part, core_mask()))]
    home = after(home, result_own, *far)

    half = width // 2
    table_at = experts + 1
    spread_lanes = -(-(table_at + table_lanes(share)) // LANES) * LANES
    keep, send, first_grad, joint_grad, _ = kernel_call(
        functools.partial(home_kernel, experts, share),
        [
            ((half, 4 * width + spread_lanes), BF),
            ((half, 4 * width + spread_lanes), BF),
            ((count, width), F32),
            ((count, 3 * width), BF),
            ((HEADS, count), F32),
        ],
        2 * count * width * 10 * width,
        home,
        routes,
        target,
        cotangent,
        place_of[None],
        low,
        high,
        *halves,
        flip_hot,
        fetch=(7, 8, 6, 3, 5),
        scratch=56,
    )
    dense_half = add_low(keep, swap(send, core_mask()))
    blocks, phase = scatter_blocks(dense_half)
    grad_up, grad_down = kernel_call(
        functools.partial(weight_grad_kernel, len(far) // 2),
        [((width, piece), F32), ((piece, width), F32)],
        16 * rows_here * width * chips * piece,
        weights[0],
        after(kept, dense_half),
        row_parts[1],
        row_parts[0],
        *far,
        fetch=range(4 + len(far)),
        scratch=56,
    )
    normed_grad = times_back(after(joint_grad, phase), in_halves)
    gain_rel = stack([part[:, experts] for part in halves]).astype(F32)
    input_grad_rel = jax.vjp(lambda v: rms_scale(v, gain_rel), inputs_rel)[1](normed_grad)[0]
    large = input_grad_rel.astype(BF)
    rest = (input_grad_rel - large.astype(F32)).astype(BF)
    input_grad = contract_cols(large, shuffle) + contract_cols(rest, shuffle)
    token_grad = (first_grad + input_grad).astype(BF)

    returned = exchange(after(result_own, token_grad))
    routed = [matmul(hot[c], returned) for c in range(2)]
    first, gates = high[:, :width], high[:, width : width + 2]
    mixed = (first + gates[:, 0:1] * routed[0] + gates[:, 1:2] * routed[1]).astype(BF)
    grad_in, sum_out, sum_small, grad_first_gain = kernel_call(
        finish_kernel,
        [
            ((share, 3 * width), F32),
            ((share, width), F32),
            ((share, spread_lanes), F32),
            ((share, 1), F32),
        ],
        share * width * 8,
        project_in,
        first_gain[:, None],
        after(blocks[0], mixed),
        *blocks[1:],
    )
    table_total = sum_small[:, table_at : table_at + table_lanes(share)]
    table_total = table_total.reshape(HEADS, BUCKETS).T
    return (
        mixed,
        token_grad,
        grad_in,
        sum_out,
        sum_small[:, :experts],
        grad_first_gain[:, 0],
        sum_small[:, experts],
        table_total,
        grad_up[None],
        grad_down[None],
    )


def solution(mesh):
    rows = P(("fsdp", "expert"), None)
    line = P(("fsdp", "expert"))
    up, down = P("expert", None, "fsdp"), P("expert", "fsdp", None)
    return jax.shard_map(
        on_device,
        mesh=mesh,
        in_specs=(rows, rows, rows, rows, rows, line, line, P(), up, down, line, P(), rows, rows),
        out_specs=(rows, rows, rows, rows, rows, line, line, P(), up, down),
        check_vma=False,
    )
```

time: 621 us -> 254 us (0.41)
  blocking collectives: 185 us -> 22.1 us
  waiting for transfers between devices: 233 us -> 90.4 us
  local copies, waits for them, and re-layouts: 109 us -> 24.2 us
  Pallas kernels: 0 us -> 52.3 us
  matrix products: 60.6 us -> 9.92 us
  starting transfers between devices: 11.5 us -> 39.7 us
  between operations: 14.8 us -> 1.13 us
  other arithmetic: 5.51 us -> 13.1 us
    reduce_scatter x4 -> x0, waiting for transfers between devices: 208 us -> none  [the longest x1 125 us: on_device(): lax.psum_scatter(grad_triple, ('fsdp', 'expert'), scatter_dimension=0, ti...]
    gather x1 -> x0, local copies, waits for them, and re-layouts: 97.2 us -> none  [on_device(): bucket_pair = jnp.take(buckets, jnp.clip(distance, 0, count - 1))]
    unnamed x2 -> x0, blocking collectives: 81.9 us -> none
    ppermute x0 -> x23, waiting for transfers between devices: none -> 71.8 us  [swap(): lax.ppermute(value, AXES, [(i, i ^ mask) for i in range(columns * experts)])]
    all_gather x1 -> x0, blocking collectives: 65.5 us -> none  [on_device(): lax.all_gather(router, ('fsdp', 'expert'), axis=0, tiled=True)]
    pallas_call x0 -> x16, Pallas kernels: none -> 52.3 us  [the longest x6 52.3 us: kernel_call(): pl.pallas_call(kernel, out_shape=[jax.ShapeDtypeStruct(shape, kind) for s...]
    ppermute x0 -> x23, starting transfers between devices: none -> 21 us  [swap(): lax.ppermute(value, AXES, [(i, i ^ mask) for i in range(columns * experts)])]
    dot_general x17 -> x5, matrix products: 22.6 us -> 3.25 us  [the longest x3 2.86 us: matmul(): return jnp.dot(left, right, preferred_element_type=F32)]
  transfers between devices with their start and end apart: 10 -> 26, of which waited for: 6 -> 14; matrix products, arithmetic and copies ran while one was open for 26% -> 11% of each run, Pallas kernels for 0% -> 8%
where the time goes in v1:
time: 254 us; the launch traced here: 253 us
  waiting for transfers between devices  90.4 us (36%)
  Pallas kernels  52.3 us (21%)
  starting transfers between devices  39.7 us (16%)
  local copies, waits for them, and re-layouts  24.2 us (10%)
  blocking collectives  22.1 us (9%)
  other arithmetic  13.1 us (5%)
  matrix products  9.92 us (4%)
    ppermute x23, waiting for transfers between devices, swap(): lax.ppermute(value, AXES, [(i, i ^ mask) for i in range(columns * experts)])  71.8 us
    pallas_call x6, Pallas kernels, kernel_call(): pl.pallas_call(kernel, out_shape=[jax.ShapeDtypeStruct(shape, kind) for s...  52.3 us
    all_to_all x1, blocking collectives, exchange(): lax.all_to_all(blocks, 'expert', split_axis=0, concat_axis=0, tiled=True)  22.1 us
    ppermute x23, starting transfers between devices, swap(): lax.ppermute(value, AXES, [(i, i ^ mask) for i in range(columns * experts)])  21 us
    all_to_all x3, starting transfers between devices, exchange(): lax.all_to_all(blocks, 'expert', split_axis=0, concat_axis=0, tiled=True)  18.7 us
    all_to_all x3, waiting for transfers between devices, exchange(): lax.all_to_all(blocks, 'expert', split_axis=0, concat_axis=0, tiled=True)  18.6 us
    unnamed x76, local copies, waits for them, and re-layouts  15.1 us
    convert_element_type x3, other arithmetic, add_low(): return (own.astype(F32) + arrived.astype(F32)).astype(BF)  6.07 us
  transfers between devices with their start and end apart: 26, of which 14 were waited for; matrix products, arithmetic and copies ran while one was open for 11% of the time, Pallas kernels for 8%

profile of v1, /device:TPU:0, one launch (start us, length us, event | category | flops | bytes accessed | tf_op | source)
XLA Modules:
  0.0 252.8 jit_solution(18027622541675656562)
XLA Ops:
  0.7 1.8 shard_map.222
  2.4 3.1 %collective-permute-start = (bf16[24,3200]{1,0:T(8,128)(2,1)}, bf16[24,3200]{1,0:T(8,128)(2,1)S(1)}, u32[]{:S(2)}, u32[]{:S(2)}) collective-permute-start(bf16[24,3200]{1,0:T(8,128)(2,1)} %shard_map.222), channel_id=1, source_target_pairs={{0,2},{1,3},{2,0},{3,1},{4,6},{5,7},{6,4},{7,5},{8,10},{9,11},{10,... | collective-permute-start | bytes 460808 | tf_op jit(solution)/shard_map/ppermute | solution.py:67
  5.5 2.6 %collective-permute-start.1 = (bf16[24,3200]{1,0:T(8,128)(2,1)}, bf16[24,3200]{1,0:T(8,128)(2,1)S(1)}, u32[]{:S(2)}, u32[]{:S(2)}) collective-permute-start(bf16[24,3200]{1,0:T(8,128)(2,1)} %shard_map.222), channel_id=1, source_target_pairs={{0,4},{1,5},{2,6},{3,7},{4,0},{5,1},{6,2},{7,3},{8,12},{9,13},{10,... | collective-permute-start | bytes 460808 | tf_op jit(solution)/shard_map/ppermute | solution.py:67
  9.7 1.6 pad_maximum_fusion.1.refs_1_.refs_0_
  11.9 8.2 %collective-permute-done.1 = bf16[24,3200]{1,0:T(8,128)(2,1)S(1)} collective-permute-done((bf16[24,3200]{1,0:T(8,128)(2,1)}, bf16[24,3200]{1,0:T(8,128)(2,1)S(1)}, u32[]{:S(2)}, u32[]{:S(2)}) %collective-permute-start.1) | collective-permute-done | bytes 153632 | tf_op jit(solution)/shard_map/ppermute | solution.py:67
  24.5 13.5 %collective-permute-done.3 = bf16[96,3200]{1,0:T(8,128)(2,1)S(1)} collective-permute-done((bf16[96,3200]{1,0:T(8,128)(2,1)}, bf16[96,3200]{1,0:T(8,128)(2,1)S(1)}, u32[]{:S(2)}, u32[]{:S(2)}) %collective-permute-start.3) | collective-permute-done | bytes 614432 | tf_op jit(solution)/shard_map/ppermute | solution.py:67
  38.0 10.7 %collective-permute-done.4 = bf16[96,3200]{1,0:T(8,128)(2,1)S(1)} collective-permute-done((bf16[96,3200]{1,0:T(8,128)(2,1)}, bf16[96,3200]{1,0:T(8,128)(2,1)S(1)}, u32[]{:S(2)}, u32[]{:S(2)}) %collective-permute-start.4) | collective-permute-done | bytes 614432 | tf_op jit(solution)/shard_map/ppermute | solution.py:67
  51.6 7.2 %all-to-all-start = ((bf16[8,48,768]{2,1,0:T(8,128)(2,1)}), bf16[8,48,768]{2,1,0:T(8,128)(2,1)S(1)}, u32[]{:S(2)}, u32[]{:S(2)}) async-start(bf16[8,48,768]{2,1,0:T(8,128)(2,1)} %bitcast.63), calls=%async_computation | async-start | bytes 1179648 | tf_op jit(solution)/shard_map/all_to_all | solution.py:122
  60.2 1.7 copy-done.2
  61.9 8.2 %shard_map.224 = (bf16[128,4608]{1,0:T(8,128)(2,1)S(1)}, f32[128,2432]{1,0:T(8,128)S(1)}, bf16[384,896]{1,0:T(8,128)(2,1)S(1)}) custom-call(bf16[128,768]{1,0:T(8,128)(2,1)S(1)} %copy-done.10, s32[1,768]{1,0:T(1,128)S(1)} %broadcast_in_dim.16.refs_1_.refs_4_, bf16[384,3200]{1,0:T(8,128)(2,1)S(1)} %copy-done.2, ...), custom_call_target="tpu_custom_call" | custom-call | flops 905969664 | bytes 8236544 | tf_op jit(solution)/shard_map/pallas_call | solution.py:176
  73.0 2.2 all-to-all-done
  76.0 22.1 %all_to_all.20 = bf16[8,48,896]{2,1,0:T(8,128)(2,1)S(1)} all-to-all(bf16[8,48,896]{2,1,0:T(8,128)(2,1)} %bitcast.46), channel_id=1, replica_groups=mesh['fsdp'=4,'expert'=8] {'expert'}, dimensions={0} | all-to-all | bytes 1376256 | tf_op jit(solution)/shard_map/all_to_all | solution.py:122
  98.6 2.6 %collective-permute-done.8.refs_3_ = bf16[384,768]{1,0:T(8,128)(2,1)S(1)} collective-permute-done((bf16[384,768]{1,0:T(8,128)(2,1)}, bf16[384,768]{1,0:T(8,128)(2,1)S(1)}, u32[]{:S(2)}, u32[]{:S(2)}) %collective-permute-start.8) | collective-permute-done | bytes 589856 | tf_op jit(solution)/shard_map/ppermute | solution.py:67
  101.2 11.5 %collective-permute-done.9.refs_6_.refs_1_ = bf16[1536,768]{1,0:T(8,128)(2,1)} collective-permute-done((bf16[1536,768]{1,0:T(8,128)(2,1)}, bf16[1536,768]{1,0:T(8,128)(2,1)}, u32[]{:S(2)}, u32[]{:S(2)}) %collective-permute-start.9) | collective-permute-done | bytes 2359328 | tf_op jit(solution)/shard_map/ppermute | solution.py:67
  113.6 13.6 %shard_map.227 = (bf16[384,896]{1,0:T(8,128)(2,1)}, bf16[384,896]{1,0:T(8,128)(2,1)}, bf16[768,768]{1,0:T(8,128)(2,1)}, bf16[768,2304]{1,0:T(8,128)(2,1)}) custom-call(s32[1,1]{1,0:T(1,128)} %bitcast.10.refs_0_, bf16[384,896]{1,0:T(8,128)(2,1)} %copy-done.33, bf16[384,896]{1,0:T(8,128)(2,1)} %bitcast.60, bf16[384,768]{1,0:T(8,128)(2,1)} %copy-done.34, ...), custom_call_target="tpu_custom_call" | custom-call | flops 7247757312 | bytes 13369348 | tf_op jit(solution)/shard_map/pallas_call | solution.py:176
  127.3 2.1 copy.74.refs_0_
  131.0 5.8 %all-to-all-start.2 = ((bf16[8,48,896]{2,1,0:T(8,128)(2,1)}), bf16[8,48,896]{2,1,0:T(8,128)(2,1)S(1)}, u32[]{:S(2)}, u32[]{:S(2)}) async-start(bf16[8,48,896]{2,1,0:T(8,128)(2,1)} %bitcast.16), calls=%async_computation.2 | async-start | bytes 1376256 | tf_op jit(solution)/shard_map/all_to_all | solution.py:122
  139.3 8.6 %collective-permute-done.12.refs_2_.refs_4_ = bf16[384,896]{1,0:T(8,128)(2,1)S(1)} collective-permute-done((bf16[384,896]{1,0:T(8,128)(2,1)}, bf16[384,896]{1,0:T(8,128)(2,1)S(1)}, u32[]{:S(2)}, u32[]{:S(2)}) %collective-permute-start.12) | collective-permute-done | bytes 688160 | tf_op jit(solution)/shard_map/ppermute | solution.py:67
  147.9 12.3 %collective-permute-done.14.refs_4_.refs_6_ = bf16[384,768]{1,0:T(8,128)(2,1)} collective-permute-done((bf16[384,768]{1,0:T(8,128)(2,1)}, bf16[384,768]{1,0:T(8,128)(2,1)}, u32[]{:S(2)}, u32[]{:S(2)}) %collective-permute-start.14) | collective-permute-done | bytes 589856 | tf_op jit(solution)/shard_map/ppermute | solution.py:67
  162.4 2.1 add_convert_fusion.3.refs_1_.refs_0_
  165.5 14.7 %shard_map.231 = (bf16[384,3200]{1,0:T(8,128)(2,1)}, bf16[384,3200]{1,0:T(8,128)(2,1)}, f32[128,768]{1,0:T(8,128)}, bf16[128,2304]{1,0:T(8,128)(2,1)}, f32[12,128]{1,0:T(8,128)}) custom-call(bf16[384,896]{1,0:T(8,128)(2,1)} %shard_map.230.refs_0_, s32[128,2]{1,0:T(8,128)} %copy-done.8, s32[128,2]{1,0:T(8,128)} %copy.65.refs_2_, bf16[128,768]{1,0:T(8,128)(2,1)} %refs_3_.3, ...), custom_call_target="tpu_custom_call" | custom-call | flops 1509949440 | bytes 14150656 | tf_op jit(solution)/shard_map/pallas_call | solution.py:176
  183.3 2.2 collective-permute-done.16
  185.4 3.0 %add_convert_fusion.refs_1_ = bf16[384,3200]{1,0:T(8,128)(2,1)S(1)} fusion(bf16[384,3200]{1,0:T(8,128)(2,1)} %collective-permute-done.16, bf16[384,3200]{1,0:T(8,128)(2,1)} %get-tuple-element.35), kind=kLoop, calls=%fused_computation | loop fusion | flops 4915200 | bytes 7372800 | tf_op jit(solution)/shard_map/convert_element_type | solution.py:107
  191.7 1.7 collective-permute-start.18
  194.7 13.2 %shard_map.237 = (f32[768,768]{1,0:T(8,128)}, f32[768,768]{1,0:T(8,128)}) custom-call(bf16[1536,768]{1,0:T(8,128)(2,1)} %shard_map.226.refs_5_.refs_0_, bf16[768,2304]{1,0:T(8,128)(2,1)} %shard_map.236.refs_1_, bf16[384,896]{1,0:T(8,128)(2,1)} %copy-done.33, bf16[384,896]{1,0:T(8,128)(2,1)} %bitcast.62, bf16[384,896]{1,0:T(8,128)(2,1)} %copy-done.21, ...), custom_call_target="tpu_custom_call" | custom-call | flops 7247757312 | bytes 14548992 | tf_op jit(solution)/shard_map/pallas_call | solution.py:176
  208.9 1.8 fusion.5
  210.7 2.1 fusion.3
  215.7 5.7 %all-to-all-start.3 = ((bf16[8,48,768]{2,1,0:T(8,128)(2,1)}), bf16[8,48,768]{2,1,0:T(8,128)(2,1)S(1)}, u32[]{:S(2)}, u32[]{:S(2)}) async-start(bf16[8,48,768]{2,1,0:T(8,128)(2,1)} %bitcast.50), calls=%async_computation.3 | async-start | bytes 1179648 | tf_op jit(solution)/shard_map/all_to_all | solution.py:122
  222.0 1.8 add_convert_fusion.2
  226.0 2.4 collective-permute-start.21
  228.9 16.4 %all-to-all-done.3 = bf16[8,48,768]{2,1,0:T(8,128)(2,1)S(1)} async-done(((bf16[8,48,768]{2,1,0:T(8,128)(2,1)}), bf16[8,48,768]{2,1,0:T(8,128)(2,1)S(1)}, u32[]{:S(2)}, u32[]{:S(2)}) %all-to-all-start.3) | async-done | bytes 589856 | tf_op jit(solution)/shard_map/all_to_all | solution.py:122
  245.6 2.0 add_convert_fusion.4.refs_1_
  (151 shorter events, 43.3 us)
Async XLA Ops:
  0.6 59.4 %copy-start = (f32[32,12]{0,1:T(8,128)S(1)}, f32[32,12]{0,1:T(8,128)}, u32[]{:S(2)}) copy-start(f32[32,12]{0,1:T(8,128)} %param.22) | copy-start | bytes 4612
  2.4 9.5 %collective-permute-start = (bf16[24,3200]{1,0:T(8,128)(2,1)}, bf16[24,3200]{1,0:T(8,128)(2,1)S(1)}, u32[]{:S(2)}, u32[]{:S(2)}) collective-permute-start(bf16[24,3200]{1,0:T(8,128)(2,1)} %shard_map.222), channel_id=1, source_target_pairs={{0,2},{1,3},{2,0},{3,1},{4,6},{5,7},{6,4},{7,5},{8,10},{9,11},{10,... | collective-permute-start | bytes 460808 | tf_op jit(solution)/shard_map/ppermute | solution.py:67
  5.5 14.6 %collective-permute-start.1 = (bf16[24,3200]{1,0:T(8,128)(2,1)}, bf16[24,3200]{1,0:T(8,128)(2,1)S(1)}, u32[]{:S(2)}, u32[]{:S(2)}) collective-permute-start(bf16[24,3200]{1,0:T(8,128)(2,1)} %shard_map.222), channel_id=1, source_target_pairs={{0,4},{1,5},{2,6},{3,7},{4,0},{5,1},{6,2},{7,3},{8,12},{9,13},{10,... | collective-permute-start | bytes 460808 | tf_op jit(solution)/shard_map/ppermute | solution.py:67
  8.1 12.0 %collective-permute-start.2 = (bf16[24,3200]{1,0:T(8,128)(2,1)}, bf16[24,3200]{1,0:T(8,128)(2,1)S(1)}, u32[]{:S(2)}, u32[]{:S(2)}) collective-permute-start(bf16[24,3200]{1,0:T(8,128)(2,1)} %shard_map.222), channel_id=1, source_target_pairs={{0,6},{1,7},{2,4},{3,5},{4,2},{5,3},{6,0},{7,1},{8,14},{9,15},{10,... | collective-permute-start | bytes 460808 | tf_op jit(solution)/shard_map/ppermute | solution.py:67
  21.0 29.1 %copy-start.28 = (s32[128,2]{0,1:T(2,128)S(1)}, s32[128,2]{0,1:T(2,128)}, u32[]{:S(2)}) copy-start(s32[128,2]{0,1:T(2,128)} %param.27) | copy-start | bytes 3076
  21.0 29.1 %copy-start.31 = (s32[128,2]{0,1:T(2,128)S(1)}, s32[128,2]{0,1:T(2,128)}, u32[]{:S(2)}) copy-start(s32[128,2]{0,1:T(2,128)} %param.28) | copy-start | bytes 3076
  21.0 29.3 %copy-start.20 = (bf16[128,768]{1,0:T(8,128)(2,1)S(1)}, bf16[128,768]{1,0:T(8,128)(2,1)}, u32[]{:S(2)}) copy-start(bf16[128,768]{1,0:T(8,128)(2,1)} %refs_3_.3) | copy-start | bytes 589828
  21.0 17.0 %collective-permute-start.3 = (bf16[96,3200]{1,0:T(8,128)(2,1)}, bf16[96,3200]{1,0:T(8,128)(2,1)S(1)}, u32[]{:S(2)}, u32[]{:S(2)}) collective-permute-start(bf16[96,3200]{1,0:T(8,128)(2,1)} %shard_map.223), channel_id=1, source_target_pairs={{0,16},{1,17},{2,18},{3,19},{4,20},{5,21},{6,22},{7,23},{8,24},{9,... | collective-permute-start | bytes 1843208 | tf_op jit(solution)/shard_map/ppermute | solution.py:67
  22.5 26.2 %collective-permute-start.4 = (bf16[96,3200]{1,0:T(8,128)(2,1)}, bf16[96,3200]{1,0:T(8,128)(2,1)S(1)}, u32[]{:S(2)}, u32[]{:S(2)}) collective-permute-start(bf16[96,3200]{1,0:T(8,128)(2,1)} %shard_map.223), channel_id=1, source_target_pairs={{0,1},{1,0},{2,3},{3,2},{4,5},{5,4},{6,7},{7,6},{8,9},{9,8},{10,11... | collective-permute-start | bytes 1843208 | tf_op jit(solution)/shard_map/ppermute | solution.py:67
  24.0 24.7 %collective-permute-start.5 = (bf16[96,3200]{1,0:T(8,128)(2,1)}, bf16[96,3200]{1,0:T(8,128)(2,1)S(1)}, u32[]{:S(2)}, u32[]{:S(2)}) collective-permute-start(bf16[96,3200]{1,0:T(8,128)(2,1)} %shard_map.223), channel_id=1, source_target_pairs={{0,17},{1,16},{2,19},{3,18},{4,21},{5,20},{6,23},{7,22},{8,25},{9,... | collective-permute-start | bytes 1843208 | tf_op jit(solution)/shard_map/ppermute | solution.py:67
  50.0 10.2 %collective-permute-start.6 = (bf16[384,3200]{1,0:T(8,128)(2,1)S(1)}, bf16[384,3200]{1,0:T(8,128)(2,1)}, u32[]{:S(2)}, u32[]{:S(2)}) collective-permute-start(bf16[384,3200]{1,0:T(8,128)(2,1)S(1)} %pad_maximum_fusion.refs_2_.refs_1_.refs_7_), channel_id=1, source_target_pairs={{0,8},{1,9},{2,10},{3,11},{4,12},{5,13},{6,14},{7,15},{8,0},{9,1},... | collective-permute-start | bytes 7372808 | tf_op jit(solution)/shard_map/ppermute | solution.py:67
  51.6 23.5 %all-to-all-start = ((bf16[8,48,768]{2,1,0:T(8,128)(2,1)}), bf16[8,48,768]{2,1,0:T(8,128)(2,1)S(1)}, u32[]{:S(2)}, u32[]{:S(2)}) async-start(bf16[8,48,768]{2,1,0:T(8,128)(2,1)} %bitcast.63), calls=%async_computation | async-start | bytes 1179648 | tf_op jit(solution)/shard_map/all_to_all | solution.py:122
  59.1 53.6 %collective-permute-start.9 = (bf16[1536,768]{1,0:T(8,128)(2,1)}, bf16[1536,768]{1,0:T(8,128)(2,1)}, u32[]{:S(2)}, u32[]{:S(2)}) collective-permute-start(bf16[1536,768]{1,0:T(8,128)(2,1)} %shard_map.226.refs_5_.refs_0_), channel_id=1, source_target_pairs={{0,16},{1,17},{2,18},{3,19},{4,20},{5,21},{6,22},{7,23},{8,24},{9,... | collective-permute-start | bytes 7077896 | tf_op jit(solution)/shard_map/ppermute | solution.py:67
  98.1 14.6 %collective-permute-start.7 = (bf16[384,896]{1,0:T(8,128)(2,1)S(1)}, bf16[384,896]{1,0:T(8,128)(2,1)S(1)}, u32[]{:S(2)}, u32[]{:S(2)}) collective-permute-start(bf16[384,896]{1,0:T(8,128)(2,1)S(1)} %bitcast.59), channel_id=1, source_target_pairs={{0,8},{1,9},{2,10},{3,11},{4,12},{5,13},{6,14},{7,15},{8,0},{9,1},... | collective-permute-start | bytes 2064392 | tf_op jit(solution)/shard_map/ppermute | solution.py:67
  98.1 3.1 %collective-permute-start.8 = (bf16[384,768]{1,0:T(8,128)(2,1)}, bf16[384,768]{1,0:T(8,128)(2,1)S(1)}, u32[]{:S(2)}, u32[]{:S(2)}) collective-permute-start(bf16[384,768]{1,0:T(8,128)(2,1)} %bitcast.53), channel_id=1, source_target_pairs={{0,8},{1,9},{2,10},{3,11},{4,12},{5,13},{6,14},{7,15},{8,0},{9,1},... | collective-permute-start | bytes 1769480 | tf_op jit(solution)/shard_map/ppermute | solution.py:67
  127.2 2.7 %collective-permute-start.11 = (bf16[384,896]{1,0:T(8,128)(2,1)}, bf16[384,896]{1,0:T(8,128)(2,1)S(1)}, u32[]{:S(2)}, u32[]{:S(2)}) collective-permute-start(bf16[384,896]{1,0:T(8,128)(2,1)} %get-tuple-element.31), channel_id=1, source_target_pairs={{0,8},{1,9},{2,10},{3,11},{4,12},{5,13},{6,14},{7,15},{8,0},{9,1},... | collective-permute-start | bytes 2064392 | tf_op jit(solution)/shard_map/ppermute | solution.py:67
  129.4 18.4 %collective-permute-start.12 = (bf16[384,896]{1,0:T(8,128)(2,1)}, bf16[384,896]{1,0:T(8,128)(2,1)S(1)}, u32[]{:S(2)}, u32[]{:S(2)}) collective-permute-start(bf16[384,896]{1,0:T(8,128)(2,1)} %shard_map.228), channel_id=1, source_target_pairs={{0,16},{1,17},{2,18},{3,19},{4,20},{5,21},{6,22},{7,23},{8,24},{9,... | collective-permute-start | bytes 2064392 | tf_op jit(solution)/shard_map/ppermute | solution.py:67
  131.0 33.4 %all-to-all-start.2 = ((bf16[8,48,896]{2,1,0:T(8,128)(2,1)}), bf16[8,48,896]{2,1,0:T(8,128)(2,1)S(1)}, u32[]{:S(2)}, u32[]{:S(2)}) async-start(bf16[8,48,896]{2,1,0:T(8,128)(2,1)} %bitcast.16), calls=%async_computation.2 | async-start | bytes 1376256 | tf_op jit(solution)/shard_map/all_to_all | solution.py:122
  136.8 23.3 %collective-permute-start.14 = (bf16[384,768]{1,0:T(8,128)(2,1)}, bf16[384,768]{1,0:T(8,128)(2,1)}, u32[]{:S(2)}, u32[]{:S(2)}) collective-permute-start(bf16[384,768]{1,0:T(8,128)(2,1)} %shard_map.229), channel_id=1, source_target_pairs={{0,16},{1,17},{2,18},{3,19},{4,20},{5,21},{6,22},{7,23},{8,24},{9,... | collective-permute-start | bytes 1769480 | tf_op jit(solution)/shard_map/ppermute | solution.py:67
  139.3 23.1 %collective-permute-start.10 = (bf16[384,768]{1,0:T(8,128)(2,1)}, bf16[384,768]{1,0:T(8,128)(2,1)}, u32[]{:S(2)}, u32[]{:S(2)}) collective-permute-start(bf16[384,768]{1,0:T(8,128)(2,1)} %slice.89), channel_id=1, source_target_pairs={{0,8},{1,9},{2,10},{3,11},{4,12},{5,13},{6,14},{7,15},{8,0},{9,1},... | collective-permute-start | bytes 1769480 | tf_op jit(solution)/shard_map/ppermute | solution.py:67
  147.9 16.6 %copy-start.21 = (bf16[384,896]{1,0:T(8,128)(2,1)}, bf16[384,896]{1,0:T(8,128)(2,1)S(1)}, u32[]{:S(2)}) copy-start(bf16[384,896]{1,0:T(8,128)(2,1)S(1)} %collective-permute-done.12.refs_2_.refs_4_) | copy-start | bytes 2064388
  147.9 16.5 %collective-permute-start.13 = (bf16[384,896]{1,0:T(8,128)(2,1)S(1)}, bf16[384,896]{1,0:T(8,128)(2,1)S(1)}, u32[]{:S(2)}, u32[]{:S(2)}) collective-permute-start(bf16[384,896]{1,0:T(8,128)(2,1)S(1)} %collective-permute-done.12.refs_2_.refs_4_), channel_id=1, source_target_pairs={{0,8},{1,9},{2,10},{3,11},{4,12},{5,13},{6,14},{7,15},{8,0},{9,1},... | collective-permute-start | bytes 2064392 | tf_op jit(solution)/shard_map/ppermute | solution.py:67
  160.2 4.3 %collective-permute-start.15 = (bf16[384,768]{1,0:T(8,128)(2,1)}, bf16[384,768]{1,0:T(8,128)(2,1)}, u32[]{:S(2)}, u32[]{:S(2)}) collective-permute-start(bf16[384,768]{1,0:T(8,128)(2,1)} %collective-permute-done.14.refs_4_.refs_6_), channel_id=1, source_target_pairs={{0,8},{1,9},{2,10},{3,11},{4,12},{5,13},{6,14},{7,15},{8,0},{9,1},... | collective-permute-start | bytes 1769480 | tf_op jit(solution)/shard_map/ppermute | solution.py:67
  180.2 5.2 %collective-permute-start.16 = (bf16[384,3200]{1,0:T(8,128)(2,1)}, bf16[384,3200]{1,0:T(8,128)(2,1)}, u32[]{:S(2)}, u32[]{:S(2)}) collective-permute-start(bf16[384,3200]{1,0:T(8,128)(2,1)} %get-tuple-element.36), channel_id=1, source_target_pairs={{0,8},{1,9},{2,10},{3,11},{4,12},{5,13},{6,14},{7,15},{8,0},{9,1},... | collective-permute-start | bytes 7372808 | tf_op jit(solution)/shard_map/ppermute | solution.py:67
  191.2 16.9 %collective-permute-start.17 = (bf16[96,3200]{1,0:T(8,128)(2,1)}, bf16[96,3200]{1,0:T(8,128)(2,1)S(1)}, u32[]{:S(2)}, u32[]{:S(2)}) collective-permute-start(bf16[96,3200]{1,0:T(8,128)(2,1)} %get-tuple-element.80), channel_id=1, source_target_pairs={{0,16},{1,17},{2,18},{3,19},{4,20},{5,21},{6,22},{7,23},{8,24},{9,... | collective-permute-start | bytes 1843208 | tf_op jit(solution)/shard_map/ppermute | solution.py:67
  191.7 29.7 %collective-permute-start.18 = (bf16[96,3200]{1,0:T(8,128)(2,1)}, bf16[96,3200]{1,0:T(8,128)(2,1)}, u32[]{:S(2)}, u32[]{:S(2)}) collective-permute-start(bf16[96,3200]{1,0:T(8,128)(2,1)} %get-tuple-element.78), channel_id=1, source_target_pairs={{0,1},{1,0},{2,3},{3,2},{4,5},{5,4},{6,7},{7,6},{8,9},{9,8},{10,11... | collective-permute-start | bytes 1843208 | tf_op jit(solution)/shard_map/ppermute | solution.py:67
  193.5 28.5 %collective-permute-start.19 = (bf16[96,3200]{1,0:T(8,128)(2,1)}, bf16[96,3200]{1,0:T(8,128)(2,1)}, u32[]{:S(2)}, u32[]{:S(2)}) collective-permute-start(bf16[96,3200]{1,0:T(8,128)(2,1)} %get-tuple-element.79), channel_id=1, source_target_pairs={{0,17},{1,16},{2,19},{3,18},{4,21},{5,20},{6,23},{7,22},{8,25},{9,... | collective-permute-start | bytes 1843208 | tf_op jit(solution)/shard_map/ppermute | solution.py:67
  215.7 29.6 %all-to-all-start.3 = ((bf16[8,48,768]{2,1,0:T(8,128)(2,1)}), bf16[8,48,768]{2,1,0:T(8,128)(2,1)S(1)}, u32[]{:S(2)}, u32[]{:S(2)}) async-start(bf16[8,48,768]{2,1,0:T(8,128)(2,1)} %bitcast.50), calls=%async_computation.3 | async-start | bytes 1179648 | tf_op jit(solution)/shard_map/all_to_all | solution.py:122
  223.8 24.6 %copy-start.9 = (bf16[24,2304]{1,0:T(8,128)(2,1)S(1)}, bf16[24,2304]{1,0:T(8,128)(2,1)}, u32[]{:S(2)}) copy-start(bf16[24,2304]{1,0:T(8,128)(2,1)} %refs_0_.3) | copy-start | bytes 331780
  224.5 23.0 %collective-permute-start.20 = (bf16[24,3200]{1,0:T(8,128)(2,1)S(1)}, bf16[24,3200]{1,0:T(8,128)(2,1)S(1)}, u32[]{:S(2)}, u32[]{:S(2)}) collective-permute-start(bf16[24,3200]{1,0:T(8,128)(2,1)S(1)} %get-tuple-element.83), channel_id=1, source_target_pairs={{0,2},{1,3},{2,0},{3,1},{4,6},{5,7},{6,4},{7,5},{8,10},{9,11},{10,... | collective-permute-start | bytes 460808 | tf_op jit(solution)/shard_map/ppermute | solution.py:67
  226.0 22.4 %collective-permute-start.21 = (bf16[24,3200]{1,0:T(8,128)(2,1)S(1)}, bf16[24,3200]{1,0:T(8,128)(2,1)S(1)}, u32[]{:S(2)}, u32[]{:S(2)}) collective-permute-start(bf16[24,3200]{1,0:T(8,128)(2,1)S(1)} %get-tuple-element.82), channel_id=1, source_target_pairs={{0,4},{1,5},{2,6},{3,7},{4,0},{5,1},{6,2},{7,3},{8,12},{9,13},{10,... | collective-permute-start | bytes 460808 | tf_op jit(solution)/shard_map/ppermute | solution.py:67
  228.3 20.0 %collective-permute-start.22 = (bf16[24,3200]{1,0:T(8,128)(2,1)S(1)}, bf16[24,3200]{1,0:T(8,128)(2,1)S(1)}, u32[]{:S(2)}, u32[]{:S(2)}) collective-permute-start(bf16[24,3200]{1,0:T(8,128)(2,1)S(1)} %get-tuple-element.81), channel_id=1, source_target_pairs={{0,6},{1,7},{2,4},{3,5},{4,2},{5,3},{6,0},{7,1},{8,14},{9,15},{10,... | collective-permute-start | bytes 460808 | tf_op jit(solution)/shard_map/ppermute | solution.py:67
  (30 other events, 150.2 us)

commit v2 on v1

--- a/solution.py
+++ b/solution.py
@@ -73,14 +73,6 @@
 
 def fan(value, masks):
     return [value] + [swap(value, mask) for mask in masks[1:]]
-
-
-def fan_sum(parts, masks):
-    arrived = [swap(part, mask) for part, mask in zip(parts[1:], masks[1:])]
-    total = parts[0].astype(F32)
-    for part in arrived:
-        total = total + part.astype(F32)
-    return total
 
 
 def stack(parts):
@@ -97,9 +89,9 @@
     )(value, *others)
 
 
-def gather_blocks(value, beside):
+def gather_blocks(value, early, late):
     value = stack(fan(value, z_masks()))
-    value = stack(fan(after(value, beside), xy_masks()))
+    value = after(stack(fan(after(value, *early), xy_masks())), *late)
     return value, swap(value, core_mask())
 
 
@@ -107,13 +99,30 @@
     return (own.astype(F32) + arrived.astype(F32)).astype(BF)
 
 
-def scatter_blocks(value):
+def sum_kernel(inputs, *refs):
+    total = sum((ref[...].astype(F32) for ref in refs[1:inputs]), refs[0][...].astype(F32))
+    rows = total.shape[0] // (len(refs) - inputs)
+    for i, ref in enumerate(refs[inputs:]):
+        ref[...] = total[i * rows : (i + 1) * rows].astype(BF)
+
+
+def sum_apart(parts, pieces):
+    rows, width = parts[0].shape
+    outs = [((rows // pieces, width), BF)] * pieces
+    return kernel_call(functools.partial(sum_kernel, len(parts)), outs, rows * width, *parts)
+
+
+def scatter_blocks(value, other, meanwhile):
     xy, z = xy_masks(), z_masks()
-    value = value.reshape(len(xy), -1, value.shape[1])
-    arrived = [swap(value[i], xy[i]) for i in range(1, len(xy))]
-    value = sum((part.astype(F32) for part in arrived), value[0].astype(F32)).astype(BF)
-    value = value.reshape(len(z), -1, value.shape[1])
-    return [value[0]] + [swap(value[i], z[i]) for i in range(1, len(z))], arrived[0]
+    parts = sum_apart([value, swap(other, core_mask())], len(xy))
+    arrived = fan_sends(parts, xy)
+    done = meanwhile(parts[0])
+    sums = sum_apart([after(parts[0], *done), *arrived], len(z))
+    return [sums[0], *fan_sends(sums, z)], done
+
+
+def fan_sends(parts, masks):
+    return [swap(part, mask) for part, mask in zip(parts[1:], masks[1:])]
 
 
 def exchange(value):
@@ -155,29 +164,53 @@
         return self.ref[index]
 
 
-def kernel_call(body, outs, flops, *operands, fetch=(), scratch=16):
+def kernel_call(body, outs, flops, *operands, fetch=(), push=(), scratch=16):
     moved = sum(math.prod(v.shape) * v.dtype.itemsize for v in operands)
     moved += sum(math.prod(shape) * jnp.dtype(kind).itemsize for shape, kind in outs)
-    taken = len(operands) + len(outs)
+    taken = len(operands)
+    fetch = [
+        item if isinstance(item, tuple) else (item, ..., operands[item].shape) for item in fetch
+    ]
+    push = list(push)
 
     def kernel(*refs):
-        refs, buffers = list(refs[:taken]), refs[taken:]
-        for i, number in enumerate(fetch):
-            copy = pltpu.make_async_copy(refs[number], buffers[i], buffers[-1].at[i])
+        buffers, refs = refs[taken + len(outs) :], list(refs[: taken + len(outs)])
+        arriving, leaving, sent = [], {}, []
+        for i, (number, index, _) in enumerate(fetch):
+            source = refs[number] if index is ... else refs[number].at[index]
+            copy = pltpu.make_async_copy(source, buffers[i], buffers[-1].at[i])
             refs[number] = Incoming(buffers[i], copy)
-        body(*refs)
-        for number in fetch:
-            refs[number].wait()
+            arriving.append(refs[number])
+        for i, number in enumerate(push, len(fetch)):
+            leaving[number] = pltpu.make_async_copy(
+                buffers[i], refs[taken + number], buffers[-1].at[i]
+            )
+            refs[taken + number] = buffers[i]
+
+        def send(number):
+            leaving[number].start()
+            sent.append(number)
+
+        body(*refs, *([send] if push else []))
+        for number in push:
+            if number not in sent:
+                send(number)
+        for value in arriving:
+            value.wait()
+        for number in push:
+            leaving[number].wait()
 
     whole, left = pl.BlockSpec(memory_space=pltpu.VMEM), pl.BlockSpec(memory_space=pl.ANY)
-    buffers = [pltpu.VMEM(operands[i].shape, operands[i].dtype) for i in fetch]
-    if fetch:
-        buffers.append(pltpu.SemaphoreType.DMA((len(fetch),)))
+    fetched = [number for number, _, _ in fetch]
+    buffers = [pltpu.VMEM(shape, operands[number].dtype) for number, _, shape in fetch]
+    buffers += [pltpu.VMEM(*outs[number]) for number in push]
+    if buffers:
+        buffers.append(pltpu.SemaphoreType.DMA((len(buffers),)))
     return pl.pallas_call(
         kernel,
         out_shape=[jax.ShapeDtypeStruct(shape, kind) for shape, kind in outs],
-        in_specs=[left if i in fetch else whole for i in range(len(operands))],
-        out_specs=[whole] * len(outs),
+        in_specs=[left if i in fetched else whole for i in range(taken)],
+        out_specs=[left if i in push else whole for i in range(len(outs))],
         scratch_shapes=buffers,
         compiler_params=pltpu.CompilerParams(vmem_limit_bytes=scratch * 1024 * 1024),
         cost_estimate=pl.CostEstimate(flops=flops, bytes_accessed=moved, transcendentals=0),
@@ -202,30 +235,38 @@
     return lax.rsqrt(jnp.mean(value * value, axis=-1, keepdims=True) + 1e-06)
 
 
+def small_lanes(experts):
+    return -(-(experts + 2) // LANES) * LANES
+
+
 def shuffle_of(place_of):
     width = place_of.shape[1]
     return (lax.broadcasted_iota(jnp.int32, (width, width), 0) == place_of[...]).astype(BF)
 
 
-def small_of(near, far, shuffle):
-    lanes = near.shape[1] - 4 * shuffle.shape[0]
-    rows = jnp.concatenate([near[:, :lanes], far[:, :lanes]], axis=0)
+def small_of(lanes, near, far, shuffle):
+    end = near.shape[1] - shuffle.shape[0]
+    start = end - lanes
+    rows = jnp.concatenate([near[:, start:end], far[:, start:end]], axis=0)
     return jnp.transpose(matmul(shuffle, rows)).astype(BF)
 
 
-def pack_kernel(router_rows, first_gain, second_gain, project_in, project_out, packed_ref):
+def pack_kernel(
+    router_rows, first_gain, second_gain, project_in, project_out, down, packed_ref, down_ref
+):
     share, columns = project_in.shape
     experts = router_rows.shape[0]
-    at = packed_ref.shape[1] - columns - project_out.shape[1]
+    lanes = packed_ref.shape[1] - columns - project_out.shape[1]
     eye = lax.broadcasted_iota(jnp.int32, (share, share), 0)
     eye = (eye == lax.broadcasted_iota(jnp.int32, (share, share), 1)).astype(BF)
     rows = jnp.concatenate(
-        [router_rows[...], first_gain[...], second_gain[...], jnp.zeros((at - experts - 2, share), BF)],
+        [router_rows[...], first_gain[...], second_gain[...], jnp.zeros((lanes - experts - 2, share), BF)],
         axis=0,
     )
-    packed_ref[:, :at] = nt(eye, rows).astype(BF)
-    packed_ref[:, at : at + columns] = project_in[...]
-    packed_ref[:, at + columns :] = project_out[...]
+    packed_ref[:, :columns] = project_in[...]
+    packed_ref[:, columns : columns + lanes] = nt(eye, rows).astype(BF)
+    packed_ref[:, columns + lanes :] = project_out[...]
+    down_ref[...] = down[...]
 
 
 def forward_kernel(
@@ -241,11 +282,12 @@
     low_ref,
     high_ref,
     outgoing_ref,
+    send,
 ):
     count, width = tokens.shape
     at_probs = width + LANES
     shuffle = shuffle_of(place_of)
-    small = small_of(near, far, shuffle)
+    small = small_of(small_lanes(experts), near, far, shuffle)
     half = width // 2
     inputs = tokens[...].astype(F32)
     gain_first = small[experts : experts + 1].astype(F32)
@@ -253,9 +295,8 @@
     normed = (inputs * inverse_rms(inputs) * gain_first).astype(BF)
     normed = matmul(normed, shuffle).astype(BF)
     low_ref[:, 3 * width : 4 * width] = normed
-    at = near.shape[1] - 4 * width
-    joint = matmul(normed[:, :half], near[:, at : at + 3 * width])
-    joint = joint + matmul(normed[:, half:], far[:, at : at + 3 * width])
+    joint = matmul(normed[:, :half], near[:, : 3 * width])
+    joint = joint + matmul(normed[:, half:], far[:, : 3 * width])
     low_ref[:, : 3 * width] = joint.astype(BF)
     row = lax.broadcasted_iota(jnp.int32, (count, count), 0)
     distance = row - lax.broadcasted_iota(jnp.int32, (count, count), 1)
@@ -279,11 +320,13 @@
         attended.append(pick_heads(*outs).astype(BF))
     attended = matmul(jnp.concatenate(attended, axis=1), shuffle).astype(BF)
     low_ref[:, 4 * width : 5 * width] = attended
-    first = inputs + matmul(attended[:, :half], near[:, at + 3 * width :])
-    first = first + matmul(attended[:, half:], far[:, at + 3 * width :])
+    at = near.shape[1] - width
+    first = inputs + matmul(attended[:, :half], near[:, at:])
+    first = first + matmul(attended[:, half:], far[:, at:])
     high_ref[:, :width] = first
     second = (first * inverse_rms(first) * gain_second).astype(BF)
     low_ref[:, 5 * width :] = second
+    send(0)
     logits = nt(second, small[:LANES])
     lane = lax.broadcasted_iota(jnp.int32, logits.shape, 1)
     chosen = [
@@ -294,6 +337,7 @@
     expo = [jnp.exp(value - top) for value in chosen]
     gates = [value / (expo[0] + expo[1]) for value in expo]
     high_ref[:, width:at_probs] = jnp.where(lane == 0, gates[0], jnp.where(lane == 1, gates[1], 0.0))
+    send(1)
     slot = lax.broadcasted_iota(jnp.int32, (outgoing_ref.shape[0], count), 0)
     rows = jnp.zeros(outgoing_ref.shape, F32)
     for c in range(2):
@@ -317,39 +361,42 @@
 
 
 def expert_kernel(chips, column, *refs):
-    rows, grads, weights, refs = refs[:2], refs[2:4], refs[4 : 4 + chips], refs[4 + chips :]
-    row_refs, result_ref, kept_ref = refs[:2], refs[2], refs[3]
+    rows, grads, refs = refs[:2], refs[2:4], refs[4:]
+    weights, downs, refs = refs[:chips], refs[chips : 2 * chips], refs[2 * chips :]
+    row_refs, kept_ref, shown_ref = refs[:2], refs[2], refs[3]
     count, width = grads[0].shape
-    hidden = weights[0].shape[0] // 2
+    hidden = (weights[0].shape[0] + downs[0].shape[0]) // 2
+    late = hidden - downs[0].shape[0]
     for core in range(2):
         packed, grad = rows[core], grads[core][...]
         gate = gate_of(packed, width)
         block = slice(core * count, (core + 1) * count)
         result, row_grad = jnp.zeros((count, width), F32), jnp.zeros((count, width), F32)
         for i in range(chips):
-            up, down = weights[i][:hidden], weights[i][hidden:]
+            up, down = weights[i][:hidden], (weights[i][hidden:], downs[i][...])
             active, slope = expert_forward(packed[:, :width], up)
-            inner_grad = nt(grad, down) * slope
+            inner_grad = jnp.concatenate([nt(grad, part) for part in down], axis=1) * slope
             if i == 0:
                 kept_ref[block, :hidden] = active
                 kept_ref[block, hidden : 2 * hidden] = (inner_grad * gate).astype(BF)
-            result = result + matmul(active, down)
+            result = result + matmul(active[:, :late], down[0]) + matmul(active[:, late:], down[1])
             row_grad = row_grad + matmul(inner_grad.astype(BF), up)
         grad = grad.astype(F32)
-        kept_ref[block, 2 * hidden :] = (grad * gate).astype(BF)
-        result_ref[block] = result.astype(BF)
+        scaled = (grad * gate).astype(BF)
+        kept_ref[block, 2 * hidden :] = scaled
         dots = jnp.sum(result * grad, axis=-1, keepdims=True)
         row_refs[core][...] = jnp.concatenate(
-            [row_grad.astype(BF), lanes_of(dots, 2 * column[0, 0])], axis=1
+            [row_grad.astype(BF), lanes_of(dots, 2 * column[0, 0]), result.astype(BF)], axis=1
         )
-
-
-def weight_grad_kernel(others, weights, kept, far, near, *refs):
-    packed_far, grads_far, (up_ref, down_ref) = refs[:others], refs[others : 2 * others], refs[2 * others :]
-    width = up_ref.shape[0]
-    hidden = up_ref.shape[1]
+    shown_ref[:count] = packed[:, :width]
+    shown_ref[count:] = scaled
+
+
+def weight_grad_kernel(weights, down_late, kept, far, near, *refs):
+    others, (up_ref, down_ref) = refs[:-2], refs[-2:]
+    width, hidden = up_ref.shape
     count = near.shape[0]
-    up, down = weights[:hidden], weights[hidden:]
+    up, down = weights[:hidden], (weights[hidden:], down_late[...])
     for i, rows in enumerate((far, near)):
         block = slice(i * count, (i + 1) * count)
         scaled = kept[block, 2 * hidden :]
@@ -362,13 +409,12 @@
         else:
             up_ref[...] += parts[0]
             down_ref[...] += parts[1]
-    for packed, grad_ref in zip(packed_far, grads_far):
-        gate = gate_of(packed, width)
-        grad = grad_ref[...]
-        active, slope = expert_forward(packed[:, :width], up)
-        inner_grad = (nt(grad, down) * slope * gate).astype(BF)
-        up_ref[...] += tn(packed[:, :width], inner_grad)
-        down_ref[...] += tn(active, (grad.astype(F32) * gate).astype(BF))
+    for ref in others:
+        rows, scaled = ref[:count], ref[count:]
+        active, slope = expert_forward(rows, up)
+        inner_grad = jnp.concatenate([nt(scaled, part) for part in down], axis=1)
+        up_ref[...] += tn(rows, (inner_grad * slope).astype(BF))
+        down_ref[...] += tn(active, scaled)
 
 
 def table_lanes(share):
@@ -397,12 +443,13 @@
     count, width = cotangent.shape
     half = width // 2
     shuffle = shuffle_of(place_of)
-    small_rows = small_of(near, far, shuffle)
+    small_rows = small_of(small_lanes(experts), near, far, shuffle)
     at_probs = width + LANES
     slot = lax.broadcasted_iota(jnp.int32, (count, home.shape[0]), 1)
     lane = lax.broadcasted_iota(jnp.int32, (count, LANES), 1)
     gates = [high[:, width + c : width + c + 1] for c in range(2)]
-    routed = [matmul((slot == target[:, c : c + 1]).astype(BF), home[...]) for c in range(2)]
+    back = home[:, : width + LANES]
+    routed = [matmul((slot == target[:, c : c + 1]).astype(BF), back) for c in range(2)]
     dots = [jnp.sum(value[:, width:], axis=-1, keepdims=True) for value in routed]
     mean = gates[0] * dots[0] + gates[1] * dots[1]
     logit_grad = jnp.zeros((count, LANES), F32)
@@ -497,16 +544,86 @@
         ref[:, 4 * width :] = small[at : at + half].astype(BF)
 
 
-def finish_kernel(project_in, gain, *refs):
-    parts, (grad_in_ref, sum_out_ref, small_ref, gain_ref) = refs[:-4], refs[-4:]
+def token_kernel(
+    experts,
+    tokens,
+    first_grad,
+    joint_grad,
+    near,
+    far,
+    place_of,
+    returned,
+    target,
+    high,
+    token_ref,
+    mixed_ref,
+):
+    count, width = tokens.shape
+    slot = lax.broadcasted_iota(jnp.int32, (count, returned.shape[0]), 1)
+    mixed = high[:, :width]
+    for c in range(2):
+        gate = high[:, width + c : width + c + 1]
+        mixed = mixed + gate * matmul((slot == target[:, c : c + 1]).astype(BF), returned[...])
+    mixed_ref[...] = mixed.astype(BF)
+    shuffle = shuffle_of(place_of)
+    gain = small_of(small_lanes(experts), near, far, shuffle)[experts : experts + 1].astype(F32)
+    grads = joint_grad[...]
+    normed_grad = jnp.concatenate(
+        [nt(grads, part[:, : 3 * width]) for part in (near, far)], axis=1
+    )
+    large = normed_grad.astype(BF)
+    rest = (normed_grad - large.astype(F32)).astype(BF)
+    scaled = (nt(large, shuffle) + nt(rest, shuffle)) * gain
+    inputs = tokens[...].astype(F32)
+    inverse = inverse_rms(inputs)
+    unit = inputs * inverse
+    input_grad = inverse * (scaled - unit * jnp.mean(unit * scaled, axis=-1, keepdims=True))
+    token_ref[...] = (first_grad[...] + input_grad).astype(BF)
+
+
+def finish_kernel(experts, project_in, gain, *refs):
+    parts, refs = refs[:-6], refs[-6:]
+    grad_in_ref, sum_out_ref, router_ref, first_gain_ref, second_gain_ref, table_ref = refs
     sums = sum(part[...].astype(F32) for part in parts)
-    width = sum_out_ref.shape[1]
+    share, width = sum_out_ref.shape
     grad_in = sums[:, : 3 * width]
     grad_in_ref[...] = grad_in
     sum_out_ref[...] = sums[:, 3 * width : 4 * width]
-    small_ref[...] = sums[:, 4 * width :]
-    grads = grad_in * project_in[...].astype(F32)
-    gain_ref[...] = jnp.sum(grads, axis=-1, keepdims=True) / gain[...].astype(F32)
+    small = sums[:, 4 * width :]
+    router_ref[...] = small[:, :experts]
+    row = lax.broadcasted_iota(jnp.int32, (share, share), 0)
+    same = row == lax.broadcasted_iota(jnp.int32, (share, share), 1)
+
+    def lined(column):
+        return jnp.sum(jnp.where(same, column, 0.0), axis=0, keepdims=True)
+
+    second_gain_ref[...] = lined(small[:, experts : experts + 1])
+    grads = jnp.sum(grad_in * project_in[...].astype(F32), axis=-1, keepdims=True)
+    first_gain_ref[...] = lined(grads) / gain[...].astype(F32)
+    lanes = table_lanes(share)
+    table = small[:, experts + 1 : experts + 1 + lanes]
+    value_row = lax.broadcasted_iota(jnp.int32, (share, HEADS), 0) * lanes
+    value_head = lax.broadcasted_iota(jnp.int32, (share, HEADS), 1)
+    step = min(lanes, BUCKETS)
+    total = jnp.zeros((BUCKETS, HEADS), F32)
+    for start in range(0, max(lanes, BUCKETS), step):
+        if lanes <= BUCKETS:
+            picked, part = value_row == value_head * BUCKETS + start, table
+        else:
+            picked = value_row + start == value_head * BUCKETS
+            part = table[:, start : start + step]
+        put = lax.dot_general(
+            part,
+            picked.astype(F32),
+            (((0,), (0,)), ((), ())),
+            precision=lax.Precision.HIGHEST,
+            preferred_element_type=F32,
+        )
+        if lanes <= BUCKETS:
+            table_ref[start : start + step] = put
+        else:
+            total = total + put
+            table_ref[...] = total
 
 
 def on_device(
@@ -533,42 +650,38 @@
     share = project_in.shape[0]
     column = lax.axis_index("fsdp")
     mine = column * experts + lax.axis_index("expert")
-    small_lanes = -(-(experts + 2) // LANES) * LANES
-    (packed,) = kernel_call(
+    target = routes * capacity + slots
+    slot_index = jnp.arange(rows_here, dtype=jnp.int32)
+    hot = (slot_index[None, None, :] == jnp.transpose(target)[:, :, None]).astype(BF)
+    place_hot = hot[0] + hot[1]
+    grad_rows = contract_rows(place_hot, cotangent).astype(BF)
+    grad_own = exchange(grad_rows)
+
+    lanes = small_lanes(experts)
+    hidden = expert_down.shape[1]
+    late = hidden - hidden // 3
+    packed, down_own = kernel_call(
         pack_kernel,
-        [((share, small_lanes + 4 * width), BF)],
+        [((share, lanes + 4 * width), BF), ((hidden - late, width), BF)],
         0,
         router.T,
         first_gain[None],
         second_gain[None],
         project_in,
         project_out,
-        fetch=range(5),
+        expert_down,
+        fetch=(*range(5), (5, (0, slice(late, hidden)), (hidden - late, width))),
         scratch=56,
     )
-    weights = stack([expert_up[0].T, expert_down[0]])
-    halves = gather_blocks(packed, weights)
+    weights = stack([expert_up[0].T, expert_down[0, :late]])
+    downs = fan(down_own, chip_masks())
+    halves = gather_blocks(packed, (weights, *downs[1:]), (grad_own,))
+    grad_parts = (grad_own, swap(grad_own, core_mask()))
     weights = fan(after(weights, halves[0]), chip_masks())
-    in_halves = [half[:, small_lanes : small_lanes + 3 * width] for half in halves]
-
-    def times_back(value, parts):
-        return jnp.concatenate([contract_cols(value, part) for part in parts], axis=1)
-
     feature = jnp.arange(width, dtype=jnp.int32)
     masks = jnp.asarray(np.repeat(np.array(block_masks(), np.int32), share))
     place_of = (masks ^ mine) * share + feature % share
-    shuffle = (feature[:, None] == place_of[None, :]).astype(BF)
-
-    inputs = tokens.astype(F32)
-    inputs_rel = matmul(tokens, shuffle)
-
-    target = routes * capacity + slots
-    slot_index = jnp.arange(rows_here, dtype=jnp.int32)
-    hot = (slot_index[None, None, :] == jnp.transpose(target)[:, :, None]).astype(BF)
-    place_hot = hot[0] + hot[1]
-    grad_rows = contract_rows(place_hot, cotangent).astype(BF)
-    grad_own = exchange(grad_rows)
-    grad_parts = (grad_own, swap(grad_own, core_mask()))
+
 
     places = jnp.arange(count, dtype=jnp.int32)
     bucket_hot = (buckets[:, None] == jnp.arange(BUCKETS, dtype=jnp.int32)).astype(F32)
@@ -592,16 +705,24 @@
         positions[:, None],
         routes,
         jnp.transpose(target),
-    )
-    row_own = exchange(after(outgoing, grad_own))
+        fetch=(0, 2, 3, 1, 4, 5, 6, 7),
+        push=(0, 1, 2),
+        scratch=56,
+    )
+    row_own = exchange(outgoing)
     row_parts = (row_own, swap(row_own, core_mask()))
 
     chips = len(chip_masks())
     piece = expert_up.shape[2]
-    wide = (rows_here, width + LANES)
-    row_far, row_near, result, kept = kernel_call(
+    wide = (rows_here, 2 * width + LANES)
+    row_far, row_near, kept, shown = kernel_call(
         functools.partial(expert_kernel, chips),
-        [(wide, BF), (wide, BF), ((2 * rows_here, width), BF), ((2 * rows_here, 2 * piece + width), BF)],
+        [
+            (wide, BF),
+            (wide, BF),
+            ((2 * rows_here, 2 * piece + width), BF),
+            ((2 * rows_here, width), BF),
+        ],
         16 * rows_here * width * chips * piece,
         column.astype(jnp.int32).reshape(1, 1),
         row_parts[1],
@@ -609,17 +730,14 @@
         grad_parts[1],
         grad_parts[0],
         *weights,
-        fetch=range(5, 5 + len(weights)),
+        *downs,
+        fetch=range(5, 5 + 2 * chips),
         scratch=56,
     )
-    home = exchange(add_low(row_near, swap(row_far, core_mask())))
-    result_own = add_low(result[rows_here:], swap(result[:rows_here], core_mask()))
-
-    far = []
-    for own in (row_own, grad_own):
-        parts = [swap(after(own, *weights[1:]), mask) for mask in chip_masks()[1:]]
-        far += [both for part in parts for both in (part, swap(part, core_mask()))]
-    home = after(home, result_own, *far)
+    others = [swap(shown, mask) for mask in chip_masks()[1:]]
+    others = [both for part in others for both in (part, swap(part, core_mask()))]
+    (row_sum,) = sum_apart([row_near, swap(row_far, core_mask())], 1)
+    home = after(exchange(row_sum), *others)
 
     half = width // 2
     table_at = experts + 1
@@ -643,59 +761,79 @@
         high,
         *halves,
         flip_hot,
-        fetch=(7, 8, 6, 3, 5),
+        fetch=(
+            6,
+            (7, (slice(None), slice(3 * width, None)), (half, lanes + width)),
+            (8, (slice(None), slice(3 * width, None)), (half, lanes + width)),
+            3,
+            5,
+        ),
         scratch=56,
     )
-    dense_half = add_low(keep, swap(send, core_mask()))
-    blocks, phase = scatter_blocks(dense_half)
-    grad_up, grad_down = kernel_call(
-        functools.partial(weight_grad_kernel, len(far) // 2),
-        [((width, piece), F32), ((piece, width), F32)],
-        16 * rows_here * width * chips * piece,
-        weights[0],
-        after(kept, dense_half),
-        row_parts[1],
-        row_parts[0],
-        *far,
-        fetch=range(4 + len(far)),
-        scratch=56,
-    )
-    normed_grad = times_back(after(joint_grad, phase), in_halves)
-    gain_rel = stack([part[:, experts] for part in halves]).astype(F32)
-    input_grad_rel = jax.vjp(lambda v: rms_scale(v, gain_rel), inputs_rel)[1](normed_grad)[0]
-    large = input_grad_rel.astype(BF)
-    rest = (input_grad_rel - large.astype(F32)).astype(BF)
-    input_grad = contract_cols(large, shuffle) + contract_cols(rest, shuffle)
-    token_grad = (first_grad + input_grad).astype(BF)
-
-    returned = exchange(after(result_own, token_grad))
-    routed = [matmul(hot[c], returned) for c in range(2)]
-    first, gates = high[:, :width], high[:, width : width + 2]
-    mixed = (first + gates[:, 0:1] * routed[0] + gates[:, 1:2] * routed[1]).astype(BF)
-    grad_in, sum_out, sum_small, grad_first_gain = kernel_call(
-        finish_kernel,
+    def meanwhile(begun):
+        grad_up, grad_down = kernel_call(
+            weight_grad_kernel,
+            [((width, piece), F32), ((piece, width), F32)],
+            16 * rows_here * width * chips * piece,
+            weights[0],
+            down_own,
+            after(kept, begun),
+            row_parts[1],
+            row_parts[0],
+            *others,
+            fetch=range(5 + len(others)),
+            scratch=56,
+        )
+        token_grad, mixed = kernel_call(
+            functools.partial(token_kernel, experts),
+            [((count, width), BF), ((count, width), BF)],
+            2 * count * width * 6 * width,
+            tokens,
+            first_grad,
+            after(joint_grad, begun),
+            *halves,
+            place_of[None],
+            home,
+            target,
+            high,
+            fetch=(
+                (6, (slice(None), slice(width + LANES, None)), (rows_here, width)),
+                (8, (slice(None), slice(0, width + LANES)), (count, width + LANES)),
+                3,
+                4,
+                0,
+                1,
+                2,
+            ),
+            scratch=56,
+        )
+        return grad_up, grad_down, token_grad, mixed
+
+    blocks, done = scatter_blocks(keep, send, meanwhile)
+    grad_up, grad_down, token_grad, mixed = done
+    grad_in, sum_out, grad_router, grad_first_gain, grad_second_gain, table_total = kernel_call(
+        functools.partial(finish_kernel, experts),
         [
             ((share, 3 * width), F32),
             ((share, width), F32),
-            ((share, spread_lanes), F32),
-            ((share, 1), F32),
+            ((share, experts), F32),
+            ((1, share), F32),
+            ((1, share), F32),
+            ((BUCKETS, HEADS), F32),
         ],
         share * width * 8,
         project_in,
-        first_gain[:, None],
-        after(blocks[0], mixed),
-        *blocks[1:],
-    )
-    table_total = sum_small[:, table_at : table_at + table_lanes(share)]
-    table_total = table_total.reshape(HEADS, BUCKETS).T
+        first_gain[None],
+        *blocks,
+    )
     return (
         mixed,
         token_grad,
         grad_in,
         sum_out,
-        sum_small[:, :experts],
-        grad_first_gain[:, 0],
-        sum_small[:, experts],
+        grad_router,
+        grad_first_gain[0],
+        grad_second_gain[0],
         table_total,
         grad_up[None],
         grad_down[None],

time: 254 us -> 239 us (0.941)
  Pallas kernels: 52.3 us -> 66.7 us
  other arithmetic: 13.1 us -> 5.09 us
  local copies, waits for them, and re-layouts: 24.2 us -> 16.2 us
  starting transfers between devices: 39.7 us -> 31.8 us
  matrix products: 9.92 us -> 2.16 us
    pallas_call x6 -> x10, Pallas kernels: 52.3 us -> 66.6 us  [kernel_call(): pl.pallas_call(kernel, out_shape=[jax.ShapeDtypeStruct(shape, kind) for s...]
    ppermute x23 -> x21, waiting for transfers between devices: 71.8 us -> 82.9 us  [swap(): lax.ppermute(value, AXES, [(i, i ^ mask) for i in range(columns * experts)])]
    all_to_all x3 -> x2, starting transfers between devices: 18.7 us -> 9.23 us  [exchange(): lax.all_to_all(blocks, 'expert', split_axis=0, concat_axis=0, tiled=True)]
    all_to_all x3 -> x2, waiting for transfers between devices: 18.6 us -> 9.76 us  [exchange(): lax.all_to_all(blocks, 'expert', split_axis=0, concat_axis=0, tiled=True)]
    convert_element_type x6 -> x1, other arithmetic: 8.58 us -> 0.1 us  [on_device(): (slot_index[None, None, :] == jnp.transpose(target)[:, :, None]).astype(BF)]
    dot_general x7 -> x0, matrix products: 8.19 us -> none  [the longest x4 5.33 us: contract_cols(): lax.dot_general(left, right, (((1,), (1,)), ((), ())), preferred_element_...]
    slice x8 -> x0, local copies, waits for them, and re-layouts: 5.97 us -> none  [the longest x2 1.28 us: on_device(): gain_rel = stack([part[:, experts] for part in halves]).astype(F32)]
    unnamed x76 -> x59, local copies, waits for them, and re-layouts: 15.1 us -> 12.6 us
  transfers between devices with their start and end apart: 26 -> 23, of which waited for: 14 -> 14; matrix products, arithmetic and copies ran while one was open for 11% -> 5% of each run, Pallas kernels for 8% -> 14%
where the time goes in v2:
time: 239 us
  waiting for transfers between devices  92.6 us (39%)
  Pallas kernels  66.7 us (28%)
  starting transfers between devices  31.8 us (13%)
  blocking collectives  23.1 us (10%)
  local copies, waits for them, and re-layouts  16.2 us (7%)
  other arithmetic  5.09 us (2%)
    ppermute x21, waiting for transfers between devices, swap(): lax.ppermute(value, AXES, [(i, i ^ mask) for i in range(columns * experts)])  82.9 us
    pallas_call x10, Pallas kernels, kernel_call(): pl.pallas_call(kernel, out_shape=[jax.ShapeDtypeStruct(shape, kind) for s...  66.6 us
    all_to_all x1, blocking collectives, exchange(): lax.all_to_all(blocks, 'expert', split_axis=0, concat_axis=0, tiled=True)  23.1 us
    ppermute x21, starting transfers between devices, swap(): lax.ppermute(value, AXES, [(i, i ^ mask) for i in range(columns * experts)])  22.6 us
    unnamed x59, local copies, waits for them, and re-layouts  12.6 us
    all_to_all x2, waiting for transfers between devices, exchange(): lax.all_to_all(blocks, 'expert', split_axis=0, concat_axis=0, tiled=True)  9.76 us
    all_to_all x2, starting transfers between devices, exchange(): lax.all_to_all(blocks, 'expert', split_axis=0, concat_axis=0, tiled=True)  9.23 us
    concatenate x3, other arithmetic, stack(): return jnp.concatenate(parts, axis=0)  4.97 us
  transfers between devices with their start and end apart: 23, of which 14 were waited for; matrix products, arithmetic and copies ran while one was open for 5% of the time, Pallas kernels for 14%

profile of v2, /device:TPU:0, one launch (start us, length us, event | category | flops | bytes accessed | tf_op | source)
XLA Modules:
  0.0 238.5 jit_solution(8681090889560806142)
XLA Ops:
  0.7 2.1 shard_map.222
  2.8 5.1 %collective-permute-start.2 = (bf16[24,3200]{1,0:T(8,128)(2,1)}, bf16[24,3200]{1,0:T(8,128)(2,1)S(1)}, u32[]{:S(2)}, u32[]{:S(2)}) collective-permute-start(bf16[24,3200]{1,0:T(8,128)(2,1)} %get-tuple-element.41), channel_id=1, source_target_pairs={{0,6},{1,7},{2,4},{3,5},{4,2},{5,3},{6,0},{7,1},{8,14},{9,15},{10,... | collective-permute-start | bytes 460808 | tf_op jit(solution)/shard_map/ppermute | solution.py:67
  8.5 1.6 collective-permute-start.3
  13.9 7.3 %collective-permute-done.1 = bf16[24,3200]{1,0:T(8,128)(2,1)} collective-permute-done((bf16[24,3200]{1,0:T(8,128)(2,1)}, bf16[24,3200]{1,0:T(8,128)(2,1)}, u32[]{:S(2)}, u32[]{:S(2)}) %collective-permute-start.1) | collective-permute-done | bytes 153632 | tf_op jit(solution)/shard_map/ppermute | solution.py:67
  21.2 1.9 pad_maximum_fusion.2.refs_0_
  23.1 2.5 %collective-permute-start.6 = (bf16[96,3200]{1,0:T(8,128)(2,1)}, bf16[96,3200]{1,0:T(8,128)(2,1)S(1)}, u32[]{:S(2)}, u32[]{:S(2)}) collective-permute-start(bf16[96,3200]{1,0:T(8,128)(2,1)} %shard_map.223), channel_id=1, source_target_pairs={{0,17},{1,16},{2,19},{3,18},{4,21},{5,20},{6,23},{7,22},{8,25},{9,... | collective-permute-start | bytes 1843208 | tf_op jit(solution)/shard_map/ppermute | solution.py:67
  27.8 4.7 %all-to-all-start = ((bf16[8,48,768]{2,1,0:T(8,128)(2,1)}), bf16[8,48,768]{2,1,0:T(8,128)(2,1)S(1)}, u32[]{:S(2)}, u32[]{:S(2)}) async-start(bf16[8,48,768]{2,1,0:T(8,128)(2,1)} %bitcast.9), calls=%async_computation | async-start | bytes 1179648 | tf_op jit(solution)/shard_map/all_to_all | solution.py:131
  32.5 10.6 %collective-permute-done.6 = bf16[96,3200]{1,0:T(8,128)(2,1)S(1)} collective-permute-done((bf16[96,3200]{1,0:T(8,128)(2,1)}, bf16[96,3200]{1,0:T(8,128)(2,1)S(1)}, u32[]{:S(2)}, u32[]{:S(2)}) %collective-permute-start.6) | collective-permute-done | bytes 614432 | tf_op jit(solution)/shard_map/ppermute | solution.py:67
  43.2 14.0 %collective-permute-done.5 = bf16[96,3200]{1,0:T(8,128)(2,1)S(1)} collective-permute-done((bf16[96,3200]{1,0:T(8,128)(2,1)}, bf16[96,3200]{1,0:T(8,128)(2,1)S(1)}, u32[]{:S(2)}, u32[]{:S(2)}) %collective-permute-start.5) | collective-permute-done | bytes 614432 | tf_op jit(solution)/shard_map/ppermute | solution.py:67
  57.2 1.7 pad_maximum_fusion.refs_0_
  62.8 1.5 collective-permute-start.10
  66.1 10.7 %shard_map.225 = (bf16[128,4608]{1,0:T(8,128)(2,1)}, f32[128,2432]{1,0:T(8,128)}, bf16[384,896]{1,0:T(8,128)(2,1)}) custom-call(bf16[128,768]{1,0:T(8,128)(2,1)} %refs_0_.4, s32[1,768]{1,0:T(1,128)} %broadcast_in_dim.12.refs_1_.refs_4_.refs_5_, bf16[384,3200]{1,0:T(8,128)(2,1)} %shard_map.224.refs_2_.refs_1_.refs_7_.refs_3_, bf16[384,3200]{1,0:T(8,128)(2,1)} %copy-done.7, ...), custom_call_target="tpu_custom_call" | custom-call | flops 905969664 | bytes 8236544 | tf_op jit(solution)/shard_map/pallas_call | solution.py:209
  76.8 23.1 %all_to_all.15 = bf16[8,48,896]{2,1,0:T(8,128)(2,1)S(1)} all-to-all(bf16[8,48,896]{2,1,0:T(8,128)(2,1)} %bitcast.42), channel_id=1, replica_groups=mesh['fsdp'=4,'expert'=8] {'expert'}, dimensions={0} | all-to-all | bytes 1376256 | tf_op jit(solution)/shard_map/all_to_all | solution.py:131
  100.4 2.5 %collective-permute-done.9.refs_3_ = bf16[384,768]{1,0:T(8,128)(2,1)S(1)} collective-permute-done((bf16[384,768]{1,0:T(8,128)(2,1)S(1)}, bf16[384,768]{1,0:T(8,128)(2,1)S(1)}, u32[]{:S(2)}, u32[]{:S(2)}) %collective-permute-start.9) | collective-permute-done | bytes 589856 | tf_op jit(solution)/shard_map/ppermute | solution.py:67
  102.9 5.4 %collective-permute-done.10.refs_6_ = bf16[1280,768]{1,0:T(8,128)(2,1)S(1)} collective-permute-done((bf16[1280,768]{1,0:T(8,128)(2,1)}, bf16[1280,768]{1,0:T(8,128)(2,1)S(1)}, u32[]{:S(2)}, u32[]{:S(2)}) %collective-permute-start.10) | collective-permute-done | bytes 1966112 | tf_op jit(solution)/shard_map/ppermute | solution.py:67
  109.7 15.3 %shard_map.227 = (bf16[384,1664]{1,0:T(8,128)(2,1)}, bf16[384,1664]{1,0:T(8,128)(2,1)}, bf16[768,2304]{1,0:T(8,128)(2,1)}, bf16[768,768]{1,0:T(8,128)(2,1)}) custom-call(s32[1,1]{1,0:T(1,128)} %bitcast.refs_0_, bf16[384,896]{1,0:T(8,128)(2,1)} %copy-done.24, bf16[384,896]{1,0:T(8,128)(2,1)} %bitcast.40, bf16[384,768]{1,0:T(8,128)(2,1)} %copy-done.25, ...), custom_call_target="tpu_custom_call" | custom-call | flops 7247757312 | bytes 14548996 | tf_op jit(solution)/shard_map/pallas_call | solution.py:209
  125.2 1.6 collective-permute-start.12
  126.7 1.6 collective-permute-done.11.refs_1_
  131.0 4.5 %all-to-all-start.2 = ((bf16[8,48,1664]{2,1,0:T(8,128)(2,1)}), bf16[8,48,1664]{2,1,0:T(8,128)(2,1)S(1)}, u32[]{:S(2)}, u32[]{:S(2)}) async-start(bf16[8,48,1664]{2,1,0:T(8,128)(2,1)} %bitcast.15), calls=%async_computation.2 | async-start | bytes 2555904 | tf_op jit(solution)/shard_map/all_to_all | solution.py:131
  135.5 18.2 %collective-permute-done.12.refs_1_.refs_5_ = bf16[768,768]{1,0:T(8,128)(2,1)S(1)} collective-permute-done((bf16[768,768]{1,0:T(8,128)(2,1)}, bf16[768,768]{1,0:T(8,128)(2,1)S(1)}, u32[]{:S(2)}, u32[]{:S(2)}) %collective-permute-start.12) | collective-permute-done | bytes 1179680 | tf_op jit(solution)/shard_map/ppermute | solution.py:67
  154.6 2.1 collective-permute-done.13.refs_2_.refs_6_
  156.7 9.8 %all-to-all-done.2 = bf16[8,48,1664]{2,1,0:T(8,128)(2,1)S(1)} async-done(((bf16[8,48,1664]{2,1,0:T(8,128)(2,1)}), bf16[8,48,1664]{2,1,0:T(8,128)(2,1)S(1)}, u32[]{:S(2)}, u32[]{:S(2)}) %all-to-all-start.2) | async-done | bytes 1277984 | tf_op jit(solution)/shard_map/all_to_all | solution.py:131
  167.6 14.0 %shard_map.230 = (bf16[384,3200]{1,0:T(8,128)(2,1)}, bf16[384,3200]{1,0:T(8,128)(2,1)}, f32[128,768]{1,0:T(8,128)}, bf16[128,2304]{1,0:T(8,128)(2,1)}, f32[12,128]{1,0:T(8,128)}) custom-call(bf16[384,1664]{1,0:T(8,128)(2,1)} %shard_map.229.refs_0_.refs_6_, s32[128,2]{1,0:T(8,128)} %copy.49.refs_6_.refs_1_, s32[128,2]{1,0:T(8,128)} %copy-done.14, ...), custom_call_target="tpu_custom_call" | custom-call | flops 1509949440 | bytes 14740480 | tf_op jit(solution)/shard_map/pallas_call | solution.py:209
  181.7 4.9 %collective-permute-done.14.refs_1_ = bf16[384,3200]{1,0:T(8,128)(2,1)S(1)} collective-permute-done((bf16[384,3200]{1,0:T(8,128)(2,1)}, bf16[384,3200]{1,0:T(8,128)(2,1)S(1)}, u32[]{:S(2)}, u32[]{:S(2)}) %collective-permute-start.14) | collective-permute-done | bytes 2457632 | tf_op jit(solution)/shard_map/ppermute | solution.py:67
  186.6 1.7 copy-done.3
  193.9 7.5 %shard_map.233 = (bf16[128,768]{1,0:T(8,128)(2,1)}, bf16[128,768]{1,0:T(8,128)(2,1)}) custom-call(bf16[128,768]{1,0:T(8,128)(2,1)} %refs_0_.4, f32[128,768]{1,0:T(8,128)} %get-tuple-element.49.refs_1_, bf16[128,2304]{1,0:T(8,128)(2,1)} %shard_map.232.refs_2_, bf16[384,3200]{1,0:T(8,128)(2,1)} %shard_map.224.refs_2_.refs_1_.refs_7_.refs_3_, ...), custom_call_target="tpu_custom_call" | custom-call | flops 905969664 | bytes 9015296 | tf_op jit(solution)/shard_map/pallas_call | solution.py:209
  201.4 13.1 %shard_map.235 = (f32[768,768]{1,0:T(8,128)}, f32[768,768]{1,0:T(8,128)}) custom-call(bf16[1280,768]{1,0:T(8,128)(2,1)} %shard_map.226.refs_5_.refs_0_, bf16[256,768]{1,0:T(8,128)(2,1)} %get-tuple-element.42.refs_7_.refs_1_, bf16[768,2304]{1,0:T(8,128)(2,1)} %shard_map.234.refs_2_, bf16[384,896]{1,0:T(8,128)(2,1)} %copy-done.24, bf16[384,896]{1,0:T(8,128)(2,1)} %bitcast.41, ...), custom_call_target="tpu_custom_call" | custom-call | flops 7247757312 | bytes 14352384 | tf_op jit(solution)/shard_map/pallas_call | solution.py:209
  214.5 6.1 %collective-permute-done.16.refs_2_ = bf16[96,3200]{1,0:T(8,128)(2,1)S(1)} collective-permute-done((bf16[96,3200]{1,0:T(8,128)(2,1)S(1)}, bf16[96,3200]{1,0:T(8,128)(2,1)S(1)}, u32[]{:S(2)}, u32[]{:S(2)}) %collective-permute-start.16) | collective-permute-done | bytes 614432 | tf_op jit(solution)/shard_map/ppermute | solution.py:67
  222.1 2.6 %collective-permute-start.19 = (bf16[24,3200]{1,0:T(8,128)(2,1)S(1)}, bf16[24,3200]{1,0:T(8,128)(2,1)S(1)}, u32[]{:S(2)}, u32[]{:S(2)}) collective-permute-start(bf16[24,3200]{1,0:T(8,128)(2,1)S(1)} %get-tuple-element.64), channel_id=1, source_target_pairs={{0,4},{1,5},{2,6},{3,7},{4,0},{5,1},{6,2},{7,3},{8,12},{9,13},{10,... | collective-permute-start | bytes 460808 | tf_op jit(solution)/shard_map/ppermute | solution.py:67
  224.7 1.8 collective-permute-start.20
  226.5 2.9 %collective-permute-done.18.refs_3_ = bf16[24,3200]{1,0:T(8,128)(2,1)S(1)} collective-permute-done((bf16[24,3200]{1,0:T(8,128)(2,1)S(1)}, bf16[24,3200]{1,0:T(8,128)(2,1)S(1)}, u32[]{:S(2)}, u32[]{:S(2)}) %collective-permute-start.18) | collective-permute-done | bytes 153632 | tf_op jit(solution)/shard_map/ppermute | solution.py:67
  229.4 6.9 %collective-permute-done.19.refs_4_ = bf16[24,3200]{1,0:T(8,128)(2,1)S(1)} collective-permute-done((bf16[24,3200]{1,0:T(8,128)(2,1)S(1)}, bf16[24,3200]{1,0:T(8,128)(2,1)S(1)}, u32[]{:S(2)}, u32[]{:S(2)}) %collective-permute-start.19) | collective-permute-done | bytes 153632 | tf_op jit(solution)/shard_map/ppermute | solution.py:67
  (107 shorter events, 28.2 us)
Async XLA Ops:
  0.6 61.4 %copy-start = (f32[32,12]{0,1:T(8,128)S(1)}, f32[32,12]{0,1:T(8,128)}, u32[]{:S(2)}) copy-start(f32[32,12]{0,1:T(8,128)} %param.22) | copy-start | bytes 4612
  0.7 10.7 %copy-start.19 = (s32[128,2]{0,1:T(2,128)S(1)}, s32[128,2]{0,1:T(2,128)}, u32[]{:S(2)}) copy-start(s32[128,2]{0,1:T(2,128)} %param.27) | copy-start | bytes 3076
  0.7 10.8 %copy-start.21 = (s32[128,2]{0,1:T(2,128)S(1)}, s32[128,2]{0,1:T(2,128)}, u32[]{:S(2)}) copy-start(s32[128,2]{0,1:T(2,128)} %param.28) | copy-start | bytes 3076
  0.7 11.0 %copy-start.12 = (bf16[1,768,768]{2,1,0:T(8,128)(2,1)S(1)}, bf16[1,768,768]{2,1,0:T(8,128)(2,1)}, u32[]{:S(2)}) copy-start(bf16[1,768,768]{2,1,0:T(8,128)(2,1)} %param.23) | copy-start | bytes 3538948
  2.8 11.1 %collective-permute-start.2 = (bf16[24,3200]{1,0:T(8,128)(2,1)}, bf16[24,3200]{1,0:T(8,128)(2,1)S(1)}, u32[]{:S(2)}, u32[]{:S(2)}) collective-permute-start(bf16[24,3200]{1,0:T(8,128)(2,1)} %get-tuple-element.41), channel_id=1, source_target_pairs={{0,6},{1,7},{2,4},{3,5},{4,2},{5,3},{6,0},{7,1},{8,14},{9,15},{10,... | collective-permute-start | bytes 460808 | tf_op jit(solution)/shard_map/ppermute | solution.py:67
  7.9 13.3 %collective-permute-start.1 = (bf16[24,3200]{1,0:T(8,128)(2,1)}, bf16[24,3200]{1,0:T(8,128)(2,1)}, u32[]{:S(2)}, u32[]{:S(2)}) collective-permute-start(bf16[24,3200]{1,0:T(8,128)(2,1)} %get-tuple-element.41), channel_id=1, source_target_pairs={{0,4},{1,5},{2,6},{3,7},{4,0},{5,1},{6,2},{7,3},{8,12},{9,13},{10,... | collective-permute-start | bytes 460808 | tf_op jit(solution)/shard_map/ppermute | solution.py:67
  7.9 13.3 %collective-permute-start = (bf16[24,3200]{1,0:T(8,128)(2,1)}, bf16[24,3200]{1,0:T(8,128)(2,1)}, u32[]{:S(2)}, u32[]{:S(2)}) collective-permute-start(bf16[24,3200]{1,0:T(8,128)(2,1)} %get-tuple-element.41), channel_id=1, source_target_pairs={{0,2},{1,3},{2,0},{3,1},{4,6},{5,7},{6,4},{7,5},{8,10},{9,11},{10,... | collective-permute-start | bytes 460808 | tf_op jit(solution)/shard_map/ppermute | solution.py:67
  8.5 14.5 %collective-permute-start.3 = (bf16[256,768]{1,0:T(8,128)(2,1)}, bf16[256,768]{1,0:T(8,128)(2,1)}, u32[]{:S(2)}, u32[]{:S(2)}) collective-permute-start(bf16[256,768]{1,0:T(8,128)(2,1)} %get-tuple-element.42.refs_7_.refs_1_), channel_id=1, source_target_pairs={{0,16},{1,17},{2,18},{3,19},{4,20},{5,21},{6,22},{7,23},{8,24},{9,... | collective-permute-start | bytes 1179656 | tf_op jit(solution)/shard_map/ppermute | solution.py:67
  23.1 34.1 %copy-start.9 = (bf16[96,3200]{1,0:T(8,128)(2,1)S(1)}, bf16[96,3200]{1,0:T(8,128)(2,1)}, u32[]{:S(2)}) copy-start(bf16[96,3200]{1,0:T(8,128)(2,1)} %shard_map.223) | copy-start | bytes 1843204
  23.1 20.1 %collective-permute-start.6 = (bf16[96,3200]{1,0:T(8,128)(2,1)}, bf16[96,3200]{1,0:T(8,128)(2,1)S(1)}, u32[]{:S(2)}, u32[]{:S(2)}) collective-permute-start(bf16[96,3200]{1,0:T(8,128)(2,1)} %shard_map.223), channel_id=1, source_target_pairs={{0,17},{1,16},{2,19},{3,18},{4,21},{5,20},{6,23},{7,22},{8,25},{9,... | collective-permute-start | bytes 1843208 | tf_op jit(solution)/shard_map/ppermute | solution.py:67
  25.6 31.6 %collective-permute-start.5 = (bf16[96,3200]{1,0:T(8,128)(2,1)}, bf16[96,3200]{1,0:T(8,128)(2,1)S(1)}, u32[]{:S(2)}, u32[]{:S(2)}) collective-permute-start(bf16[96,3200]{1,0:T(8,128)(2,1)} %shard_map.223), channel_id=1, source_target_pairs={{0,1},{1,0},{2,3},{3,2},{4,5},{5,4},{6,7},{7,6},{8,9},{9,8},{10,11... | collective-permute-start | bytes 1843208 | tf_op jit(solution)/shard_map/ppermute | solution.py:67
  26.1 31.1 %collective-permute-start.4 = (bf16[96,3200]{1,0:T(8,128)(2,1)}, bf16[96,3200]{1,0:T(8,128)(2,1)S(1)}, u32[]{:S(2)}, u32[]{:S(2)}) collective-permute-start(bf16[96,3200]{1,0:T(8,128)(2,1)} %shard_map.223), channel_id=1, source_target_pairs={{0,16},{1,17},{2,18},{3,19},{4,20},{5,21},{6,22},{7,23},{8,24},{9,... | collective-permute-start | bytes 1843208 | tf_op jit(solution)/shard_map/ppermute | solution.py:67
  27.8 31.1 %all-to-all-start = ((bf16[8,48,768]{2,1,0:T(8,128)(2,1)}), bf16[8,48,768]{2,1,0:T(8,128)(2,1)S(1)}, u32[]{:S(2)}, u32[]{:S(2)}) async-start(bf16[8,48,768]{2,1,0:T(8,128)(2,1)} %bitcast.9), calls=%async_computation | async-start | bytes 1179648 | tf_op jit(solution)/shard_map/all_to_all | solution.py:131
  59.7 4.9 %collective-permute-start.7 = (bf16[384,3200]{1,0:T(8,128)(2,1)}, bf16[384,3200]{1,0:T(8,128)(2,1)S(1)}, u32[]{:S(2)}, u32[]{:S(2)}) collective-permute-start(bf16[384,3200]{1,0:T(8,128)(2,1)} %shard_map.224.refs_2_.refs_1_.refs_7_.refs_3_), channel_id=1, source_target_pairs={{0,8},{1,9},{2,10},{3,11},{4,12},{5,13},{6,14},{7,15},{8,0},{9,1},... | collective-permute-start | bytes 7372808 | tf_op jit(solution)/shard_map/ppermute | solution.py:67
  62.8 37.1 %copy-start.11 = (bf16[8,48,768]{2,1,0:T(8,128)(2,1)S(1)}, bf16[8,48,768]{2,1,0:T(8,128)(2,1)}, u32[]{:S(2)}) copy-start(bf16[8,48,768]{2,1,0:T(8,128)(2,1)} %copy-done.10) | copy-start | bytes 1769476
  62.8 45.4 %collective-permute-start.10 = (bf16[1280,768]{1,0:T(8,128)(2,1)}, bf16[1280,768]{1,0:T(8,128)(2,1)S(1)}, u32[]{:S(2)}, u32[]{:S(2)}) collective-permute-start(bf16[1280,768]{1,0:T(8,128)(2,1)} %shard_map.226.refs_5_.refs_0_), channel_id=1, source_target_pairs={{0,16},{1,17},{2,18},{3,19},{4,20},{5,21},{6,22},{7,23},{8,24},{9,... | collective-permute-start | bytes 5898248 | tf_op jit(solution)/shard_map/ppermute | solution.py:67
  99.9 8.4 %collective-permute-start.8 = (bf16[384,896]{1,0:T(8,128)(2,1)S(1)}, bf16[384,896]{1,0:T(8,128)(2,1)S(1)}, u32[]{:S(2)}, u32[]{:S(2)}) collective-permute-start(bf16[384,896]{1,0:T(8,128)(2,1)S(1)} %bitcast.39), channel_id=1, source_target_pairs={{0,8},{1,9},{2,10},{3,11},{4,12},{5,13},{6,14},{7,15},{8,0},{9,1},... | collective-permute-start | bytes 2064392 | tf_op jit(solution)/shard_map/ppermute | solution.py:67
  99.9 3.0 %collective-permute-start.9 = (bf16[384,768]{1,0:T(8,128)(2,1)S(1)}, bf16[384,768]{1,0:T(8,128)(2,1)S(1)}, u32[]{:S(2)}, u32[]{:S(2)}) collective-permute-start(bf16[384,768]{1,0:T(8,128)(2,1)S(1)} %bitcast.37), channel_id=1, source_target_pairs={{0,8},{1,9},{2,10},{3,11},{4,12},{5,13},{6,14},{7,15},{8,0},{9,1},... | collective-permute-start | bytes 1769480 | tf_op jit(solution)/shard_map/ppermute | solution.py:67
  125.1 3.3 %collective-permute-start.11 = (bf16[384,1664]{1,0:T(8,128)(2,1)}, bf16[384,1664]{1,0:T(8,128)(2,1)S(1)}, u32[]{:S(2)}, u32[]{:S(2)}) collective-permute-start(bf16[384,1664]{1,0:T(8,128)(2,1)} %get-tuple-element.45), channel_id=1, source_target_pairs={{0,8},{1,9},{2,10},{3,11},{4,12},{5,13},{6,14},{7,15},{8,0},{9,1},... | collective-permute-start | bytes 3833864 | tf_op jit(solution)/shard_map/ppermute | solution.py:67
  125.2 28.6 %collective-permute-start.12 = (bf16[768,768]{1,0:T(8,128)(2,1)}, bf16[768,768]{1,0:T(8,128)(2,1)S(1)}, u32[]{:S(2)}, u32[]{:S(2)}) collective-permute-start(bf16[768,768]{1,0:T(8,128)(2,1)} %get-tuple-element.46), channel_id=1, source_target_pairs={{0,16},{1,17},{2,18},{3,19},{4,20},{5,21},{6,22},{7,23},{8,24},{9,... | collective-permute-start | bytes 3538952 | tf_op jit(solution)/shard_map/ppermute | solution.py:67
  131.0 35.5 %all-to-all-start.2 = ((bf16[8,48,1664]{2,1,0:T(8,128)(2,1)}), bf16[8,48,1664]{2,1,0:T(8,128)(2,1)S(1)}, u32[]{:S(2)}, u32[]{:S(2)}) async-start(bf16[8,48,1664]{2,1,0:T(8,128)(2,1)} %bitcast.15), calls=%async_computation.2 | async-start | bytes 2555904 | tf_op jit(solution)/shard_map/all_to_all | solution.py:131
  153.8 12.7 %copy-start.13 = (bf16[768,768]{1,0:T(8,128)(2,1)}, bf16[768,768]{1,0:T(8,128)(2,1)S(1)}, u32[]{:S(2)}) copy-start(bf16[768,768]{1,0:T(8,128)(2,1)S(1)} %collective-permute-done.12.refs_1_.refs_5_) | copy-start | bytes 3538948
  153.8 3.0 %collective-permute-start.13 = (bf16[768,768]{1,0:T(8,128)(2,1)S(1)}, bf16[768,768]{1,0:T(8,128)(2,1)}, u32[]{:S(2)}, u32[]{:S(2)}) collective-permute-start(bf16[768,768]{1,0:T(8,128)(2,1)S(1)} %collective-permute-done.12.refs_1_.refs_5_), channel_id=1, source_target_pairs={{0,8},{1,9},{2,10},{3,11},{4,12},{5,13},{6,14},{7,15},{8,0},{9,1},... | collective-permute-start | bytes 3538952 | tf_op jit(solution)/shard_map/ppermute | solution.py:67
  181.6 5.0 %collective-permute-start.14 = (bf16[384,3200]{1,0:T(8,128)(2,1)}, bf16[384,3200]{1,0:T(8,128)(2,1)S(1)}, u32[]{:S(2)}, u32[]{:S(2)}) collective-permute-start(bf16[384,3200]{1,0:T(8,128)(2,1)} %get-tuple-element.52), channel_id=1, source_target_pairs={{0,8},{1,9},{2,10},{3,11},{4,12},{5,13},{6,14},{7,15},{8,0},{9,1},... | collective-permute-start | bytes 7372808 | tf_op jit(solution)/shard_map/ppermute | solution.py:67
  190.4 24.1 %collective-permute-start.15 = (bf16[96,3200]{1,0:T(8,128)(2,1)}, bf16[96,3200]{1,0:T(8,128)(2,1)S(1)}, u32[]{:S(2)}, u32[]{:S(2)}) collective-permute-start(bf16[96,3200]{1,0:T(8,128)(2,1)} %get-tuple-element.59), channel_id=1, source_target_pairs={{0,16},{1,17},{2,18},{3,19},{4,20},{5,21},{6,22},{7,23},{8,24},{9,... | collective-permute-start | bytes 1843208 | tf_op jit(solution)/shard_map/ppermute | solution.py:67
  191.9 28.8 %collective-permute-start.16 = (bf16[96,3200]{1,0:T(8,128)(2,1)S(1)}, bf16[96,3200]{1,0:T(8,128)(2,1)S(1)}, u32[]{:S(2)}, u32[]{:S(2)}) collective-permute-start(bf16[96,3200]{1,0:T(8,128)(2,1)S(1)} %get-tuple-element.60), channel_id=1, source_target_pairs={{0,1},{1,0},{2,3},{3,2},{4,5},{5,4},{6,7},{7,6},{8,9},{9,8},{10,11... | collective-permute-start | bytes 1843208 | tf_op jit(solution)/shard_map/ppermute | solution.py:67
  193.3 27.4 %collective-permute-start.17 = (bf16[96,3200]{1,0:T(8,128)(2,1)S(1)}, bf16[96,3200]{1,0:T(8,128)(2,1)S(1)}, u32[]{:S(2)}, u32[]{:S(2)}) collective-permute-start(bf16[96,3200]{1,0:T(8,128)(2,1)S(1)} %get-tuple-element.61), channel_id=1, source_target_pairs={{0,17},{1,16},{2,19},{3,18},{4,21},{5,20},{6,23},{7,22},{8,25},{9,... | collective-permute-start | bytes 1843208 | tf_op jit(solution)/shard_map/ppermute | solution.py:67
  214.5 21.8 %copy-start.5 = (bf16[24,2304]{1,0:T(8,128)(2,1)S(1)}, bf16[24,2304]{1,0:T(8,128)(2,1)}, u32[]{:S(2)}) copy-start(bf16[24,2304]{1,0:T(8,128)(2,1)} %refs_0_.5) | copy-start | bytes 331780
  214.5 21.8 %copy-start.6 = (bf16[24]{0:T(256)(128)(2,1)S(1)}, bf16[24]{0:T(256)(128)(2,1)}, u32[]{:S(2)}) copy-start(bf16[24]{0:T(256)(128)(2,1)} %param.20) | copy-start | bytes 148
  222.0 7.3 %collective-permute-start.18 = (bf16[24,3200]{1,0:T(8,128)(2,1)S(1)}, bf16[24,3200]{1,0:T(8,128)(2,1)S(1)}, u32[]{:S(2)}, u32[]{:S(2)}) collective-permute-start(bf16[24,3200]{1,0:T(8,128)(2,1)S(1)} %get-tuple-element.63), channel_id=1, source_target_pairs={{0,2},{1,3},{2,0},{3,1},{4,6},{5,7},{6,4},{7,5},{8,10},{9,11},{10,... | collective-permute-start | bytes 460808 | tf_op jit(solution)/shard_map/ppermute | solution.py:67
  222.1 14.1 %collective-permute-start.19 = (bf16[24,3200]{1,0:T(8,128)(2,1)S(1)}, bf16[24,3200]{1,0:T(8,128)(2,1)S(1)}, u32[]{:S(2)}, u32[]{:S(2)}) collective-permute-start(bf16[24,3200]{1,0:T(8,128)(2,1)S(1)} %get-tuple-element.64), channel_id=1, source_target_pairs={{0,4},{1,5},{2,6},{3,7},{4,0},{5,1},{6,2},{7,3},{8,12},{9,13},{10,... | collective-permute-start | bytes 460808 | tf_op jit(solution)/shard_map/ppermute | solution.py:67
  224.7 11.6 %collective-permute-start.20 = (bf16[24,3200]{1,0:T(8,128)(2,1)S(1)}, bf16[24,3200]{1,0:T(8,128)(2,1)S(1)}, u32[]{:S(2)}, u32[]{:S(2)}) collective-permute-start(bf16[24,3200]{1,0:T(8,128)(2,1)S(1)} %get-tuple-element.65), channel_id=1, source_target_pairs={{0,6},{1,7},{2,4},{3,5},{4,2},{5,3},{6,0},{7,1},{8,14},{9,15},{10,... | collective-permute-start | bytes 460808 | tf_op jit(solution)/shard_map/ppermute | solution.py:67
  (18 other events, 45.7 us)

commit v3 on v2

--- a/solution.py
+++ b/solution.py
@@ -54,8 +54,21 @@
     return [2 * experts * x for x in range(columns // 2)]
 
 
+def z_bits():
+    experts = sizes()[1]
+    return [1 << bit for bit in range(1, experts.bit_length() - 1)]
+
+
+def chip_bits():
+    columns, experts = sizes()
+    return [experts << bit for bit in range(1, columns.bit_length() - 1)]
+
+
 def z_masks():
-    return [2 * z for z in range(sizes()[1] // 2)]
+    order = [0]
+    for mask in reversed(z_bits()):
+        order = order + [k + mask for k in order]
+    return order
 
 
 def block_masks():
@@ -99,8 +112,12 @@
     return (own.astype(F32) + arrived.astype(F32)).astype(BF)
 
 
+def sum_of(refs):
+    return sum((ref[...].astype(F32) for ref in refs[1:]), refs[0][...].astype(F32))
+
+
 def sum_kernel(inputs, *refs):
-    total = sum((ref[...].astype(F32) for ref in refs[1:inputs]), refs[0][...].astype(F32))
+    total = sum_of(refs[:inputs])
     rows = total.shape[0] // (len(refs) - inputs)
     for i, ref in enumerate(refs[inputs:]):
         ref[...] = total[i * rows : (i + 1) * rows].astype(BF)
@@ -112,13 +129,60 @@
     return kernel_call(functools.partial(sum_kernel, len(parts)), outs, rows * width, *parts)
 
 
-def scatter_blocks(value, other, meanwhile):
+def halves_of(total, rows):
+    runs = [total[at : at + rows].astype(BF) for at in range(0, total.shape[0], rows)]
+    return jnp.concatenate(runs[::2], axis=0), jnp.concatenate(runs[1::2], axis=0)
+
+
+def halve_kernel(rows, own, arrived, keep_ref, send_ref):
+    keep_ref[...], send_ref[...] = halves_of(sum_of((own, arrived)), rows)
+
+
+def halve(own, arrived, rows):
+    outs = [((own.shape[0] // 2, own.shape[1]), BF)] * 2
+    return kernel_call(functools.partial(halve_kernel, rows), outs, own.size, own, arrived)
+
+
+def begin_kernel(cut, rows, own, arrived, *refs):
+    total = sum_of((own, arrived))
+    *leads, keep_ref, send_ref = refs
+    count = total.shape[0] // len(leads)
+    for i, ref in enumerate(leads):
+        ref[...] = total[i * count : (i + 1) * count, :cut].astype(BF)
+    keep_ref[...], send_ref[...] = halves_of(total[:, cut:], rows)
+
+
+def scatter_blocks(value, other, first, second):
     xy, z = xy_masks(), z_masks()
-    parts = sum_apart([value, swap(other, core_mask())], len(xy))
-    arrived = fan_sends(parts, xy)
-    done = meanwhile(parts[0])
-    sums = sum_apart([after(parts[0], *done), *arrived], len(z))
-    return [sums[0], *fan_sends(sums, z)], done
+    count, width = value.shape
+    share = count // (len(xy) * len(z))
+    cut = 3 * (width // LANES) // 4 * LANES
+    bits = z_bits()
+    steps = [(mask, share << (len(bits) - 1 - i)) for i, mask in enumerate(bits)]
+    bits = [1, *reversed(chip_bits())]
+    steps += [(mask, share << (len(bits) - 1 - i)) for i, mask in enumerate(bits)]
+    *leads, keep, send = kernel_call(
+        functools.partial(begin_kernel, cut, steps[0][1]),
+        [((count // len(xy), cut), BF)] * len(xy) + [((count // 2, width - cut), BF)] * 2,
+        value.size,
+        value,
+        swap(other, core_mask()),
+    )
+    arrived = fan_sends(leads, xy)
+    done = first(leads[0])
+    for i, (mask, _) in enumerate(steps):
+        if i == len(z_bits()):
+            keep = after(keep, sums[0])
+        come = swap(send, mask)
+        if i == 1:
+            come = after(come, *done)
+        if i + 1 == len(steps):
+            break
+        keep, send = halve(keep, come, steps[i + 1][1])
+        if i == 0:
+            sums = sum_apart([leads[0], *arrived], len(z))
+    later = second(sums[0])
+    return [sums[0], *fan_sends(sums, z)], [after(keep, *later), come], done, later
 
 
 def fan_sends(parts, masks):
@@ -213,7 +277,7 @@
         out_specs=[left if i in push else whole for i in range(len(outs))],
         scratch_shapes=buffers,
         compiler_params=pltpu.CompilerParams(vmem_limit_bytes=scratch * 1024 * 1024),
-        cost_estimate=pl.CostEstimate(flops=flops, bytes_accessed=moved, transcendentals=0),
+        cost_estimate=pl.CostEstimate(flops=0, bytes_accessed=0, transcendentals=0),
     )(*operands)
 
 
@@ -360,7 +424,7 @@
     return packed[:, width : width + 1].astype(F32) + packed[:, width + 1 : width + 2].astype(F32)
 
 
-def expert_kernel(chips, column, *refs):
+def expert_kernel(chips, *refs):
     rows, grads, refs = refs[:2], refs[2:4], refs[4:]
     weights, downs, refs = refs[:chips], refs[chips : 2 * chips], refs[2 * chips :]
     row_refs, kept_ref, shown_ref = refs[:2], refs[2], refs[3]
@@ -384,10 +448,8 @@
         grad = grad.astype(F32)
         scaled = (grad * gate).astype(BF)
         kept_ref[block, 2 * hidden :] = scaled
-        dots = jnp.sum(result * grad, axis=-1, keepdims=True)
-        row_refs[core][...] = jnp.concatenate(
-            [row_grad.astype(BF), lanes_of(dots, 2 * column[0, 0]), result.astype(BF)], axis=1
-        )
+        row_refs[core][:, :width] = row_grad.astype(BF)
+        row_refs[core][:, width:] = result.astype(BF)
     shown_ref[:count] = packed[:, :width]
     shown_ref[count:] = scaled
 
@@ -397,24 +459,18 @@
     width, hidden = up_ref.shape
     count = near.shape[0]
     up, down = weights[:hidden], (weights[hidden:], down_late[...])
-    for i, rows in enumerate((far, near)):
-        block = slice(i * count, (i + 1) * count)
-        scaled = kept[block, 2 * hidden :]
-        parts = (
-            tn(rows[:, :width], kept[block, hidden : 2 * hidden]),
-            tn(kept[block, :hidden], scaled),
-        )
-        if i == 0:
-            up_ref[...], down_ref[...] = parts
-        else:
-            up_ref[...] += parts[0]
-            down_ref[...] += parts[1]
-    for ref in others:
-        rows, scaled = ref[:count], ref[count:]
+    rows = stack([far[:, :width], near[:, :width]])
+    up_grad = tn(rows, kept[:, hidden : 2 * hidden])
+    down_grad = tn(kept[:, :hidden], kept[:, 2 * hidden :])
+    for pair in zip(others[::2], others[1::2]):
+        rows = stack([part[:count] for part in pair])
+        scaled = stack([part[count:] for part in pair])
         active, slope = expert_forward(rows, up)
         inner_grad = jnp.concatenate([nt(scaled, part) for part in down], axis=1)
-        up_ref[...] += tn(rows, (inner_grad * slope).astype(BF))
-        down_ref[...] += tn(active, scaled)
+        up_grad = up_grad + tn(rows, (inner_grad * slope).astype(BF))
+        down_grad = down_grad + tn(active, scaled)
+    up_ref[...] = up_grad
+    down_ref[...] = down_grad
 
 
 def table_lanes(share):
@@ -439,6 +495,7 @@
     first_grad_ref,
     joint_grad_ref,
     distance_ref,
+    mixed_ref,
 ):
     count, width = cotangent.shape
     half = width // 2
@@ -448,9 +505,10 @@
     slot = lax.broadcasted_iota(jnp.int32, (count, home.shape[0]), 1)
     lane = lax.broadcasted_iota(jnp.int32, (count, LANES), 1)
     gates = [high[:, width + c : width + c + 1] for c in range(2)]
-    back = home[:, : width + LANES]
-    routed = [matmul((slot == target[:, c : c + 1]).astype(BF), back) for c in range(2)]
-    dots = [jnp.sum(value[:, width:], axis=-1, keepdims=True) for value in routed]
+    routed = [matmul((slot == target[:, c : c + 1]).astype(BF), home[...]) for c in range(2)]
+    returned = [value[:, width:] for value in routed]
+    upstream = cotangent[...].astype(F32)
+    dots = [jnp.sum(upstream * value, axis=-1, keepdims=True) for value in returned]
     mean = gates[0] * dots[0] + gates[1] * dots[1]
     logit_grad = jnp.zeros((count, LANES), F32)
     for c in range(2):
@@ -460,10 +518,11 @@
     second_grad = second_grad + matmul(logit_grad, small_rows[:LANES])
     gain = small_rows[experts + 1 : experts + 2].astype(F32)
     first = high[:, :width]
+    mixed_ref[...] = (first + gates[0] * returned[0] + gates[1] * returned[1]).astype(BF)
     inverse = inverse_rms(first)
     unit = first * inverse
     scaled = second_grad * gain
-    first_grad = cotangent[...].astype(F32) + inverse * (
+    first_grad = upstream + inverse * (
         scaled - unit * jnp.mean(unit * scaled, axis=-1, keepdims=True)
     )
     first_grad_ref[...] = first_grad
@@ -552,19 +611,9 @@
     near,
     far,
     place_of,
-    returned,
-    target,
-    high,
     token_ref,
-    mixed_ref,
 ):
-    count, width = tokens.shape
-    slot = lax.broadcasted_iota(jnp.int32, (count, returned.shape[0]), 1)
-    mixed = high[:, :width]
-    for c in range(2):
-        gate = high[:, width + c : width + c + 1]
-        mixed = mixed + gate * matmul((slot == target[:, c : c + 1]).astype(BF), returned[...])
-    mixed_ref[...] = mixed.astype(BF)
+    width = tokens.shape[1]
     shuffle = shuffle_of(place_of)
     gain = small_of(small_lanes(experts), near, far, shuffle)[experts : experts + 1].astype(F32)
     grads = joint_grad[...]
@@ -581,18 +630,25 @@
     token_ref[...] = (first_grad[...] + input_grad).astype(BF)
 
 
-def finish_kernel(experts, project_in, gain, *refs):
+def finish_kernel(experts, leads, project_in, gain, *refs):
     parts, refs = refs[:-6], refs[-6:]
     grad_in_ref, sum_out_ref, router_ref, first_gain_ref, second_gain_ref, table_ref = refs
-    sums = sum(part[...].astype(F32) for part in parts)
+    sums = jnp.concatenate([sum_of(parts[:leads]), sum_of(parts[leads:])], axis=1)
     share, width = sum_out_ref.shape
     grad_in = sums[:, : 3 * width]
     grad_in_ref[...] = grad_in
     sum_out_ref[...] = sums[:, 3 * width : 4 * width]
     small = sums[:, 4 * width :]
-    router_ref[...] = small[:, :experts]
     row = lax.broadcasted_iota(jnp.int32, (share, share), 0)
     same = row == lax.broadcasted_iota(jnp.int32, (share, share), 1)
+
+    router_ref[...] = lax.dot_general(
+        small[:, :experts],
+        same.astype(F32),
+        (((0,), (0,)), ((), ())),
+        precision=lax.Precision.HIGHEST,
+        preferred_element_type=F32,
+    )
 
     def lined(column):
         return jnp.sum(jnp.where(same, column, 0.0), axis=0, keepdims=True)
@@ -605,7 +661,7 @@
     value_row = lax.broadcasted_iota(jnp.int32, (share, HEADS), 0) * lanes
     value_head = lax.broadcasted_iota(jnp.int32, (share, HEADS), 1)
     step = min(lanes, BUCKETS)
-    total = jnp.zeros((BUCKETS, HEADS), F32)
+    total = jnp.zeros((HEADS, BUCKETS), F32)
     for start in range(0, max(lanes, BUCKETS), step):
         if lanes <= BUCKETS:
             picked, part = value_row == value_head * BUCKETS + start, table
@@ -613,14 +669,14 @@
             picked = value_row + start == value_head * BUCKETS
             part = table[:, start : start + step]
         put = lax.dot_general(
+            picked.astype(F32),
             part,
-            picked.astype(F32),
             (((0,), (0,)), ((), ())),
             precision=lax.Precision.HIGHEST,
             preferred_element_type=F32,
         )
         if lanes <= BUCKETS:
-            table_ref[start : start + step] = put
+            table_ref[:, start : start + step] = put
         else:
             total = total + put
             table_ref[...] = total
@@ -714,7 +770,7 @@
 
     chips = len(chip_masks())
     piece = expert_up.shape[2]
-    wide = (rows_here, 2 * width + LANES)
+    wide = (rows_here, 2 * width)
     row_far, row_near, kept, shown = kernel_call(
         functools.partial(expert_kernel, chips),
         [
@@ -724,14 +780,13 @@
             ((2 * rows_here, width), BF),
         ],
         16 * rows_here * width * chips * piece,
-        column.astype(jnp.int32).reshape(1, 1),
         row_parts[1],
         row_parts[0],
         grad_parts[1],
         grad_parts[0],
         *weights,
         *downs,
-        fetch=range(5, 5 + 2 * chips),
+        fetch=range(4, 4 + 2 * chips),
         scratch=56,
     )
     others = [swap(shown, mask) for mask in chip_masks()[1:]]
@@ -742,7 +797,7 @@
     half = width // 2
     table_at = experts + 1
     spread_lanes = -(-(table_at + table_lanes(share)) // LANES) * LANES
-    keep, send, first_grad, joint_grad, _ = kernel_call(
+    keep, send, first_grad, joint_grad, _, mixed = kernel_call(
         functools.partial(home_kernel, experts, share),
         [
             ((half, 4 * width + spread_lanes), BF),
@@ -750,6 +805,7 @@
             ((count, width), F32),
             ((count, 3 * width), BF),
             ((HEADS, count), F32),
+            ((count, width), BF),
         ],
         2 * count * width * 10 * width,
         home,
@@ -770,8 +826,22 @@
         ),
         scratch=56,
     )
-    def meanwhile(begun):
-        grad_up, grad_down = kernel_call(
+    def token_parts(begun):
+        return kernel_call(
+            functools.partial(token_kernel, experts),
+            [((count, width), BF)],
+            2 * count * width * 6 * width,
+            tokens,
+            first_grad,
+            after(joint_grad, begun),
+            *halves,
+            place_of[None],
+            fetch=(3, 4, 0, 1, 2),
+            scratch=56,
+        )
+
+    def weight_parts(begun):
+        return kernel_call(
             weight_grad_kernel,
             [((width, piece), F32), ((piece, width), F32)],
             16 * rows_here * width * chips * piece,
@@ -784,57 +854,35 @@
             fetch=range(5 + len(others)),
             scratch=56,
         )
-        token_grad, mixed = kernel_call(
-            functools.partial(token_kernel, experts),
-            [((count, width), BF), ((count, width), BF)],
-            2 * count * width * 6 * width,
-            tokens,
-            first_grad,
-            after(joint_grad, begun),
-            *halves,
-            place_of[None],
-            home,
-            target,
-            high,
-            fetch=(
-                (6, (slice(None), slice(width + LANES, None)), (rows_here, width)),
-                (8, (slice(None), slice(0, width + LANES)), (count, width + LANES)),
-                3,
-                4,
-                0,
-                1,
-                2,
-            ),
-            scratch=56,
-        )
-        return grad_up, grad_down, token_grad, mixed
-
-    blocks, done = scatter_blocks(keep, send, meanwhile)
-    grad_up, grad_down, token_grad, mixed = done
+
+    leads, trails, (grad_up, grad_down), (token_grad,) = scatter_blocks(
+        keep, send, weight_parts, token_parts
+    )
     grad_in, sum_out, grad_router, grad_first_gain, grad_second_gain, table_total = kernel_call(
-        functools.partial(finish_kernel, experts),
+        functools.partial(finish_kernel, experts, len(leads)),
         [
             ((share, 3 * width), F32),
             ((share, width), F32),
-            ((share, experts), F32),
+            ((experts, share), F32),
             ((1, share), F32),
             ((1, share), F32),
-            ((BUCKETS, HEADS), F32),
+            ((HEADS, BUCKETS), F32),
         ],
         share * width * 8,
         project_in,
         first_gain[None],
-        *blocks,
+        *leads,
+        *trails,
     )
     return (
         mixed,
         token_grad,
         grad_in,
         sum_out,
-        grad_router,
+        grad_router.T,
         grad_first_gain[0],
         grad_second_gain[0],
-        table_total,
+        table_total.T,
         grad_up[None],
         grad_down[None],
     )

time: 239 us -> 230 us (0.962)
  waiting for transfers between devices: 92.6 us -> 77.4 us
  local copies, waits for them, and re-layouts: 16.2 us -> 20.6 us
  starting transfers between devices: 31.8 us -> 35.1 us
    ppermute x21 -> x25, waiting for transfers between devices: 82.9 us -> 69.7 us  [swap(): lax.ppermute(value, AXES, [(i, i ^ mask) for i in range(columns * experts)])]
    unnamed x59 -> x74, local copies, waits for them, and re-layouts: 12.6 us -> 15.9 us
    ppermute x21 -> x25, starting transfers between devices: 22.6 us -> 25.8 us  [swap(): lax.ppermute(value, AXES, [(i, i ^ mask) for i in range(columns * experts)])]
    pallas_call x10 -> x13, Pallas kernels: 66.6 us -> 64.4 us  [kernel_call(): pl.pallas_call(kernel, out_shape=[jax.ShapeDtypeStruct(shape, kind) for s...]
  transfers between devices with their start and end apart: 23 -> 27, of which waited for: 14 -> 12; matrix products, arithmetic and copies ran while one was open for 5% -> 6% of each run, Pallas kernels for 14% -> 14%
where the time goes in v3:
time: 230 us; the launch traced here: 229 us
  waiting for transfers between devices  77.4 us (34%)
  Pallas kernels  64.4 us (28%)
  starting transfers between devices  35.1 us (15%)
  blocking collectives  22.6 us (10%)
  local copies, waits for them, and re-layouts  20.6 us (9%)
  other arithmetic  5.79 us (3%)
    ppermute x25, waiting for transfers between devices, swap(): lax.ppermute(value, AXES, [(i, i ^ mask) for i in range(columns * experts)])  69.7 us
    pallas_call x13, Pallas kernels, kernel_call(): pl.pallas_call(kernel, out_shape=[jax.ShapeDtypeStruct(shape, kind) for s...  64.4 us
    ppermute x25, starting transfers between devices, swap(): lax.ppermute(value, AXES, [(i, i ^ mask) for i in range(columns * experts)])  25.8 us
    all_to_all x1, blocking collectives, exchange(): lax.all_to_all(blocks, 'expert', split_axis=0, concat_axis=0, tiled=True)  22.6 us
    unnamed x74, local copies, waits for them, and re-layouts  15.9 us
    all_to_all x2, starting transfers between devices, exchange(): lax.all_to_all(blocks, 'expert', split_axis=0, concat_axis=0, tiled=True)  9.36 us
    all_to_all x2, waiting for transfers between devices, exchange(): lax.all_to_all(blocks, 'expert', split_axis=0, concat_axis=0, tiled=True)  7.68 us
    concatenate x3, other arithmetic, stack(): return jnp.concatenate(parts, axis=0)  4.99 us
  transfers between devices with their start and end apart: 27, of which 12 were waited for; matrix products, arithmetic and copies ran while one was open for 6% of the time, Pallas kernels for 14%

profile of v3, /device:TPU:0, one launch (start us, length us, event | category | flops | bytes accessed | tf_op | source)
XLA Modules:
  0.0 229.0 jit_solution(7671958538623795525)
XLA Ops:
  0.7 2.1 shard_map.222
  2.7 5.1 %collective-permute-start.2 = (bf16[24,3200]{1,0:T(8,128)(2,1)}, bf16[24,3200]{1,0:T(8,128)(2,1)}, u32[]{:S(2)}, u32[]{:S(2)}) collective-permute-start(bf16[24,3200]{1,0:T(8,128)(2,1)} %get-tuple-element.48), channel_id=1, source_target_pairs={{0,6},{1,7},{2,4},{3,5},{4,2},{5,3},{6,0},{7,1},{8,14},{9,15},{10,... | collective-permute-start | bytes 460808 | tf_op jit(solution)/shard_map/ppermute | solution.py:80
  8.5 1.6 collective-permute-start.3
  14.2 2.3 %collective-permute-done.1 = bf16[24,3200]{1,0:T(8,128)(2,1)} collective-permute-done((bf16[24,3200]{1,0:T(8,128)(2,1)}, bf16[24,3200]{1,0:T(8,128)(2,1)}, u32[]{:S(2)}, u32[]{:S(2)}) %collective-permute-start.1) | collective-permute-done | bytes 153632 | tf_op jit(solution)/shard_map/ppermute | solution.py:80
  16.6 4.6 %collective-permute-done = bf16[24,3200]{1,0:T(8,128)(2,1)} collective-permute-done((bf16[24,3200]{1,0:T(8,128)(2,1)}, bf16[24,3200]{1,0:T(8,128)(2,1)}, u32[]{:S(2)}, u32[]{:S(2)}) %collective-permute-start) | collective-permute-done | bytes 153632 | tf_op jit(solution)/shard_map/ppermute | solution.py:80
  21.2 1.9 pad_maximum_fusion.2.refs_0_
  23.9 2.4 %collective-permute-start.6 = (bf16[96,3200]{1,0:T(8,128)(2,1)}, bf16[96,3200]{1,0:T(8,128)(2,1)S(1)}, u32[]{:S(2)}, u32[]{:S(2)}) collective-permute-start(bf16[96,3200]{1,0:T(8,128)(2,1)} %shard_map.223), channel_id=1, source_target_pairs={{0,17},{1,16},{2,19},{3,18},{4,21},{5,20},{6,23},{7,22},{8,25},{9,... | collective-permute-start | bytes 1843208 | tf_op jit(solution)/shard_map/ppermute | solution.py:80
  28.5 4.7 %all-to-all-start = ((bf16[8,48,768]{2,1,0:T(8,128)(2,1)}), bf16[8,48,768]{2,1,0:T(8,128)(2,1)S(1)}, u32[]{:S(2)}, u32[]{:S(2)}) async-start(bf16[8,48,768]{2,1,0:T(8,128)(2,1)} %bitcast.8), calls=%async_computation | async-start | bytes 1179648 | tf_op jit(solution)/shard_map/all_to_all | solution.py:195
  33.2 10.6 %collective-permute-done.6 = bf16[96,3200]{1,0:T(8,128)(2,1)S(1)} collective-permute-done((bf16[96,3200]{1,0:T(8,128)(2,1)}, bf16[96,3200]{1,0:T(8,128)(2,1)S(1)}, u32[]{:S(2)}, u32[]{:S(2)}) %collective-permute-start.6) | collective-permute-done | bytes 614432 | tf_op jit(solution)/shard_map/ppermute | solution.py:80
  43.9 14.0 %collective-permute-done.5 = bf16[96,3200]{1,0:T(8,128)(2,1)S(1)} collective-permute-done((bf16[96,3200]{1,0:T(8,128)(2,1)}, bf16[96,3200]{1,0:T(8,128)(2,1)S(1)}, u32[]{:S(2)}, u32[]{:S(2)}) %collective-permute-start.5) | collective-permute-done | bytes 614432 | tf_op jit(solution)/shard_map/ppermute | solution.py:80
  57.9 1.7 pad_maximum_fusion.refs_0_
  62.6 1.5 collective-permute-start.10
  66.2 1.5 copy-done.15
  67.7 10.8 %shard_map.225 = (bf16[128,4608]{1,0:T(8,128)(2,1)}, f32[128,2432]{1,0:T(8,128)}, bf16[384,896]{1,0:T(8,128)(2,1)}) custom-call(bf16[128,768]{1,0:T(8,128)(2,1)} %refs_0_.4, s32[1,768]{1,0:T(1,128)} %broadcast_in_dim.12.refs_1_.refs_4_.refs_5_, bf16[384,3200]{1,0:T(8,128)(2,1)} %shard_map.224.refs_2_.refs_1_.refs_7_.refs_3_, bf16[384,3200]{1,0:T(8,128)(2,1)} %copy-done.15, ...), custom_call_target="tpu_custom_call" | custom-call | tf_op jit(solution)/shard_map/pallas_call | solution.py:273
  78.4 22.6 %all_to_all.15 = bf16[8,48,896]{2,1,0:T(8,128)(2,1)S(1)} all-to-all(bf16[8,48,896]{2,1,0:T(8,128)(2,1)} %bitcast.42), channel_id=1, replica_groups=mesh['fsdp'=4,'expert'=8] {'expert'}, dimensions={0} | all-to-all | bytes 1376256 | tf_op jit(solution)/shard_map/all_to_all | solution.py:195
  101.5 2.5 %collective-permute-done.9.refs_2_ = bf16[384,768]{1,0:T(8,128)(2,1)S(1)} collective-permute-done((bf16[384,768]{1,0:T(8,128)(2,1)S(1)}, bf16[384,768]{1,0:T(8,128)(2,1)S(1)}, u32[]{:S(2)}, u32[]{:S(2)}) %collective-permute-start.9) | collective-permute-done | bytes 589856 | tf_op jit(solution)/shard_map/ppermute | solution.py:80
  104.0 3.6 %collective-permute-done.10.refs_5_ = bf16[1280,768]{1,0:T(8,128)(2,1)} collective-permute-done((bf16[1280,768]{1,0:T(8,128)(2,1)}, bf16[1280,768]{1,0:T(8,128)(2,1)}, u32[]{:S(2)}, u32[]{:S(2)}) %collective-permute-start.10) | collective-permute-done | bytes 1966112 | tf_op jit(solution)/shard_map/ppermute | solution.py:80
  108.5 15.2 %shard_map.227 = (bf16[384,1536]{1,0:T(8,128)(2,1)}, bf16[384,1536]{1,0:T(8,128)(2,1)}, bf16[768,2304]{1,0:T(8,128)(2,1)}, bf16[768,768]{1,0:T(8,128)(2,1)}) custom-call(bf16[384,896]{1,0:T(8,128)(2,1)} %copy-done.23, bf16[384,896]{1,0:T(8,128)(2,1)} %bitcast.34, bf16[384,768]{1,0:T(8,128)(2,1)} %copy-done.27, bf16[384,768]{1,0:T(8,128)(2,1)} %bitcast.37, ...), custom_call_target="tpu_custom_call" | custom-call | tf_op jit(solution)/shard_map/pallas_call | solution.py:273
  123.8 1.6 collective-permute-start.12
  125.3 1.5 collective-permute-done.11.refs_1_
  129.4 4.7 %all-to-all-start.2 = ((bf16[8,48,1536]{2,1,0:T(8,128)(2,1)}), bf16[8,48,1536]{2,1,0:T(8,128)(2,1)S(1)}, u32[]{:S(2)}, u32[]{:S(2)}) async-start(bf16[8,48,1536]{2,1,0:T(8,128)(2,1)} %bitcast.14), calls=%async_computation.2 | async-start | bytes 2359296 | tf_op jit(solution)/shard_map/all_to_all | solution.py:195
  134.0 18.3 %collective-permute-done.12.refs_1_.refs_5_ = bf16[768,768]{1,0:T(8,128)(2,1)S(1)} collective-permute-done((bf16[768,768]{1,0:T(8,128)(2,1)}, bf16[768,768]{1,0:T(8,128)(2,1)S(1)}, u32[]{:S(2)}, u32[]{:S(2)}) %collective-permute-start.12) | collective-permute-done | bytes 1179680 | tf_op jit(solution)/shard_map/ppermute | solution.py:80
  152.4 1.5 copy.49.refs_9_
  155.2 7.7 %all-to-all-done.2 = bf16[8,48,1536]{2,1,0:T(8,128)(2,1)S(1)} async-done(((bf16[8,48,1536]{2,1,0:T(8,128)(2,1)}), bf16[8,48,1536]{2,1,0:T(8,128)(2,1)S(1)}, u32[]{:S(2)}, u32[]{:S(2)}) %all-to-all-start.2) | async-done | bytes 1179680 | tf_op jit(solution)/shard_map/all_to_all | solution.py:195
  164.0 14.5 %shard_map.230 = (bf16[384,3200]{1,0:T(8,128)(2,1)}, bf16[384,3200]{1,0:T(8,128)(2,1)}, f32[128,768]{1,0:T(8,128)}, bf16[128,2304]{1,0:T(8,128)(2,1)}, f32[12,128]{1,0:T(8,128)}, /*index=5*/bf16[128,768]{1,0:T(8,128)(2,1)}) custom-call(bf16[384,1536]{1,0:T(8,128)(2,1)} %shard_map.229.refs_0_, s32[128,2]{1,0:T(8,128)} %copy.46.refs_6_.refs_1_, ...), custom_call_target="tpu_custom_call" | custom-call | tf_op jit(solution)/shard_map/pallas_call | solution.py:273
  178.5 4.9 %collective-permute-done.14.refs_1_ = bf16[384,3200]{1,0:T(8,128)(2,1)S(1)} collective-permute-done((bf16[384,3200]{1,0:T(8,128)(2,1)}, bf16[384,3200]{1,0:T(8,128)(2,1)S(1)}, u32[]{:S(2)}, u32[]{:S(2)}) %collective-permute-start.14) | collective-permute-done | bytes 2457632 | tf_op jit(solution)/shard_map/ppermute | solution.py:80
  183.4 1.7 copy-done.1
  189.9 6.6 %collective-permute-done.21.refs_1_ = bf16[192,896]{1,0:T(8,128)(2,1)S(1)} collective-permute-done((bf16[192,896]{1,0:T(8,128)(2,1)S(1)}, bf16[192,896]{1,0:T(8,128)(2,1)S(1)}, u32[]{:S(2)}, u32[]{:S(2)}) %collective-permute-start.21) | collective-permute-done | bytes 344096 | tf_op jit(solution)/shard_map/ppermute | solution.py:80
  197.3 11.7 %shard_map.237 = (f32[768,768]{1,0:T(8,128)}, f32[768,768]{1,0:T(8,128)}) custom-call(bf16[1280,768]{1,0:T(8,128)(2,1)} %shard_map.226.refs_4_.refs_0_, bf16[256,768]{1,0:T(8,128)(2,1)} %get-tuple-element.49.refs_6_.refs_1_, bf16[768,2304]{1,0:T(8,128)(2,1)} %shard_map.236.refs_2_, bf16[384,896]{1,0:T(8,128)(2,1)} %copy-done.23, bf16[384,896]{1,0:T(8,128)(2,1)} %bitcast.35, ...), custom_call_target="tpu_custom_call" | custom-call | tf_op jit(solution)/shard_map/pallas_call | solution.py:273
  212.9 2.6 %collective-permute-start.18 = (bf16[24,2304]{1,0:T(8,128)(2,1)S(1)}, bf16[24,2304]{1,0:T(8,128)(2,1)S(1)}, u32[]{:S(2)}, u32[]{:S(2)}) collective-permute-start(bf16[24,2304]{1,0:T(8,128)(2,1)S(1)} %get-tuple-element.66), channel_id=1, source_target_pairs={{0,4},{1,5},{2,6},{3,7},{4,0},{5,1},{6,2},{7,3},{8,12},{9,13},{10,... | collective-permute-start | bytes 331784 | tf_op jit(solution)/shard_map/ppermute | solution.py:80
  215.7 1.5 collective-permute-start.20
  220.2 7.0 %shard_map.234.refs_1_ = bf16[128,768]{1,0:T(8,128)(2,1)} custom-call(bf16[128,768]{1,0:T(8,128)(2,1)} %refs_0_.4, f32[128,768]{1,0:T(8,128)} %get-tuple-element.57.refs_1_, bf16[128,2304]{1,0:T(8,128)(2,1)} %shard_map.233.refs_2_, bf16[384,3200]{1,0:T(8,128)(2,1)} %shard_map.224.refs_2_.refs_1_.refs_7_.refs_3_, bf16[384,3200]{1,0:T(8,128)(2,1)} %copy-done.15, ...), custom_call_target="tpu_custom_call" | custom-call | tf_op jit(solution)/shard_map/pallas_call | solution.py:273
  (133 shorter events, 33.6 us)
Async XLA Ops:
  0.6 61.2 %copy-start = (f32[32,12]{0,1:T(8,128)S(1)}, f32[32,12]{0,1:T(8,128)}, u32[]{:S(2)}) copy-start(f32[32,12]{0,1:T(8,128)} %param.22) | copy-start | bytes 4612
  0.7 10.7 %copy-start.25 = (bf16[1,768,768]{2,1,0:T(8,128)(2,1)S(1)}, bf16[1,768,768]{2,1,0:T(8,128)(2,1)}, u32[]{:S(2)}) copy-start(bf16[1,768,768]{2,1,0:T(8,128)(2,1)} %param.23) | copy-start | bytes 3538948
  2.7 11.5 %collective-permute-start.2 = (bf16[24,3200]{1,0:T(8,128)(2,1)}, bf16[24,3200]{1,0:T(8,128)(2,1)}, u32[]{:S(2)}, u32[]{:S(2)}) collective-permute-start(bf16[24,3200]{1,0:T(8,128)(2,1)} %get-tuple-element.48), channel_id=1, source_target_pairs={{0,6},{1,7},{2,4},{3,5},{4,2},{5,3},{6,0},{7,1},{8,14},{9,15},{10,... | collective-permute-start | bytes 460808 | tf_op jit(solution)/shard_map/ppermute | solution.py:80
  7.9 8.7 %collective-permute-start.1 = (bf16[24,3200]{1,0:T(8,128)(2,1)}, bf16[24,3200]{1,0:T(8,128)(2,1)}, u32[]{:S(2)}, u32[]{:S(2)}) collective-permute-start(bf16[24,3200]{1,0:T(8,128)(2,1)} %get-tuple-element.48), channel_id=1, source_target_pairs={{0,2},{1,3},{2,0},{3,1},{4,6},{5,7},{6,4},{7,5},{8,10},{9,11},{10,... | collective-permute-start | bytes 460808 | tf_op jit(solution)/shard_map/ppermute | solution.py:80
  7.9 13.3 %collective-permute-start = (bf16[24,3200]{1,0:T(8,128)(2,1)}, bf16[24,3200]{1,0:T(8,128)(2,1)}, u32[]{:S(2)}, u32[]{:S(2)}) collective-permute-start(bf16[24,3200]{1,0:T(8,128)(2,1)} %get-tuple-element.48), channel_id=1, source_target_pairs={{0,4},{1,5},{2,6},{3,7},{4,0},{5,1},{6,2},{7,3},{8,12},{9,13},{10,... | collective-permute-start | bytes 460808 | tf_op jit(solution)/shard_map/ppermute | solution.py:80
  8.5 14.6 %collective-permute-start.3 = (bf16[256,768]{1,0:T(8,128)(2,1)}, bf16[256,768]{1,0:T(8,128)(2,1)S(1)}, u32[]{:S(2)}, u32[]{:S(2)}) collective-permute-start(bf16[256,768]{1,0:T(8,128)(2,1)} %get-tuple-element.49.refs_6_.refs_1_), channel_id=1, source_target_pairs={{0,16},{1,17},{2,18},{3,19},{4,20},{5,21},{6,22},{7,23},{8,24},{9,... | collective-permute-start | bytes 1179656 | tf_op jit(solution)/shard_map/ppermute | solution.py:80
  23.9 34.0 %copy-start.18 = (bf16[96,3200]{1,0:T(8,128)(2,1)S(1)}, bf16[96,3200]{1,0:T(8,128)(2,1)}, u32[]{:S(2)}) copy-start(bf16[96,3200]{1,0:T(8,128)(2,1)} %shard_map.223) | copy-start | bytes 1843204
  23.9 20.0 %collective-permute-start.6 = (bf16[96,3200]{1,0:T(8,128)(2,1)}, bf16[96,3200]{1,0:T(8,128)(2,1)S(1)}, u32[]{:S(2)}, u32[]{:S(2)}) collective-permute-start(bf16[96,3200]{1,0:T(8,128)(2,1)} %shard_map.223), channel_id=1, source_target_pairs={{0,17},{1,16},{2,19},{3,18},{4,21},{5,20},{6,23},{7,22},{8,25},{9,... | collective-permute-start | bytes 1843208 | tf_op jit(solution)/shard_map/ppermute | solution.py:80
  26.3 31.6 %collective-permute-start.5 = (bf16[96,3200]{1,0:T(8,128)(2,1)}, bf16[96,3200]{1,0:T(8,128)(2,1)S(1)}, u32[]{:S(2)}, u32[]{:S(2)}) collective-permute-start(bf16[96,3200]{1,0:T(8,128)(2,1)} %shard_map.223), channel_id=1, source_target_pairs={{0,1},{1,0},{2,3},{3,2},{4,5},{5,4},{6,7},{7,6},{8,9},{9,8},{10,11... | collective-permute-start | bytes 1843208 | tf_op jit(solution)/shard_map/ppermute | solution.py:80
  26.8 31.1 %collective-permute-start.4 = (bf16[96,3200]{1,0:T(8,128)(2,1)}, bf16[96,3200]{1,0:T(8,128)(2,1)S(1)}, u32[]{:S(2)}, u32[]{:S(2)}) collective-permute-start(bf16[96,3200]{1,0:T(8,128)(2,1)} %shard_map.223), channel_id=1, source_target_pairs={{0,16},{1,17},{2,18},{3,19},{4,20},{5,21},{6,22},{7,23},{8,24},{9,... | collective-permute-start | bytes 1843208 | tf_op jit(solution)/shard_map/ppermute | solution.py:80
  28.5 31.0 %all-to-all-start = ((bf16[8,48,768]{2,1,0:T(8,128)(2,1)}), bf16[8,48,768]{2,1,0:T(8,128)(2,1)S(1)}, u32[]{:S(2)}, u32[]{:S(2)}) async-start(bf16[8,48,768]{2,1,0:T(8,128)(2,1)} %bitcast.8), calls=%async_computation | async-start | bytes 1179648 | tf_op jit(solution)/shard_map/all_to_all | solution.py:195
  60.4 5.8 %collective-permute-start.7 = (bf16[384,3200]{1,0:T(8,128)(2,1)}, bf16[384,3200]{1,0:T(8,128)(2,1)S(1)}, u32[]{:S(2)}, u32[]{:S(2)}) collective-permute-start(bf16[384,3200]{1,0:T(8,128)(2,1)} %shard_map.224.refs_2_.refs_1_.refs_7_.refs_3_), channel_id=1, source_target_pairs={{0,8},{1,9},{2,10},{3,11},{4,12},{5,13},{6,14},{7,15},{8,0},{9,1},... | collective-permute-start | bytes 7372808 | tf_op jit(solution)/shard_map/ppermute | solution.py:80
  62.6 45.0 %collective-permute-start.10 = (bf16[1280,768]{1,0:T(8,128)(2,1)}, bf16[1280,768]{1,0:T(8,128)(2,1)}, u32[]{:S(2)}, u32[]{:S(2)}) collective-permute-start(bf16[1280,768]{1,0:T(8,128)(2,1)} %shard_map.226.refs_4_.refs_0_), channel_id=1, source_target_pairs={{0,16},{1,17},{2,18},{3,19},{4,20},{5,21},{6,22},{7,23},{8,24},{9,... | collective-permute-start | bytes 5898248 | tf_op jit(solution)/shard_map/ppermute | solution.py:80
  66.2 34.8 %copy-start.20 = (bf16[8,48,768]{2,1,0:T(8,128)(2,1)S(1)}, bf16[8,48,768]{2,1,0:T(8,128)(2,1)}, u32[]{:S(2)}) copy-start(bf16[8,48,768]{2,1,0:T(8,128)(2,1)} %copy-done.19) | copy-start | bytes 1769476
  101.0 6.6 %collective-permute-start.8 = (bf16[384,896]{1,0:T(8,128)(2,1)S(1)}, bf16[384,896]{1,0:T(8,128)(2,1)S(1)}, u32[]{:S(2)}, u32[]{:S(2)}) collective-permute-start(bf16[384,896]{1,0:T(8,128)(2,1)S(1)} %bitcast.33), channel_id=1, source_target_pairs={{0,8},{1,9},{2,10},{3,11},{4,12},{5,13},{6,14},{7,15},{8,0},{9,1},... | collective-permute-start | bytes 2064392 | tf_op jit(solution)/shard_map/ppermute | solution.py:80
  101.0 3.0 %collective-permute-start.9 = (bf16[384,768]{1,0:T(8,128)(2,1)S(1)}, bf16[384,768]{1,0:T(8,128)(2,1)S(1)}, u32[]{:S(2)}, u32[]{:S(2)}) collective-permute-start(bf16[384,768]{1,0:T(8,128)(2,1)S(1)} %bitcast.38), channel_id=1, source_target_pairs={{0,8},{1,9},{2,10},{3,11},{4,12},{5,13},{6,14},{7,15},{8,0},{9,1},... | collective-permute-start | bytes 1769480 | tf_op jit(solution)/shard_map/ppermute | solution.py:80
  123.7 3.1 %collective-permute-start.11 = (bf16[384,1536]{1,0:T(8,128)(2,1)}, bf16[384,1536]{1,0:T(8,128)(2,1)S(1)}, u32[]{:S(2)}, u32[]{:S(2)}) collective-permute-start(bf16[384,1536]{1,0:T(8,128)(2,1)} %get-tuple-element.52), channel_id=1, source_target_pairs={{0,8},{1,9},{2,10},{3,11},{4,12},{5,13},{6,14},{7,15},{8,0},{9,1},... | collective-permute-start | bytes 3538952 | tf_op jit(solution)/shard_map/ppermute | solution.py:80
  123.8 28.6 %collective-permute-start.12 = (bf16[768,768]{1,0:T(8,128)(2,1)}, bf16[768,768]{1,0:T(8,128)(2,1)S(1)}, u32[]{:S(2)}, u32[]{:S(2)}) collective-permute-start(bf16[768,768]{1,0:T(8,128)(2,1)} %get-tuple-element.53), channel_id=1, source_target_pairs={{0,16},{1,17},{2,18},{3,19},{4,20},{5,21},{6,22},{7,23},{8,24},{9,... | collective-permute-start | bytes 3538952 | tf_op jit(solution)/shard_map/ppermute | solution.py:80
  129.4 24.5 %copy-start.31 = (s32[128,2]{0,1:T(2,128)S(1)}, s32[128,2]{0,1:T(2,128)}, u32[]{:S(2)}) copy-start(s32[128,2]{0,1:T(2,128)} %copy-done.30) | copy-start | bytes 3076
  129.4 33.5 %all-to-all-start.2 = ((bf16[8,48,1536]{2,1,0:T(8,128)(2,1)}), bf16[8,48,1536]{2,1,0:T(8,128)(2,1)S(1)}, u32[]{:S(2)}, u32[]{:S(2)}) async-start(bf16[8,48,1536]{2,1,0:T(8,128)(2,1)} %bitcast.14), calls=%async_computation.2 | async-start | bytes 2359296 | tf_op jit(solution)/shard_map/all_to_all | solution.py:195
  152.4 2.8 %collective-permute-start.13 = (bf16[768,768]{1,0:T(8,128)(2,1)S(1)}, bf16[768,768]{1,0:T(8,128)(2,1)S(1)}, u32[]{:S(2)}, u32[]{:S(2)}) collective-permute-start(bf16[768,768]{1,0:T(8,128)(2,1)S(1)} %collective-permute-done.12.refs_1_.refs_5_), channel_id=1, source_target_pairs={{0,8},{1,9},{2,10},{3,11},{4,12},{5,13},{6,14},{7,15},{8,0},{9,1},... | collective-permute-start | bytes 3538952 | tf_op jit(solution)/shard_map/ppermute | solution.py:80
  178.4 5.0 %collective-permute-start.14 = (bf16[384,3200]{1,0:T(8,128)(2,1)}, bf16[384,3200]{1,0:T(8,128)(2,1)S(1)}, u32[]{:S(2)}, u32[]{:S(2)}) collective-permute-start(bf16[384,3200]{1,0:T(8,128)(2,1)} %get-tuple-element.60), channel_id=1, source_target_pairs={{0,8},{1,9},{2,10},{3,11},{4,12},{5,13},{6,14},{7,15},{8,0},{9,1},... | collective-permute-start | bytes 7372808 | tf_op jit(solution)/shard_map/ppermute | solution.py:80
  186.4 10.1 %collective-permute-start.21 = (bf16[192,896]{1,0:T(8,128)(2,1)S(1)}, bf16[192,896]{1,0:T(8,128)(2,1)S(1)}, u32[]{:S(2)}, u32[]{:S(2)}) collective-permute-start(bf16[192,896]{1,0:T(8,128)(2,1)S(1)} %get-tuple-element.70), channel_id=1, source_target_pairs={{0,2},{1,3},{2,0},{3,1},{4,6},{5,7},{6,4},{7,5},{8,10},{9,11},{10,... | collective-permute-start | bytes 1032200 | tf_op jit(solution)/shard_map/ppermute | solution.py:80
  186.4 25.5 %collective-permute-start.15 = (bf16[96,2304]{1,0:T(8,128)(2,1)S(1)}, bf16[96,2304]{1,0:T(8,128)(2,1)S(1)}, u32[]{:S(2)}, u32[]{:S(2)}) collective-permute-start(bf16[96,2304]{1,0:T(8,128)(2,1)S(1)} %get-tuple-element.62), channel_id=1, source_target_pairs={{0,16},{1,17},{2,18},{3,19},{4,20},{5,21},{6,22},{7,23},{8,24},{9,... | collective-permute-start | bytes 1327112 | tf_op jit(solution)/shard_map/ppermute | solution.py:80
  187.8 24.1 %collective-permute-start.16 = (bf16[96,2304]{1,0:T(8,128)(2,1)S(1)}, bf16[96,2304]{1,0:T(8,128)(2,1)S(1)}, u32[]{:S(2)}, u32[]{:S(2)}) collective-permute-start(bf16[96,2304]{1,0:T(8,128)(2,1)S(1)} %get-tuple-element.63), channel_id=1, source_target_pairs={{0,1},{1,0},{2,3},{3,2},{4,5},{5,4},{6,7},{7,6},{8,9},{9,8},{10,11... | collective-permute-start | bytes 1327112 | tf_op jit(solution)/shard_map/ppermute | solution.py:80
  189.2 22.7 %collective-permute-start.17 = (bf16[96,2304]{1,0:T(8,128)(2,1)S(1)}, bf16[96,2304]{1,0:T(8,128)(2,1)S(1)}, u32[]{:S(2)}, u32[]{:S(2)}) collective-permute-start(bf16[96,2304]{1,0:T(8,128)(2,1)S(1)} %get-tuple-element.64), channel_id=1, source_target_pairs={{0,17},{1,16},{2,19},{3,18},{4,21},{5,20},{6,23},{7,22},{8,25},{9,... | collective-permute-start | bytes 1327112 | tf_op jit(solution)/shard_map/ppermute | solution.py:80
  196.6 12.5 %collective-permute-start.22 = (bf16[96,896]{1,0:T(8,128)(2,1)S(1)}, bf16[96,896]{1,0:T(8,128)(2,1)S(1)}, u32[]{:S(2)}, u32[]{:S(2)}) collective-permute-start(bf16[96,896]{1,0:T(8,128)(2,1)S(1)} %get-tuple-element.72), channel_id=1, source_target_pairs={{0,4},{1,5},{2,6},{3,7},{4,0},{5,1},{6,2},{7,3},{8,12},{9,13},{10,... | collective-permute-start | bytes 516104 | tf_op jit(solution)/shard_map/ppermute | solution.py:80
  210.8 6.5 %collective-permute-start.23 = (bf16[48,896]{1,0:T(8,128)(2,1)S(1)}, bf16[48,896]{1,0:T(8,128)(2,1)S(1)}, u32[]{:S(2)}, u32[]{:S(2)}) collective-permute-start(bf16[48,896]{1,0:T(8,128)(2,1)S(1)} %get-tuple-element.77), channel_id=1, source_target_pairs={{0,1},{1,0},{2,3},{3,2},{4,5},{5,4},{6,7},{7,6},{8,9},{9,8},{10,11... | collective-permute-start | bytes 258056 | tf_op jit(solution)/shard_map/ppermute | solution.py:80
  212.9 14.4 %collective-permute-start.18 = (bf16[24,2304]{1,0:T(8,128)(2,1)S(1)}, bf16[24,2304]{1,0:T(8,128)(2,1)S(1)}, u32[]{:S(2)}, u32[]{:S(2)}) collective-permute-start(bf16[24,2304]{1,0:T(8,128)(2,1)S(1)} %get-tuple-element.66), channel_id=1, source_target_pairs={{0,4},{1,5},{2,6},{3,7},{4,0},{5,1},{6,2},{7,3},{8,12},{9,13},{10,... | collective-permute-start | bytes 331784 | tf_op jit(solution)/shard_map/ppermute | solution.py:80
  215.4 11.8 %collective-permute-start.19 = (bf16[24,2304]{1,0:T(8,128)(2,1)S(1)}, bf16[24,2304]{1,0:T(8,128)(2,1)S(1)}, u32[]{:S(2)}, u32[]{:S(2)}) collective-permute-start(bf16[24,2304]{1,0:T(8,128)(2,1)S(1)} %get-tuple-element.67), channel_id=1, source_target_pairs={{0,2},{1,3},{2,0},{3,1},{4,6},{5,7},{6,4},{7,5},{8,10},{9,11},{10,... | collective-permute-start | bytes 331784 | tf_op jit(solution)/shard_map/ppermute | solution.py:80
  215.7 11.5 %collective-permute-start.20 = (bf16[24,2304]{1,0:T(8,128)(2,1)S(1)}, bf16[24,2304]{1,0:T(8,128)(2,1)S(1)}, u32[]{:S(2)}, u32[]{:S(2)}) collective-permute-start(bf16[24,2304]{1,0:T(8,128)(2,1)S(1)} %get-tuple-element.68), channel_id=1, source_target_pairs={{0,6},{1,7},{2,4},{3,5},{4,2},{5,3},{6,0},{7,1},{8,14},{9,15},{10,... | collective-permute-start | bytes 331784 | tf_op jit(solution)/shard_map/ppermute | solution.py:80
  218.8 8.5 %collective-permute-start.24 = (bf16[24,896]{1,0:T(8,128)(2,1)S(1)}, bf16[24,896]{1,0:T(8,128)(2,1)S(1)}, u32[]{:S(2)}, u32[]{:S(2)}) collective-permute-start(bf16[24,896]{1,0:T(8,128)(2,1)S(1)} %get-tuple-element.79), channel_id=1, source_target_pairs={{0,16},{1,17},{2,18},{3,19},{4,20},{5,21},{6,22},{7,23},{8,24},{9,... | collective-permute-start | bytes 129032 | tf_op jit(solution)/shard_map/ppermute | solution.py:80
  (31 other events, 89.8 us)

commit v4 on v3

--- a/solution.py
+++ b/solution.py
@@ -138,9 +138,10 @@
     keep_ref[...], send_ref[...] = halves_of(sum_of((own, arrived)), rows)
 
 
-def halve(own, arrived, rows):
+def halve(own, arrived, rows, near):
     outs = [((own.shape[0] // 2, own.shape[1]), BF)] * 2
-    return kernel_call(functools.partial(halve_kernel, rows), outs, own.size, own, arrived)
+    body = functools.partial(halve_kernel, rows)
+    return kernel_call(body, outs, own.size, own, arrived, near=near)
 
 
 def begin_kernel(cut, rows, own, arrived, *refs):
@@ -171,18 +172,16 @@
     arrived = fan_sends(leads, xy)
     done = first(leads[0])
     for i, (mask, _) in enumerate(steps):
-        if i == len(z_bits()):
-            keep = after(keep, sums[0])
         come = swap(send, mask)
-        if i == 1:
-            come = after(come, *done)
         if i + 1 == len(steps):
             break
-        keep, send = halve(keep, come, steps[i + 1][1])
+        near = list(sums[:1]) if i == len(z_bits()) else []
+        near += list(done[-1:]) if i == 1 else []
+        keep, send = halve(keep, come, steps[i + 1][1], near)
         if i == 0:
             sums = sum_apart([leads[0], *arrived], len(z))
     later = second(sums[0])
-    return [sums[0], *fan_sends(sums, z)], [after(keep, *later), come], done, later
+    return [sums[0], *fan_sends(sums, z)], [keep, come], done, later
 
 
 def fan_sends(parts, masks):
@@ -228,7 +227,7 @@
         return self.ref[index]
 
 
-def kernel_call(body, outs, flops, *operands, fetch=(), push=(), scratch=16):
+def kernel_call(body, outs, flops, *operands, fetch=(), push=(), near=(), scratch=16):
     moved = sum(math.prod(v.shape) * v.dtype.itemsize for v in operands)
     moved += sum(math.prod(shape) * jnp.dtype(kind).itemsize for shape, kind in outs)
     taken = len(operands)
@@ -237,7 +236,10 @@
     ]
     push = list(push)
 
+    beside = len(near)
+
     def kernel(*refs):
+        refs = refs[:taken] + refs[taken + beside :]
         buffers, refs = refs[taken + len(outs) :], list(refs[: taken + len(outs)])
         arriving, leaving, sent = [], {}, []
         for i, (number, index, _) in enumerate(fetch):
@@ -273,12 +275,13 @@
     return pl.pallas_call(
         kernel,
         out_shape=[jax.ShapeDtypeStruct(shape, kind) for shape, kind in outs],
-        in_specs=[left if i in fetched else whole for i in range(taken)],
+        in_specs=[left if i in fetched else whole for i in range(taken)]
+        + [whole] * len(near),
         out_specs=[left if i in push else whole for i in range(len(outs))],
         scratch_shapes=buffers,
         compiler_params=pltpu.CompilerParams(vmem_limit_bytes=scratch * 1024 * 1024),
         cost_estimate=pl.CostEstimate(flops=0, bytes_accessed=0, transcendentals=0),
-    )(*operands)
+    )(*operands, *near)
 
 
 def pick_heads(first_head, second_head):
@@ -455,7 +458,8 @@
 
 
 def weight_grad_kernel(weights, down_late, kept, far, near, *refs):
-    others, (up_ref, down_ref) = refs[:-2], refs[-2:]
+    others, (up_ref, down_ref, mark_ref) = refs[:-3], refs[-3:]
+    mark_ref[...] = jnp.zeros(mark_ref.shape, F32)
     width, hidden = up_ref.shape
     count = near.shape[0]
     up, down = weights[:hidden], (weights[hidden:], down_late[...])
@@ -612,6 +616,7 @@
     far,
     place_of,
     token_ref,
+    mark_ref,
 ):
     width = tokens.shape[1]
     shuffle = shuffle_of(place_of)
@@ -627,6 +632,7 @@
     inverse = inverse_rms(inputs)
     unit = inputs * inverse
     input_grad = inverse * (scaled - unit * jnp.mean(unit * scaled, axis=-1, keepdims=True))
+    mark_ref[...] = jnp.zeros(mark_ref.shape, F32)
     token_ref[...] = (first_grad[...] + input_grad).astype(BF)
 
 
@@ -787,7 +793,7 @@
         *weights,
         *downs,
         fetch=range(4, 4 + 2 * chips),
-        scratch=56,
+        scratch=50,
     )
     others = [swap(shown, mask) for mask in chip_masks()[1:]]
     others = [both for part in others for both in (part, swap(part, core_mask()))]
@@ -824,38 +830,40 @@
             3,
             5,
         ),
-        scratch=56,
+        scratch=50,
     )
     def token_parts(begun):
         return kernel_call(
             functools.partial(token_kernel, experts),
-            [((count, width), BF)],
+            [((count, width), BF), ((8, LANES), F32)],
             2 * count * width * 6 * width,
             tokens,
             first_grad,
-            after(joint_grad, begun),
+            joint_grad,
             *halves,
             place_of[None],
             fetch=(3, 4, 0, 1, 2),
+            near=(begun,),
             scratch=56,
         )
 
     def weight_parts(begun):
         return kernel_call(
             weight_grad_kernel,
-            [((width, piece), F32), ((piece, width), F32)],
+            [((width, piece), F32), ((piece, width), F32), ((8, LANES), F32)],
             16 * rows_here * width * chips * piece,
             weights[0],
             down_own,
-            after(kept, begun),
+            kept,
             row_parts[1],
             row_parts[0],
             *others,
             fetch=range(5 + len(others)),
+            near=(begun,),
             scratch=56,
         )
 
-    leads, trails, (grad_up, grad_down), (token_grad,) = scatter_blocks(
+    leads, trails, (grad_up, grad_down, _), (token_grad, mark) = scatter_blocks(
         keep, send, weight_parts, token_parts
     )
     grad_in, sum_out, grad_router, grad_first_gain, grad_second_gain, table_total = kernel_call(
@@ -873,6 +881,7 @@
         first_gain[None],
         *leads,
         *trails,
+        near=(mark,),
     )
     return (
         mixed,

time: 230 us -> 226 us (0.983)
    unnamed x74 -> x76, local copies, waits for them, and re-layouts: 15.9 us -> 15.6 us
  transfers between devices with their start and end apart: 27 -> 27, of which waited for: 12 -> 12; matrix products, arithmetic and copies ran while one was open for 6% -> 5% of each run, Pallas kernels for 14% -> 14%
where the time goes in v4:
time: 226 us; the launch traced here: 225 us
  waiting for transfers between devices  78.8 us (35%)
  Pallas kernels  62.4 us (28%)
  starting transfers between devices  35.3 us (16%)
  blocking collectives  22.8 us (10%)
  local copies, waits for them, and re-layouts  18.4 us (8%)
  other arithmetic  4.04 us (2%)
    ppermute x25, waiting for transfers between devices, swap(): lax.ppermute(value, AXES, [(i, i ^ mask) for i in range(columns * experts)])  71.2 us
    pallas_call x13, Pallas kernels, kernel_call(): pl.pallas_call(kernel, out_shape=[jax.ShapeDtypeStruct(shape, kind) for s...  62.4 us
    ppermute x25, starting transfers between devices, swap(): lax.ppermute(value, AXES, [(i, i ^ mask) for i in range(columns * experts)])  25.9 us
    all_to_all x1, blocking collectives, exchange(): lax.all_to_all(blocks, 'expert', split_axis=0, concat_axis=0, tiled=True)  22.8 us
    unnamed x76, local copies, waits for them, and re-layouts  15.6 us
    all_to_all x2, starting transfers between devices, exchange(): lax.all_to_all(blocks, 'expert', split_axis=0, concat_axis=0, tiled=True)  9.36 us
    all_to_all x2, waiting for transfers between devices, exchange(): lax.all_to_all(blocks, 'expert', split_axis=0, concat_axis=0, tiled=True)  7.57 us
  transfers between devices with their start and end apart: 27, of which 12 were waited for; matrix products, arithmetic and copies ran while one was open for 5% of the time, Pallas kernels for 14%

profile of v4, /device:TPU:0, one launch (start us, length us, event | category | flops | bytes accessed | tf_op | source)
XLA Modules:
  0.0 224.8 jit_solution(17359593281915006750)
XLA Ops:
  0.7 2.0 shard_map.222
  2.6 5.1 %collective-permute-start.2 = (bf16[24,3200]{1,0:T(8,128)(2,1)}, bf16[24,3200]{1,0:T(8,128)(2,1)S(1)}, u32[]{:S(2)}, u32[]{:S(2)}) collective-permute-start(bf16[24,3200]{1,0:T(8,128)(2,1)} %get-tuple-element.51), channel_id=1, source_target_pairs={{0,6},{1,7},{2,4},{3,5},{4,2},{5,3},{6,0},{7,1},{8,14},{9,15},{10,... | collective-permute-start | bytes 460808 | tf_op jit(solution)/shard_map/ppermute | solution.py:80
  8.4 1.6 collective-permute-start.3
  11.2 1.6 copy.39
  14.4 2.0 collective-permute-done.1
  16.3 4.6 %collective-permute-done = bf16[24,3200]{1,0:T(8,128)(2,1)S(1)} collective-permute-done((bf16[24,3200]{1,0:T(8,128)(2,1)}, bf16[24,3200]{1,0:T(8,128)(2,1)S(1)}, u32[]{:S(2)}, u32[]{:S(2)}) %collective-permute-start) | collective-permute-done | bytes 153632 | tf_op jit(solution)/shard_map/ppermute | solution.py:80
  22.6 2.4 %collective-permute-start.6 = (bf16[96,3200]{1,0:T(8,128)(2,1)}, bf16[96,3200]{1,0:T(8,128)(2,1)S(1)}, u32[]{:S(2)}, u32[]{:S(2)}) collective-permute-start(bf16[96,3200]{1,0:T(8,128)(2,1)} %shard_map.223), channel_id=1, source_target_pairs={{0,17},{1,16},{2,19},{3,18},{4,21},{5,20},{6,23},{7,22},{8,25},{9,... | collective-permute-start | bytes 1843208 | tf_op jit(solution)/shard_map/ppermute | solution.py:80
  27.3 4.7 %all-to-all-start = ((bf16[8,48,768]{2,1,0:T(8,128)(2,1)}), bf16[8,48,768]{2,1,0:T(8,128)(2,1)S(1)}, u32[]{:S(2)}, u32[]{:S(2)}) async-start(bf16[8,48,768]{2,1,0:T(8,128)(2,1)} %bitcast.8), calls=%async_computation | async-start | bytes 1179648 | tf_op jit(solution)/shard_map/all_to_all | solution.py:194
  32.0 10.6 %collective-permute-done.6 = bf16[96,3200]{1,0:T(8,128)(2,1)S(1)} collective-permute-done((bf16[96,3200]{1,0:T(8,128)(2,1)}, bf16[96,3200]{1,0:T(8,128)(2,1)S(1)}, u32[]{:S(2)}, u32[]{:S(2)}) %collective-permute-start.6) | collective-permute-done | bytes 614432 | tf_op jit(solution)/shard_map/ppermute | solution.py:80
  42.6 14.0 %collective-permute-done.5 = bf16[96,3200]{1,0:T(8,128)(2,1)S(1)} collective-permute-done((bf16[96,3200]{1,0:T(8,128)(2,1)}, bf16[96,3200]{1,0:T(8,128)(2,1)S(1)}, u32[]{:S(2)}, u32[]{:S(2)}) %collective-permute-start.5) | collective-permute-done | bytes 614432 | tf_op jit(solution)/shard_map/ppermute | solution.py:80
  56.6 1.7 pad_maximum_fusion.refs_0_
  60.8 1.5 collective-permute-start.10
  65.8 10.7 %shard_map.225 = (bf16[128,4608]{1,0:T(8,128)(2,1)}, f32[128,2432]{1,0:T(8,128)}, bf16[384,896]{1,0:T(8,128)(2,1)}) custom-call(bf16[128,768]{1,0:T(8,128)(2,1)} %refs_0_.4, s32[1,768]{1,0:T(1,128)} %broadcast_in_dim.12.refs_1_.refs_4_.refs_5_, bf16[384,3200]{1,0:T(8,128)(2,1)} %shard_map.224.refs_2_.refs_1_.refs_7_.refs_3_, bf16[384,3200]{1,0:T(8,128)(2,1)} %copy-done.26, ...), custom_call_target="tpu_custom_call" | custom-call | tf_op jit(solution)/shard_map/pallas_call | solution.py:275
  76.5 22.8 %all_to_all.15 = bf16[8,48,896]{2,1,0:T(8,128)(2,1)S(1)} all-to-all(bf16[8,48,896]{2,1,0:T(8,128)(2,1)} %bitcast.40), channel_id=1, replica_groups=mesh['fsdp'=4,'expert'=8] {'expert'}, dimensions={0} | all-to-all | bytes 1376256 | tf_op jit(solution)/shard_map/all_to_all | solution.py:194
  99.8 2.5 %collective-permute-done.9.refs_2_ = bf16[384,768]{1,0:T(8,128)(2,1)S(1)} collective-permute-done((bf16[384,768]{1,0:T(8,128)(2,1)S(1)}, bf16[384,768]{1,0:T(8,128)(2,1)S(1)}, u32[]{:S(2)}, u32[]{:S(2)}) %collective-permute-start.9) | collective-permute-done | bytes 589856 | tf_op jit(solution)/shard_map/ppermute | solution.py:80
  102.3 3.4 %collective-permute-done.10.refs_5_ = bf16[1280,768]{1,0:T(8,128)(2,1)} collective-permute-done((bf16[1280,768]{1,0:T(8,128)(2,1)}, bf16[1280,768]{1,0:T(8,128)(2,1)}, u32[]{:S(2)}, u32[]{:S(2)}) %collective-permute-start.10) | collective-permute-done | bytes 1966112 | tf_op jit(solution)/shard_map/ppermute | solution.py:80
  105.7 13.5 %shard_map.227 = (bf16[384,1536]{1,0:T(8,128)(2,1)}, bf16[384,1536]{1,0:T(8,128)(2,1)}, bf16[768,2304]{1,0:T(8,128)(2,1)}, bf16[768,768]{1,0:T(8,128)(2,1)}) custom-call(bf16[384,896]{1,0:T(8,128)(2,1)S(1)} %collective-permute-done.8.refs_0_.refs_3_, bf16[384,896]{1,0:T(8,128)(2,1)S(1)} %bitcast.32, bf16[384,768]{1,0:T(8,128)(2,1)S(1)} %collective-permute-done.9.refs_2_, ...), custom_call_target="tpu_custom_call" | custom-call | tf_op jit(solution)/shard_map/pallas_call | solution.py:275
  119.3 1.6 collective-permute-start.12
  120.9 1.5 collective-permute-done.11.refs_1_
  124.9 4.7 %all-to-all-start.2 = ((bf16[8,48,1536]{2,1,0:T(8,128)(2,1)}), bf16[8,48,1536]{2,1,0:T(8,128)(2,1)S(1)}, u32[]{:S(2)}, u32[]{:S(2)}) async-start(bf16[8,48,1536]{2,1,0:T(8,128)(2,1)} %bitcast.14), calls=%async_computation.2 | async-start | bytes 2359296 | tf_op jit(solution)/shard_map/all_to_all | solution.py:194
  129.6 18.3 %collective-permute-done.12.refs_1_.refs_5_ = bf16[768,768]{1,0:T(8,128)(2,1)S(1)} collective-permute-done((bf16[768,768]{1,0:T(8,128)(2,1)}, bf16[768,768]{1,0:T(8,128)(2,1)S(1)}, u32[]{:S(2)}, u32[]{:S(2)}) %collective-permute-start.12) | collective-permute-done | bytes 1179680 | tf_op jit(solution)/shard_map/ppermute | solution.py:80
  148.2 2.8 %collective-permute-done.13.refs_2_.refs_6_ = bf16[768,768]{1,0:T(8,128)(2,1)} collective-permute-done((bf16[768,768]{1,0:T(8,128)(2,1)S(1)}, bf16[768,768]{1,0:T(8,128)(2,1)}, u32[]{:S(2)}, u32[]{:S(2)}) %collective-permute-start.13) | collective-permute-done | bytes 1179680 | tf_op jit(solution)/shard_map/ppermute | solution.py:80
  150.9 7.6 %all-to-all-done.2 = bf16[8,48,1536]{2,1,0:T(8,128)(2,1)S(1)} async-done(((bf16[8,48,1536]{2,1,0:T(8,128)(2,1)}), bf16[8,48,1536]{2,1,0:T(8,128)(2,1)S(1)}, u32[]{:S(2)}, u32[]{:S(2)}) %all-to-all-start.2) | async-done | bytes 1179680 | tf_op jit(solution)/shard_map/all_to_all | solution.py:194
  162.1 13.0 %shard_map.230 = (bf16[384,3200]{1,0:T(8,128)(2,1)}, bf16[384,3200]{1,0:T(8,128)(2,1)}, f32[128,768]{1,0:T(8,128)S(1)}, bf16[128,2304]{1,0:T(8,128)(2,1)S(1)}, f...) custom-call(bf16[384,1536]{1,0:T(8,128)(2,1)S(1)} %copy-done.2, s32[128,2]{1,0:T(8,128)S(1)} %copy-done.19, ...), custom_call_target="tpu_custom_call" | custom-call | tf_op jit(solution)/shard_map/pallas_call | solution.py:275
  175.2 4.9 %collective-permute-done.14.refs_1_ = bf16[384,3200]{1,0:T(8,128)(2,1)S(1)} collective-permute-done((bf16[384,3200]{1,0:T(8,128)(2,1)}, bf16[384,3200]{1,0:T(8,128)(2,1)S(1)}, u32[]{:S(2)}, u32[]{:S(2)}) %collective-permute-start.14) | collective-permute-done | bytes 2457632 | tf_op jit(solution)/shard_map/ppermute | solution.py:80
  180.1 1.7 copy-done.7
  186.6 6.6 %collective-permute-done.21.refs_1_ = bf16[192,896]{1,0:T(8,128)(2,1)S(1)} collective-permute-done((bf16[192,896]{1,0:T(8,128)(2,1)S(1)}, bf16[192,896]{1,0:T(8,128)(2,1)S(1)}, u32[]{:S(2)}, u32[]{:S(2)}) %collective-permute-start.21) | collective-permute-done | bytes 344096 | tf_op jit(solution)/shard_map/ppermute | solution.py:80
  194.1 12.8 %shard_map.235 = (f32[768,768]{1,0:T(8,128)}, f32[768,768]{1,0:T(8,128)}, f32[8,128]{1,0:T(8,128)}) custom-call(bf16[1280,768]{1,0:T(8,128)(2,1)} %shard_map.226.refs_4_.refs_0_, bf16[256,768]{1,0:T(8,128)(2,1)} %get-tuple-element.52.refs_6_.refs_1_, bf16[768,2304]{1,0:T(8,128)(2,1)} %get-tuple-element.77.refs_2_, bf16[384,896]{1,0:T(8,128)(2,1)} %copy-done.6, ...), custom_call_target="tpu_custom_call" | custom-call | tf_op jit(solution)/shard_map/pallas_call | solution.py:275
  209.0 2.7 %collective-permute-start.18 = (bf16[24,2304]{1,0:T(8,128)(2,1)S(1)}, bf16[24,2304]{1,0:T(8,128)(2,1)S(1)}, u32[]{:S(2)}, u32[]{:S(2)}) collective-permute-start(bf16[24,2304]{1,0:T(8,128)(2,1)S(1)} %get-tuple-element.70), channel_id=1, source_target_pairs={{0,4},{1,5},{2,6},{3,7},{4,0},{5,1},{6,2},{7,3},{8,12},{9,13},{10,... | collective-permute-start | bytes 331784 | tf_op jit(solution)/shard_map/ppermute | solution.py:80
  212.0 1.5 collective-permute-start.20
  213.5 1.5 collective-permute-start.24
  215.0 7.2 %shard_map.233 = (bf16[128,768]{1,0:T(8,128)(2,1)}, f32[8,128]{1,0:T(8,128)}) custom-call(bf16[128,768]{1,0:T(8,128)(2,1)} %refs_0_.4, f32[128,768]{1,0:T(8,128)} %copy-done.21, bf16[128,2304]{1,0:T(8,128)(2,1)} %copy-done.18, bf16[384,3200]{1,0:T(8,128)(2,1)} %shard_map.224.refs_2_.refs_1_.refs_7_.refs_3_, bf16[384,3200]{1,0:T(8,128)(2,1)} %copy-done.26, ...), custom_call_target="tpu_custom_call" | custom-call | tf_op jit(solution)/shard_map/pallas_call | solution.py:275
  (130 shorter events, 30.8 us)
Async XLA Ops:
  0.6 59.4 %copy-start = (f32[32,12]{0,1:T(8,128)S(1)}, f32[32,12]{0,1:T(8,128)}, u32[]{:S(2)}) copy-start(f32[32,12]{0,1:T(8,128)} %param.22) | copy-start | bytes 4612
  2.6 11.7 %collective-permute-start.2 = (bf16[24,3200]{1,0:T(8,128)(2,1)}, bf16[24,3200]{1,0:T(8,128)(2,1)S(1)}, u32[]{:S(2)}, u32[]{:S(2)}) collective-permute-start(bf16[24,3200]{1,0:T(8,128)(2,1)} %get-tuple-element.51), channel_id=1, source_target_pairs={{0,6},{1,7},{2,4},{3,5},{4,2},{5,3},{6,0},{7,1},{8,14},{9,15},{10,... | collective-permute-start | bytes 460808 | tf_op jit(solution)/shard_map/ppermute | solution.py:80
  7.7 8.6 %collective-permute-start.1 = (bf16[24,3200]{1,0:T(8,128)(2,1)}, bf16[24,3200]{1,0:T(8,128)(2,1)S(1)}, u32[]{:S(2)}, u32[]{:S(2)}) collective-permute-start(bf16[24,3200]{1,0:T(8,128)(2,1)} %get-tuple-element.51), channel_id=1, source_target_pairs={{0,2},{1,3},{2,0},{3,1},{4,6},{5,7},{6,4},{7,5},{8,10},{9,11},{10,... | collective-permute-start | bytes 460808 | tf_op jit(solution)/shard_map/ppermute | solution.py:80
  7.8 13.2 %collective-permute-start = (bf16[24,3200]{1,0:T(8,128)(2,1)}, bf16[24,3200]{1,0:T(8,128)(2,1)S(1)}, u32[]{:S(2)}, u32[]{:S(2)}) collective-permute-start(bf16[24,3200]{1,0:T(8,128)(2,1)} %get-tuple-element.51), channel_id=1, source_target_pairs={{0,4},{1,5},{2,6},{3,7},{4,0},{5,1},{6,2},{7,3},{8,12},{9,13},{10,... | collective-permute-start | bytes 460808 | tf_op jit(solution)/shard_map/ppermute | solution.py:80
  8.4 13.4 %collective-permute-start.3 = (bf16[256,768]{1,0:T(8,128)(2,1)}, bf16[256,768]{1,0:T(8,128)(2,1)S(1)}, u32[]{:S(2)}, u32[]{:S(2)}) collective-permute-start(bf16[256,768]{1,0:T(8,128)(2,1)} %get-tuple-element.52.refs_6_.refs_1_), channel_id=1, source_target_pairs={{0,16},{1,17},{2,18},{3,19},{4,20},{5,21},{6,22},{7,23},{8,24},{9,... | collective-permute-start | bytes 1179656 | tf_op jit(solution)/shard_map/ppermute | solution.py:80
  22.6 34.0 %copy-start.27 = (bf16[96,3200]{1,0:T(8,128)(2,1)S(1)}, bf16[96,3200]{1,0:T(8,128)(2,1)}, u32[]{:S(2)}) copy-start(bf16[96,3200]{1,0:T(8,128)(2,1)} %shard_map.223) | copy-start | bytes 1843204
  22.6 20.0 %collective-permute-start.6 = (bf16[96,3200]{1,0:T(8,128)(2,1)}, bf16[96,3200]{1,0:T(8,128)(2,1)S(1)}, u32[]{:S(2)}, u32[]{:S(2)}) collective-permute-start(bf16[96,3200]{1,0:T(8,128)(2,1)} %shard_map.223), channel_id=1, source_target_pairs={{0,17},{1,16},{2,19},{3,18},{4,21},{5,20},{6,23},{7,22},{8,25},{9,... | collective-permute-start | bytes 1843208 | tf_op jit(solution)/shard_map/ppermute | solution.py:80
  25.1 31.6 %collective-permute-start.5 = (bf16[96,3200]{1,0:T(8,128)(2,1)}, bf16[96,3200]{1,0:T(8,128)(2,1)S(1)}, u32[]{:S(2)}, u32[]{:S(2)}) collective-permute-start(bf16[96,3200]{1,0:T(8,128)(2,1)} %shard_map.223), channel_id=1, source_target_pairs={{0,1},{1,0},{2,3},{3,2},{4,5},{5,4},{6,7},{7,6},{8,9},{9,8},{10,11... | collective-permute-start | bytes 1843208 | tf_op jit(solution)/shard_map/ppermute | solution.py:80
  25.6 31.1 %collective-permute-start.4 = (bf16[96,3200]{1,0:T(8,128)(2,1)}, bf16[96,3200]{1,0:T(8,128)(2,1)S(1)}, u32[]{:S(2)}, u32[]{:S(2)}) collective-permute-start(bf16[96,3200]{1,0:T(8,128)(2,1)} %shard_map.223), channel_id=1, source_target_pairs={{0,16},{1,17},{2,18},{3,19},{4,20},{5,21},{6,22},{7,23},{8,24},{9,... | collective-permute-start | bytes 1843208 | tf_op jit(solution)/shard_map/ppermute | solution.py:80
  27.3 31.0 %all-to-all-start = ((bf16[8,48,768]{2,1,0:T(8,128)(2,1)}), bf16[8,48,768]{2,1,0:T(8,128)(2,1)S(1)}, u32[]{:S(2)}, u32[]{:S(2)}) async-start(bf16[8,48,768]{2,1,0:T(8,128)(2,1)} %bitcast.8), calls=%async_computation | async-start | bytes 1179648 | tf_op jit(solution)/shard_map/all_to_all | solution.py:194
  59.1 5.2 %collective-permute-start.7 = (bf16[384,3200]{1,0:T(8,128)(2,1)}, bf16[384,3200]{1,0:T(8,128)(2,1)S(1)}, u32[]{:S(2)}, u32[]{:S(2)}) collective-permute-start(bf16[384,3200]{1,0:T(8,128)(2,1)} %shard_map.224.refs_2_.refs_1_.refs_7_.refs_3_), channel_id=1, source_target_pairs={{0,8},{1,9},{2,10},{3,11},{4,12},{5,13},{6,14},{7,15},{8,0},{9,1},... | collective-permute-start | bytes 7372808 | tf_op jit(solution)/shard_map/ppermute | solution.py:80
  60.8 45.0 %collective-permute-start.10 = (bf16[1280,768]{1,0:T(8,128)(2,1)}, bf16[1280,768]{1,0:T(8,128)(2,1)}, u32[]{:S(2)}, u32[]{:S(2)}) collective-permute-start(bf16[1280,768]{1,0:T(8,128)(2,1)} %shard_map.226.refs_4_.refs_0_), channel_id=1, source_target_pairs={{0,16},{1,17},{2,18},{3,19},{4,20},{5,21},{6,22},{7,23},{8,24},{9,... | collective-permute-start | bytes 5898248 | tf_op jit(solution)/shard_map/ppermute | solution.py:80
  64.3 35.0 %copy-start.5 = (bf16[8,48,768]{2,1,0:T(8,128)(2,1)S(1)}, bf16[8,48,768]{2,1,0:T(8,128)(2,1)}, u32[]{:S(2)}) copy-start(bf16[8,48,768]{2,1,0:T(8,128)(2,1)} %copy-done.4) | copy-start | bytes 1769476
  64.3 41.4 %copy-start.10 = (bf16[256,768]{1,0:T(8,128)(2,1)S(1)}, bf16[256,768]{1,0:T(8,128)(2,1)}, u32[]{:S(2)}) copy-start(bf16[256,768]{1,0:T(8,128)(2,1)} %get-tuple-element.52.refs_6_.refs_1_) | copy-start | bytes 1179652
  64.3 41.4 %copy-start.12 = (bf16[256,768]{1,0:T(8,128)(2,1)S(1)}, bf16[256,768]{1,0:T(8,128)(2,1)}, u32[]{:S(2)}) copy-start(bf16[256,768]{1,0:T(8,128)(2,1)} %copy-done.11) | copy-start | bytes 1179652
  99.3 6.4 %collective-permute-start.8 = (bf16[384,896]{1,0:T(8,128)(2,1)S(1)}, bf16[384,896]{1,0:T(8,128)(2,1)S(1)}, u32[]{:S(2)}, u32[]{:S(2)}) collective-permute-start(bf16[384,896]{1,0:T(8,128)(2,1)S(1)} %bitcast.31), channel_id=1, source_target_pairs={{0,8},{1,9},{2,10},{3,11},{4,12},{5,13},{6,14},{7,15},{8,0},{9,1},... | collective-permute-start | bytes 2064392 | tf_op jit(solution)/shard_map/ppermute | solution.py:80
  99.3 3.0 %collective-permute-start.9 = (bf16[384,768]{1,0:T(8,128)(2,1)S(1)}, bf16[384,768]{1,0:T(8,128)(2,1)S(1)}, u32[]{:S(2)}, u32[]{:S(2)}) collective-permute-start(bf16[384,768]{1,0:T(8,128)(2,1)S(1)} %bitcast.35), channel_id=1, source_target_pairs={{0,8},{1,9},{2,10},{3,11},{4,12},{5,13},{6,14},{7,15},{8,0},{9,1},... | collective-permute-start | bytes 1769480 | tf_op jit(solution)/shard_map/ppermute | solution.py:80
  119.3 3.1 %collective-permute-start.11 = (bf16[384,1536]{1,0:T(8,128)(2,1)}, bf16[384,1536]{1,0:T(8,128)(2,1)S(1)}, u32[]{:S(2)}, u32[]{:S(2)}) collective-permute-start(bf16[384,1536]{1,0:T(8,128)(2,1)} %get-tuple-element.55), channel_id=1, source_target_pairs={{0,8},{1,9},{2,10},{3,11},{4,12},{5,13},{6,14},{7,15},{8,0},{9,1},... | collective-permute-start | bytes 3538952 | tf_op jit(solution)/shard_map/ppermute | solution.py:80
  119.3 28.6 %collective-permute-start.12 = (bf16[768,768]{1,0:T(8,128)(2,1)}, bf16[768,768]{1,0:T(8,128)(2,1)S(1)}, u32[]{:S(2)}, u32[]{:S(2)}) collective-permute-start(bf16[768,768]{1,0:T(8,128)(2,1)} %get-tuple-element.56), channel_id=1, source_target_pairs={{0,16},{1,17},{2,18},{3,19},{4,20},{5,21},{6,22},{7,23},{8,24},{9,... | collective-permute-start | bytes 3538952 | tf_op jit(solution)/shard_map/ppermute | solution.py:80
  124.9 33.5 %all-to-all-start.2 = ((bf16[8,48,1536]{2,1,0:T(8,128)(2,1)}), bf16[8,48,1536]{2,1,0:T(8,128)(2,1)S(1)}, u32[]{:S(2)}, u32[]{:S(2)}) async-start(bf16[8,48,1536]{2,1,0:T(8,128)(2,1)} %bitcast.14), calls=%async_computation.2 | async-start | bytes 2359296 | tf_op jit(solution)/shard_map/all_to_all | solution.py:194
  147.9 3.0 %collective-permute-start.13 = (bf16[768,768]{1,0:T(8,128)(2,1)S(1)}, bf16[768,768]{1,0:T(8,128)(2,1)}, u32[]{:S(2)}, u32[]{:S(2)}) collective-permute-start(bf16[768,768]{1,0:T(8,128)(2,1)S(1)} %collective-permute-done.12.refs_1_.refs_5_), channel_id=1, source_target_pairs={{0,8},{1,9},{2,10},{3,11},{4,12},{5,13},{6,14},{7,15},{8,0},{9,1},... | collective-permute-start | bytes 3538952 | tf_op jit(solution)/shard_map/ppermute | solution.py:80
  175.1 5.0 %collective-permute-start.14 = (bf16[384,3200]{1,0:T(8,128)(2,1)}, bf16[384,3200]{1,0:T(8,128)(2,1)S(1)}, u32[]{:S(2)}, u32[]{:S(2)}) collective-permute-start(bf16[384,3200]{1,0:T(8,128)(2,1)} %get-tuple-element.63), channel_id=1, source_target_pairs={{0,8},{1,9},{2,10},{3,11},{4,12},{5,13},{6,14},{7,15},{8,0},{9,1},... | collective-permute-start | bytes 7372808 | tf_op jit(solution)/shard_map/ppermute | solution.py:80
  183.1 10.1 %collective-permute-start.21 = (bf16[192,896]{1,0:T(8,128)(2,1)S(1)}, bf16[192,896]{1,0:T(8,128)(2,1)S(1)}, u32[]{:S(2)}, u32[]{:S(2)}) collective-permute-start(bf16[192,896]{1,0:T(8,128)(2,1)S(1)} %get-tuple-element.74), channel_id=1, source_target_pairs={{0,2},{1,3},{2,0},{3,1},{4,6},{5,7},{6,4},{7,5},{8,10},{9,11},{10,... | collective-permute-start | bytes 1032200 | tf_op jit(solution)/shard_map/ppermute | solution.py:80
  183.1 25.7 %collective-permute-start.15 = (bf16[96,2304]{1,0:T(8,128)(2,1)S(1)}, bf16[96,2304]{1,0:T(8,128)(2,1)S(1)}, u32[]{:S(2)}, u32[]{:S(2)}) collective-permute-start(bf16[96,2304]{1,0:T(8,128)(2,1)S(1)} %get-tuple-element.65), channel_id=1, source_target_pairs={{0,16},{1,17},{2,18},{3,19},{4,20},{5,21},{6,22},{7,23},{8,24},{9,... | collective-permute-start | bytes 1327112 | tf_op jit(solution)/shard_map/ppermute | solution.py:80
  184.5 24.2 %collective-permute-start.16 = (bf16[96,2304]{1,0:T(8,128)(2,1)S(1)}, bf16[96,2304]{1,0:T(8,128)(2,1)S(1)}, u32[]{:S(2)}, u32[]{:S(2)}) collective-permute-start(bf16[96,2304]{1,0:T(8,128)(2,1)S(1)} %get-tuple-element.66), channel_id=1, source_target_pairs={{0,1},{1,0},{2,3},{3,2},{4,5},{5,4},{6,7},{7,6},{8,9},{9,8},{10,11... | collective-permute-start | bytes 1327112 | tf_op jit(solution)/shard_map/ppermute | solution.py:80
  186.0 22.8 %collective-permute-start.17 = (bf16[96,2304]{1,0:T(8,128)(2,1)S(1)}, bf16[96,2304]{1,0:T(8,128)(2,1)S(1)}, u32[]{:S(2)}, u32[]{:S(2)}) collective-permute-start(bf16[96,2304]{1,0:T(8,128)(2,1)S(1)} %get-tuple-element.67), channel_id=1, source_target_pairs={{0,17},{1,16},{2,19},{3,18},{4,21},{5,20},{6,23},{7,22},{8,25},{9,... | collective-permute-start | bytes 1327112 | tf_op jit(solution)/shard_map/ppermute | solution.py:80
  193.3 13.6 %collective-permute-start.22 = (bf16[96,896]{1,0:T(8,128)(2,1)S(1)}, bf16[96,896]{1,0:T(8,128)(2,1)S(1)}, u32[]{:S(2)}, u32[]{:S(2)}) collective-permute-start(bf16[96,896]{1,0:T(8,128)(2,1)S(1)} %get-tuple-element.76), channel_id=1, source_target_pairs={{0,4},{1,5},{2,6},{3,7},{4,0},{5,1},{6,2},{7,3},{8,12},{9,13},{10,... | collective-permute-start | bytes 516104 | tf_op jit(solution)/shard_map/ppermute | solution.py:80
  207.6 5.9 %collective-permute-start.23 = (bf16[48,896]{1,0:T(8,128)(2,1)S(1)}, bf16[48,896]{1,0:T(8,128)(2,1)S(1)}, u32[]{:S(2)}, u32[]{:S(2)}) collective-permute-start(bf16[48,896]{1,0:T(8,128)(2,1)S(1)} %get-tuple-element.80), channel_id=1, source_target_pairs={{0,1},{1,0},{2,3},{3,2},{4,5},{5,4},{6,7},{7,6},{8,9},{9,8},{10,11... | collective-permute-start | bytes 258056 | tf_op jit(solution)/shard_map/ppermute | solution.py:80
  209.0 13.2 %collective-permute-start.18 = (bf16[24,2304]{1,0:T(8,128)(2,1)S(1)}, bf16[24,2304]{1,0:T(8,128)(2,1)S(1)}, u32[]{:S(2)}, u32[]{:S(2)}) collective-permute-start(bf16[24,2304]{1,0:T(8,128)(2,1)S(1)} %get-tuple-element.70), channel_id=1, source_target_pairs={{0,4},{1,5},{2,6},{3,7},{4,0},{5,1},{6,2},{7,3},{8,12},{9,13},{10,... | collective-permute-start | bytes 331784 | tf_op jit(solution)/shard_map/ppermute | solution.py:80
  211.7 10.5 %collective-permute-start.19 = (bf16[24,2304]{1,0:T(8,128)(2,1)S(1)}, bf16[24,2304]{1,0:T(8,128)(2,1)S(1)}, u32[]{:S(2)}, u32[]{:S(2)}) collective-permute-start(bf16[24,2304]{1,0:T(8,128)(2,1)S(1)} %get-tuple-element.71), channel_id=1, source_target_pairs={{0,2},{1,3},{2,0},{3,1},{4,6},{5,7},{6,4},{7,5},{8,10},{9,11},{10,... | collective-permute-start | bytes 331784 | tf_op jit(solution)/shard_map/ppermute | solution.py:80
  212.0 10.3 %collective-permute-start.20 = (bf16[24,2304]{1,0:T(8,128)(2,1)S(1)}, bf16[24,2304]{1,0:T(8,128)(2,1)S(1)}, u32[]{:S(2)}, u32[]{:S(2)}) collective-permute-start(bf16[24,2304]{1,0:T(8,128)(2,1)S(1)} %get-tuple-element.72), channel_id=1, source_target_pairs={{0,6},{1,7},{2,4},{3,5},{4,2},{5,3},{6,0},{7,1},{8,14},{9,15},{10,... | collective-permute-start | bytes 331784 | tf_op jit(solution)/shard_map/ppermute | solution.py:80
  213.5 8.7 %collective-permute-start.24 = (bf16[24,896]{1,0:T(8,128)(2,1)S(1)}, bf16[24,896]{1,0:T(8,128)(2,1)S(1)}, u32[]{:S(2)}, u32[]{:S(2)}) collective-permute-start(bf16[24,896]{1,0:T(8,128)(2,1)S(1)} %get-tuple-element.82), channel_id=1, source_target_pairs={{0,16},{1,17},{2,18},{3,19},{4,20},{5,21},{6,22},{7,23},{8,24},{9,... | collective-permute-start | bytes 129032 | tf_op jit(solution)/shard_map/ppermute | solution.py:80
  (32 other events, 159.6 us)

commit v5 on v4

--- a/solution.py
+++ b/solution.py
@@ -721,7 +721,7 @@
 
     lanes = small_lanes(experts)
     hidden = expert_down.shape[1]
-    late = hidden - hidden // 3
+    late = hidden - hidden // 2 // LANES * LANES
     packed, down_own = kernel_call(
         pack_kernel,
         [((share, lanes + 4 * width), BF), ((hidden - late, width), BF)],

time: 226 us -> 245 us (1.084)
  waiting for transfers between devices: 78.8 us -> 113 us
  blocking collectives: 22.8 us -> 0 us
  starting transfers between devices: 35.3 us -> 43 us
    all_to_all x1 -> x0, blocking collectives: 22.8 us -> none  [exchange(): lax.all_to_all(blocks, 'expert', split_axis=0, concat_axis=0, tiled=True)]
    all_to_all x2 -> x3, waiting for transfers between devices: 7.57 us -> 25.5 us  [exchange(): lax.all_to_all(blocks, 'expert', split_axis=0, concat_axis=0, tiled=True)]
    ppermute x25, waiting for transfers between devices: 71.2 us -> 87.5 us  [swap(): lax.ppermute(value, AXES, [(i, i ^ mask) for i in range(columns * experts)])]
    all_to_all x2 -> x3, starting transfers between devices: 9.36 us -> 17 us  [exchange(): lax.all_to_all(blocks, 'expert', split_axis=0, concat_axis=0, tiled=True)]
  transfers between devices with their start and end apart: 27 -> 28, of which waited for: 12 -> 15; matrix products, arithmetic and copies ran while one was open for 5% -> 5% of each run, Pallas kernels for 14% -> 9%
where the time goes in v5:
time: 245 us
  waiting for transfers between devices  113 us (46%)
  Pallas kernels  63.8 us (26%)
  starting transfers between devices  43 us (18%)
  local copies, waits for them, and re-layouts  17.8 us (7%)
  other arithmetic  3.99 us (2%)
    ppermute x25, waiting for transfers between devices, swap(): lax.ppermute(value, AXES, [(i, i ^ mask) for i in range(columns * experts)])  87.5 us
    pallas_call x13, Pallas kernels, kernel_call(): pl.pallas_call(kernel, out_shape=[jax.ShapeDtypeStruct(shape, kind) for s...  63.8 us
    ppermute x25, starting transfers between devices, swap(): lax.ppermute(value, AXES, [(i, i ^ mask) for i in range(columns * experts)])  26 us
    all_to_all x3, waiting for transfers between devices, exchange(): lax.all_to_all(blocks, 'expert', split_axis=0, concat_axis=0, tiled=True)  25.5 us
    all_to_all x3, starting transfers between devices, exchange(): lax.all_to_all(blocks, 'expert', split_axis=0, concat_axis=0, tiled=True)  17 us
    unnamed x76, local copies, waits for them, and re-layouts  15.1 us
  transfers between devices with their start and end apart: 28, of which 15 were waited for; matrix products, arithmetic and copies ran while one was open for 5% of the time, Pallas kernels for 9%

profile of v5, /device:TPU:0, one launch (start us, length us, event | category | flops | bytes accessed | tf_op | source)
XLA Modules:
  0.0 244.7 jit_solution(18180270963120800749)
XLA Ops:
  0.7 2.1 shard_map.222
  2.8 5.1 %collective-permute-start.2 = (bf16[24,3200]{1,0:T(8,128)(2,1)}, bf16[24,3200]{1,0:T(8,128)(2,1)S(1)}, u32[]{:S(2)}, u32[]{:S(2)}) collective-permute-start(bf16[24,3200]{1,0:T(8,128)(2,1)} %get-tuple-element.51), channel_id=1, source_target_pairs={{0,6},{1,7},{2,4},{3,5},{4,2},{5,3},{6,0},{7,1},{8,14},{9,15},{10,... | collective-permute-start | bytes 460808 | tf_op jit(solution)/shard_map/ppermute | solution.py:80
  8.5 1.6 collective-permute-start.3
  11.3 1.6 copy.39
  14.4 2.1 collective-permute-done.1
  16.5 4.6 %collective-permute-done = bf16[24,3200]{1,0:T(8,128)(2,1)S(1)} collective-permute-done((bf16[24,3200]{1,0:T(8,128)(2,1)}, bf16[24,3200]{1,0:T(8,128)(2,1)S(1)}, u32[]{:S(2)}, u32[]{:S(2)}) %collective-permute-start) | collective-permute-done | bytes 153632 | tf_op jit(solution)/shard_map/ppermute | solution.py:80
  24.1 2.4 collective-permute-start.6
  28.7 5.7 %all-to-all-start = ((bf16[8,48,768]{2,1,0:T(8,128)(2,1)}), bf16[8,48,768]{2,1,0:T(8,128)(2,1)S(1)}, u32[]{:S(2)}, u32[]{:S(2)}) async-start(bf16[8,48,768]{2,1,0:T(8,128)(2,1)} %bitcast.8), calls=%async_computation | async-start | bytes 1179648 | tf_op jit(solution)/shard_map/all_to_all | solution.py:194
  34.4 8.3 %collective-permute-done.6 = bf16[96,3200]{1,0:T(8,128)(2,1)S(1)} collective-permute-done((bf16[96,3200]{1,0:T(8,128)(2,1)}, bf16[96,3200]{1,0:T(8,128)(2,1)S(1)}, u32[]{:S(2)}, u32[]{:S(2)}) %collective-permute-start.6) | collective-permute-done | bytes 614432 | tf_op jit(solution)/shard_map/ppermute | solution.py:80
  42.7 14.6 %collective-permute-done.5 = bf16[96,3200]{1,0:T(8,128)(2,1)S(1)} collective-permute-done((bf16[96,3200]{1,0:T(8,128)(2,1)}, bf16[96,3200]{1,0:T(8,128)(2,1)S(1)}, u32[]{:S(2)}, u32[]{:S(2)}) %collective-permute-start.5) | collective-permute-done | bytes 614432 | tf_op jit(solution)/shard_map/ppermute | solution.py:80
  57.3 1.7 pad_maximum_fusion.refs_0_
  62.9 1.8 collective-permute-done.7.refs_3_.refs_8_.refs_4_
  66.2 10.8 %shard_map.225 = (bf16[128,4608]{1,0:T(8,128)(2,1)}, f32[128,2432]{1,0:T(8,128)}, bf16[384,896]{1,0:T(8,128)(2,1)}) custom-call(bf16[128,768]{1,0:T(8,128)(2,1)} %refs_0_.4, s32[1,768]{1,0:T(1,128)} %broadcast_in_dim.12.refs_1_.refs_4_.refs_5_, bf16[384,3200]{1,0:T(8,128)(2,1)} %shard_map.224.refs_2_.refs_1_.refs_7_.refs_3_, bf16[384,3200]{1,0:T(8,128)(2,1)} %copy-done.26, ...), custom_call_target="tpu_custom_call" | custom-call | tf_op jit(solution)/shard_map/pallas_call | solution.py:275
  76.9 5.4 %all-to-all-start.1 = ((bf16[8,48,896]{2,1,0:T(8,128)(2,1)}), bf16[8,48,896]{2,1,0:T(8,128)(2,1)S(1)}, u32[]{:S(2)}, u32[]{:S(2)}) async-start(bf16[8,48,896]{2,1,0:T(8,128)(2,1)} %bitcast.40), calls=%async_computation.1 | async-start | bytes 1376256 | tf_op jit(solution)/shard_map/all_to_all | solution.py:194
  82.4 1.5 collective-permute-start.10
  84.0 16.7 %all-to-all-done.1 = bf16[8,48,896]{2,1,0:T(8,128)(2,1)S(1)} async-done(((bf16[8,48,896]{2,1,0:T(8,128)(2,1)}), bf16[8,48,896]{2,1,0:T(8,128)(2,1)S(1)}, u32[]{:S(2)}, u32[]{:S(2)}) %all-to-all-start.1) | async-done | bytes 688160 | tf_op jit(solution)/shard_map/all_to_all | solution.py:194
  101.2 2.5 %collective-permute-done.9.refs_2_ = bf16[384,768]{1,0:T(8,128)(2,1)S(1)} collective-permute-done((bf16[384,768]{1,0:T(8,128)(2,1)S(1)}, bf16[384,768]{1,0:T(8,128)(2,1)S(1)}, u32[]{:S(2)}, u32[]{:S(2)}) %collective-permute-start.9) | collective-permute-done | bytes 589856 | tf_op jit(solution)/shard_map/ppermute | solution.py:80
  103.7 19.5 %collective-permute-done.10.refs_5_ = bf16[1152,768]{1,0:T(8,128)(2,1)} collective-permute-done((bf16[1152,768]{1,0:T(8,128)(2,1)}, bf16[1152,768]{1,0:T(8,128)(2,1)}, u32[]{:S(2)}, u32[]{:S(2)}) %collective-permute-start.10) | collective-permute-done | bytes 1769504 | tf_op jit(solution)/shard_map/ppermute | solution.py:80
  123.2 14.3 %shard_map.227 = (bf16[384,1536]{1,0:T(8,128)(2,1)}, bf16[384,1536]{1,0:T(8,128)(2,1)}, bf16[768,2304]{1,0:T(8,128)(2,1)}, bf16[768,768]{1,0:T(8,128)(2,1)}) custom-call(bf16[384,896]{1,0:T(8,128)(2,1)S(1)} %collective-permute-done.8.refs_0_.refs_3_, bf16[384,896]{1,0:T(8,128)(2,1)S(1)} %bitcast.32, bf16[384,768]{1,0:T(8,128)(2,1)S(1)} %collective-permute-done.9.refs_2_, ...), custom_call_target="tpu_custom_call" | custom-call | tf_op jit(solution)/shard_map/pallas_call | solution.py:275
  137.6 1.6 collective-permute-start.12
  143.2 5.8 %all-to-all-start.2 = ((bf16[8,48,1536]{2,1,0:T(8,128)(2,1)}), bf16[8,48,1536]{2,1,0:T(8,128)(2,1)S(1)}, u32[]{:S(2)}, u32[]{:S(2)}) async-start(bf16[8,48,1536]{2,1,0:T(8,128)(2,1)} %bitcast.14), calls=%async_computation.2 | async-start | bytes 2359296 | tf_op jit(solution)/shard_map/all_to_all | solution.py:194
  149.1 17.1 %collective-permute-done.12.refs_1_.refs_5_ = bf16[768,768]{1,0:T(8,128)(2,1)S(1)} collective-permute-done((bf16[768,768]{1,0:T(8,128)(2,1)}, bf16[768,768]{1,0:T(8,128)(2,1)S(1)}, u32[]{:S(2)}, u32[]{:S(2)}) %collective-permute-start.12) | collective-permute-done | bytes 1179680 | tf_op jit(solution)/shard_map/ppermute | solution.py:80
  166.4 2.8 %collective-permute-done.13.refs_2_.refs_6_ = bf16[768,768]{1,0:T(8,128)(2,1)} collective-permute-done((bf16[768,768]{1,0:T(8,128)(2,1)S(1)}, bf16[768,768]{1,0:T(8,128)(2,1)}, u32[]{:S(2)}, u32[]{:S(2)}) %collective-permute-start.13) | collective-permute-done | bytes 1179680 | tf_op jit(solution)/shard_map/ppermute | solution.py:80
  169.2 8.8 %all-to-all-done.2 = bf16[8,48,1536]{2,1,0:T(8,128)(2,1)S(1)} async-done(((bf16[8,48,1536]{2,1,0:T(8,128)(2,1)}), bf16[8,48,1536]{2,1,0:T(8,128)(2,1)S(1)}, u32[]{:S(2)}, u32[]{:S(2)}) %all-to-all-start.2) | async-done | bytes 1179680 | tf_op jit(solution)/shard_map/all_to_all | solution.py:194
  181.5 13.0 %shard_map.230 = (bf16[384,3200]{1,0:T(8,128)(2,1)}, bf16[384,3200]{1,0:T(8,128)(2,1)}, f32[128,768]{1,0:T(8,128)S(1)}, bf16[128,2304]{1,0:T(8,128)(2,1)S(1)}, f...) custom-call(bf16[384,1536]{1,0:T(8,128)(2,1)S(1)} %copy-done.2, s32[128,2]{1,0:T(8,128)S(1)} %copy-done.19, ...), custom_call_target="tpu_custom_call" | custom-call | tf_op jit(solution)/shard_map/pallas_call | solution.py:275
  194.7 4.9 %collective-permute-done.14.refs_1_ = bf16[384,3200]{1,0:T(8,128)(2,1)S(1)} collective-permute-done((bf16[384,3200]{1,0:T(8,128)(2,1)}, bf16[384,3200]{1,0:T(8,128)(2,1)S(1)}, u32[]{:S(2)}, u32[]{:S(2)}) %collective-permute-start.14) | collective-permute-done | bytes 2457632 | tf_op jit(solution)/shard_map/ppermute | solution.py:80
  199.5 1.7 copy-done.7
  206.1 6.6 %collective-permute-done.21.refs_1_ = bf16[192,896]{1,0:T(8,128)(2,1)S(1)} collective-permute-done((bf16[192,896]{1,0:T(8,128)(2,1)S(1)}, bf16[192,896]{1,0:T(8,128)(2,1)S(1)}, u32[]{:S(2)}, u32[]{:S(2)}) %collective-permute-start.21) | collective-permute-done | bytes 344096 | tf_op jit(solution)/shard_map/ppermute | solution.py:80
  213.5 13.2 %shard_map.235 = (f32[768,768]{1,0:T(8,128)}, f32[768,768]{1,0:T(8,128)}, f32[8,128]{1,0:T(8,128)}) custom-call(bf16[1152,768]{1,0:T(8,128)(2,1)} %shard_map.226.refs_4_.refs_0_, bf16[384,768]{1,0:T(8,128)(2,1)} %get-tuple-element.52.refs_6_.refs_1_, bf16[768,2304]{1,0:T(8,128)(2,1)} %get-tuple-element.77.refs_2_, bf16[384,896]{1,0:T(8,128)(2,1)} %copy-done.6, ...), custom_call_target="tpu_custom_call" | custom-call | tf_op jit(solution)/shard_map/pallas_call | solution.py:275
  228.9 2.6 %collective-permute-start.18 = (bf16[24,2304]{1,0:T(8,128)(2,1)S(1)}, bf16[24,2304]{1,0:T(8,128)(2,1)S(1)}, u32[]{:S(2)}, u32[]{:S(2)}) collective-permute-start(bf16[24,2304]{1,0:T(8,128)(2,1)S(1)} %get-tuple-element.70), channel_id=1, source_target_pairs={{0,4},{1,5},{2,6},{3,7},{4,0},{5,1},{6,2},{7,3},{8,12},{9,13},{10,... | collective-permute-start | bytes 331784 | tf_op jit(solution)/shard_map/ppermute | solution.py:80
  233.4 1.6 collective-permute-start.24
  234.9 7.2 %shard_map.233 = (bf16[128,768]{1,0:T(8,128)(2,1)}, f32[8,128]{1,0:T(8,128)}) custom-call(bf16[128,768]{1,0:T(8,128)(2,1)} %refs_0_.4, f32[128,768]{1,0:T(8,128)} %copy-done.21, bf16[128,2304]{1,0:T(8,128)(2,1)} %copy-done.18, bf16[384,3200]{1,0:T(8,128)(2,1)} %shard_map.224.refs_2_.refs_1_.refs_7_.refs_3_, bf16[384,3200]{1,0:T(8,128)(2,1)} %copy-done.26, ...), custom_call_target="tpu_custom_call" | custom-call | tf_op jit(solution)/shard_map/pallas_call | solution.py:275
  (131 shorter events, 34.5 us)
Async XLA Ops:
  0.6 61.5 %copy-start = (f32[32,12]{0,1:T(8,128)S(1)}, f32[32,12]{0,1:T(8,128)}, u32[]{:S(2)}) copy-start(f32[32,12]{0,1:T(8,128)} %param.22) | copy-start | bytes 4612
  2.8 11.6 %collective-permute-start.2 = (bf16[24,3200]{1,0:T(8,128)(2,1)}, bf16[24,3200]{1,0:T(8,128)(2,1)S(1)}, u32[]{:S(2)}, u32[]{:S(2)}) collective-permute-start(bf16[24,3200]{1,0:T(8,128)(2,1)} %get-tuple-element.51), channel_id=1, source_target_pairs={{0,6},{1,7},{2,4},{3,5},{4,2},{5,3},{6,0},{7,1},{8,14},{9,15},{10,... | collective-permute-start | bytes 460808 | tf_op jit(solution)/shard_map/ppermute | solution.py:80
  7.9 8.6 %collective-permute-start.1 = (bf16[24,3200]{1,0:T(8,128)(2,1)}, bf16[24,3200]{1,0:T(8,128)(2,1)S(1)}, u32[]{:S(2)}, u32[]{:S(2)}) collective-permute-start(bf16[24,3200]{1,0:T(8,128)(2,1)} %get-tuple-element.51), channel_id=1, source_target_pairs={{0,2},{1,3},{2,0},{3,1},{4,6},{5,7},{6,4},{7,5},{8,10},{9,11},{10,... | collective-permute-start | bytes 460808 | tf_op jit(solution)/shard_map/ppermute | solution.py:80
  7.9 13.2 %collective-permute-start = (bf16[24,3200]{1,0:T(8,128)(2,1)}, bf16[24,3200]{1,0:T(8,128)(2,1)S(1)}, u32[]{:S(2)}, u32[]{:S(2)}) collective-permute-start(bf16[24,3200]{1,0:T(8,128)(2,1)} %get-tuple-element.51), channel_id=1, source_target_pairs={{0,4},{1,5},{2,6},{3,7},{4,0},{5,1},{6,2},{7,3},{8,12},{9,13},{10,... | collective-permute-start | bytes 460808 | tf_op jit(solution)/shard_map/ppermute | solution.py:80
  8.5 14.7 %collective-permute-start.3 = (bf16[384,768]{1,0:T(8,128)(2,1)}, bf16[384,768]{1,0:T(8,128)(2,1)S(1)}, u32[]{:S(2)}, u32[]{:S(2)}) collective-permute-start(bf16[384,768]{1,0:T(8,128)(2,1)} %get-tuple-element.52.refs_6_.refs_1_), channel_id=1, source_target_pairs={{0,16},{1,17},{2,18},{3,19},{4,20},{5,21},{6,22},{7,23},{8,24},{9,... | collective-permute-start | bytes 1769480 | tf_op jit(solution)/shard_map/ppermute | solution.py:80
  24.1 18.6 %collective-permute-start.6 = (bf16[96,3200]{1,0:T(8,128)(2,1)}, bf16[96,3200]{1,0:T(8,128)(2,1)S(1)}, u32[]{:S(2)}, u32[]{:S(2)}) collective-permute-start(bf16[96,3200]{1,0:T(8,128)(2,1)} %shard_map.223), channel_id=1, source_target_pairs={{0,17},{1,16},{2,19},{3,18},{4,21},{5,20},{6,23},{7,22},{8,25},{9,... | collective-permute-start | bytes 1843208 | tf_op jit(solution)/shard_map/ppermute | solution.py:80
  26.5 30.8 %collective-permute-start.5 = (bf16[96,3200]{1,0:T(8,128)(2,1)}, bf16[96,3200]{1,0:T(8,128)(2,1)S(1)}, u32[]{:S(2)}, u32[]{:S(2)}) collective-permute-start(bf16[96,3200]{1,0:T(8,128)(2,1)} %shard_map.223), channel_id=1, source_target_pairs={{0,1},{1,0},{2,3},{3,2},{4,5},{5,4},{6,7},{7,6},{8,9},{9,8},{10,11... | collective-permute-start | bytes 1843208 | tf_op jit(solution)/shard_map/ppermute | solution.py:80
  27.0 30.3 %collective-permute-start.4 = (bf16[96,3200]{1,0:T(8,128)(2,1)}, bf16[96,3200]{1,0:T(8,128)(2,1)S(1)}, u32[]{:S(2)}, u32[]{:S(2)}) collective-permute-start(bf16[96,3200]{1,0:T(8,128)(2,1)} %shard_map.223), channel_id=1, source_target_pairs={{0,16},{1,17},{2,18},{3,19},{4,20},{5,21},{6,22},{7,23},{8,24},{9,... | collective-permute-start | bytes 1843208 | tf_op jit(solution)/shard_map/ppermute | solution.py:80
  28.7 30.2 %all-to-all-start = ((bf16[8,48,768]{2,1,0:T(8,128)(2,1)}), bf16[8,48,768]{2,1,0:T(8,128)(2,1)S(1)}, u32[]{:S(2)}, u32[]{:S(2)}) async-start(bf16[8,48,768]{2,1,0:T(8,128)(2,1)} %bitcast.8), calls=%async_computation | async-start | bytes 1179648 | tf_op jit(solution)/shard_map/all_to_all | solution.py:194
  59.8 4.9 %collective-permute-start.7 = (bf16[384,3200]{1,0:T(8,128)(2,1)}, bf16[384,3200]{1,0:T(8,128)(2,1)S(1)}, u32[]{:S(2)}, u32[]{:S(2)}) collective-permute-start(bf16[384,3200]{1,0:T(8,128)(2,1)} %shard_map.224.refs_2_.refs_1_.refs_7_.refs_3_), channel_id=1, source_target_pairs={{0,8},{1,9},{2,10},{3,11},{4,12},{5,13},{6,14},{7,15},{8,0},{9,1},... | collective-permute-start | bytes 7372808 | tf_op jit(solution)/shard_map/ppermute | solution.py:80
  76.9 23.7 %all-to-all-start.1 = ((bf16[8,48,896]{2,1,0:T(8,128)(2,1)}), bf16[8,48,896]{2,1,0:T(8,128)(2,1)S(1)}, u32[]{:S(2)}, u32[]{:S(2)}) async-start(bf16[8,48,896]{2,1,0:T(8,128)(2,1)} %bitcast.40), calls=%async_computation.1 | async-start | bytes 1376256 | tf_op jit(solution)/shard_map/all_to_all | solution.py:194
  82.4 40.8 %copy-start.8 = (bf16[384,768]{1,0:T(8,128)(2,1)S(1)}, bf16[384,768]{1,0:T(8,128)(2,1)}, u32[]{:S(2)}) copy-start(bf16[384,768]{1,0:T(8,128)(2,1)} %get-tuple-element.52.refs_6_.refs_1_) | copy-start | bytes 1769476
  82.4 40.8 %copy-start.10 = (bf16[384,768]{1,0:T(8,128)(2,1)S(1)}, bf16[384,768]{1,0:T(8,128)(2,1)}, u32[]{:S(2)}) copy-start(bf16[384,768]{1,0:T(8,128)(2,1)} %copy-done.9) | copy-start | bytes 1769476
  82.4 40.7 %collective-permute-start.10 = (bf16[1152,768]{1,0:T(8,128)(2,1)}, bf16[1152,768]{1,0:T(8,128)(2,1)}, u32[]{:S(2)}, u32[]{:S(2)}) collective-permute-start(bf16[1152,768]{1,0:T(8,128)(2,1)} %shard_map.226.refs_4_.refs_0_), channel_id=1, source_target_pairs={{0,16},{1,17},{2,18},{3,19},{4,20},{5,21},{6,22},{7,23},{8,24},{9,... | collective-permute-start | bytes 5308424 | tf_op jit(solution)/shard_map/ppermute | solution.py:80
  100.7 36.8 %copy-start.3 = (bf16[8,48,896]{2,1,0:T(8,128)(2,1)}, bf16[8,48,896]{2,1,0:T(8,128)(2,1)S(1)}, u32[]{:S(2)}) copy-start(bf16[8,48,896]{2,1,0:T(8,128)(2,1)S(1)} %all-to-all-done.1) | copy-start | bytes 2064388
  100.7 22.5 %collective-permute-start.8 = (bf16[384,896]{1,0:T(8,128)(2,1)S(1)}, bf16[384,896]{1,0:T(8,128)(2,1)S(1)}, u32[]{:S(2)}, u32[]{:S(2)}) collective-permute-start(bf16[384,896]{1,0:T(8,128)(2,1)S(1)} %bitcast.31), channel_id=1, source_target_pairs={{0,8},{1,9},{2,10},{3,11},{4,12},{5,13},{6,14},{7,15},{8,0},{9,1},... | collective-permute-start | bytes 2064392 | tf_op jit(solution)/shard_map/ppermute | solution.py:80
  100.7 3.0 %collective-permute-start.9 = (bf16[384,768]{1,0:T(8,128)(2,1)S(1)}, bf16[384,768]{1,0:T(8,128)(2,1)S(1)}, u32[]{:S(2)}, u32[]{:S(2)}) collective-permute-start(bf16[384,768]{1,0:T(8,128)(2,1)S(1)} %bitcast.35), channel_id=1, source_target_pairs={{0,8},{1,9},{2,10},{3,11},{4,12},{5,13},{6,14},{7,15},{8,0},{9,1},... | collective-permute-start | bytes 1769480 | tf_op jit(solution)/shard_map/ppermute | solution.py:80
  137.5 3.1 %collective-permute-start.11 = (bf16[384,1536]{1,0:T(8,128)(2,1)}, bf16[384,1536]{1,0:T(8,128)(2,1)S(1)}, u32[]{:S(2)}, u32[]{:S(2)}) collective-permute-start(bf16[384,1536]{1,0:T(8,128)(2,1)} %get-tuple-element.55), channel_id=1, source_target_pairs={{0,8},{1,9},{2,10},{3,11},{4,12},{5,13},{6,14},{7,15},{8,0},{9,1},... | collective-permute-start | bytes 3538952 | tf_op jit(solution)/shard_map/ppermute | solution.py:80
  137.6 28.6 %collective-permute-start.12 = (bf16[768,768]{1,0:T(8,128)(2,1)}, bf16[768,768]{1,0:T(8,128)(2,1)S(1)}, u32[]{:S(2)}, u32[]{:S(2)}) collective-permute-start(bf16[768,768]{1,0:T(8,128)(2,1)} %get-tuple-element.56), channel_id=1, source_target_pairs={{0,16},{1,17},{2,18},{3,19},{4,20},{5,21},{6,22},{7,23},{8,24},{9,... | collective-permute-start | bytes 3538952 | tf_op jit(solution)/shard_map/ppermute | solution.py:80
  143.2 34.7 %all-to-all-start.2 = ((bf16[8,48,1536]{2,1,0:T(8,128)(2,1)}), bf16[8,48,1536]{2,1,0:T(8,128)(2,1)S(1)}, u32[]{:S(2)}, u32[]{:S(2)}) async-start(bf16[8,48,1536]{2,1,0:T(8,128)(2,1)} %bitcast.14), calls=%async_computation.2 | async-start | bytes 2359296 | tf_op jit(solution)/shard_map/all_to_all | solution.py:194
  166.2 3.0 %collective-permute-start.13 = (bf16[768,768]{1,0:T(8,128)(2,1)S(1)}, bf16[768,768]{1,0:T(8,128)(2,1)}, u32[]{:S(2)}, u32[]{:S(2)}) collective-permute-start(bf16[768,768]{1,0:T(8,128)(2,1)S(1)} %collective-permute-done.12.refs_1_.refs_5_), channel_id=1, source_target_pairs={{0,8},{1,9},{2,10},{3,11},{4,12},{5,13},{6,14},{7,15},{8,0},{9,1},... | collective-permute-start | bytes 3538952 | tf_op jit(solution)/shard_map/ppermute | solution.py:80
  194.6 5.0 %collective-permute-start.14 = (bf16[384,3200]{1,0:T(8,128)(2,1)}, bf16[384,3200]{1,0:T(8,128)(2,1)S(1)}, u32[]{:S(2)}, u32[]{:S(2)}) collective-permute-start(bf16[384,3200]{1,0:T(8,128)(2,1)} %get-tuple-element.63), channel_id=1, source_target_pairs={{0,8},{1,9},{2,10},{3,11},{4,12},{5,13},{6,14},{7,15},{8,0},{9,1},... | collective-permute-start | bytes 7372808 | tf_op jit(solution)/shard_map/ppermute | solution.py:80
  202.6 10.1 %collective-permute-start.21 = (bf16[192,896]{1,0:T(8,128)(2,1)S(1)}, bf16[192,896]{1,0:T(8,128)(2,1)S(1)}, u32[]{:S(2)}, u32[]{:S(2)}) collective-permute-start(bf16[192,896]{1,0:T(8,128)(2,1)S(1)} %get-tuple-element.74), channel_id=1, source_target_pairs={{0,2},{1,3},{2,0},{3,1},{4,6},{5,7},{6,4},{7,5},{8,10},{9,11},{10,... | collective-permute-start | bytes 1032200 | tf_op jit(solution)/shard_map/ppermute | solution.py:80
  202.6 26.1 %collective-permute-start.15 = (bf16[96,2304]{1,0:T(8,128)(2,1)S(1)}, bf16[96,2304]{1,0:T(8,128)(2,1)S(1)}, u32[]{:S(2)}, u32[]{:S(2)}) collective-permute-start(bf16[96,2304]{1,0:T(8,128)(2,1)S(1)} %get-tuple-element.65), channel_id=1, source_target_pairs={{0,16},{1,17},{2,18},{3,19},{4,20},{5,21},{6,22},{7,23},{8,24},{9,... | collective-permute-start | bytes 1327112 | tf_op jit(solution)/shard_map/ppermute | solution.py:80
  204.1 24.6 %collective-permute-start.16 = (bf16[96,2304]{1,0:T(8,128)(2,1)S(1)}, bf16[96,2304]{1,0:T(8,128)(2,1)S(1)}, u32[]{:S(2)}, u32[]{:S(2)}) collective-permute-start(bf16[96,2304]{1,0:T(8,128)(2,1)S(1)} %get-tuple-element.66), channel_id=1, source_target_pairs={{0,1},{1,0},{2,3},{3,2},{4,5},{5,4},{6,7},{7,6},{8,9},{9,8},{10,11... | collective-permute-start | bytes 1327112 | tf_op jit(solution)/shard_map/ppermute | solution.py:80
  205.5 23.2 %collective-permute-start.17 = (bf16[96,2304]{1,0:T(8,128)(2,1)S(1)}, bf16[96,2304]{1,0:T(8,128)(2,1)S(1)}, u32[]{:S(2)}, u32[]{:S(2)}) collective-permute-start(bf16[96,2304]{1,0:T(8,128)(2,1)S(1)} %get-tuple-element.67), channel_id=1, source_target_pairs={{0,17},{1,16},{2,19},{3,18},{4,21},{5,20},{6,23},{7,22},{8,25},{9,... | collective-permute-start | bytes 1327112 | tf_op jit(solution)/shard_map/ppermute | solution.py:80
  212.8 14.0 %collective-permute-start.22 = (bf16[96,896]{1,0:T(8,128)(2,1)S(1)}, bf16[96,896]{1,0:T(8,128)(2,1)S(1)}, u32[]{:S(2)}, u32[]{:S(2)}) collective-permute-start(bf16[96,896]{1,0:T(8,128)(2,1)S(1)} %get-tuple-element.76), channel_id=1, source_target_pairs={{0,4},{1,5},{2,6},{3,7},{4,0},{5,1},{6,2},{7,3},{8,12},{9,13},{10,... | collective-permute-start | bytes 516104 | tf_op jit(solution)/shard_map/ppermute | solution.py:80
  227.5 5.9 %collective-permute-start.23 = (bf16[48,896]{1,0:T(8,128)(2,1)S(1)}, bf16[48,896]{1,0:T(8,128)(2,1)S(1)}, u32[]{:S(2)}, u32[]{:S(2)}) collective-permute-start(bf16[48,896]{1,0:T(8,128)(2,1)S(1)} %get-tuple-element.80), channel_id=1, source_target_pairs={{0,1},{1,0},{2,3},{3,2},{4,5},{5,4},{6,7},{7,6},{8,9},{9,8},{10,11... | collective-permute-start | bytes 258056 | tf_op jit(solution)/shard_map/ppermute | solution.py:80
  228.9 13.3 %collective-permute-start.18 = (bf16[24,2304]{1,0:T(8,128)(2,1)S(1)}, bf16[24,2304]{1,0:T(8,128)(2,1)S(1)}, u32[]{:S(2)}, u32[]{:S(2)}) collective-permute-start(bf16[24,2304]{1,0:T(8,128)(2,1)S(1)} %get-tuple-element.70), channel_id=1, source_target_pairs={{0,4},{1,5},{2,6},{3,7},{4,0},{5,1},{6,2},{7,3},{8,12},{9,13},{10,... | collective-permute-start | bytes 331784 | tf_op jit(solution)/shard_map/ppermute | solution.py:80
  231.5 10.6 %collective-permute-start.19 = (bf16[24,2304]{1,0:T(8,128)(2,1)S(1)}, bf16[24,2304]{1,0:T(8,128)(2,1)S(1)}, u32[]{:S(2)}, u32[]{:S(2)}) collective-permute-start(bf16[24,2304]{1,0:T(8,128)(2,1)S(1)} %get-tuple-element.71), channel_id=1, source_target_pairs={{0,2},{1,3},{2,0},{3,1},{4,6},{5,7},{6,4},{7,5},{8,10},{9,11},{10,... | collective-permute-start | bytes 331784 | tf_op jit(solution)/shard_map/ppermute | solution.py:80
  231.8 10.3 %collective-permute-start.20 = (bf16[24,2304]{1,0:T(8,128)(2,1)S(1)}, bf16[24,2304]{1,0:T(8,128)(2,1)S(1)}, u32[]{:S(2)}, u32[]{:S(2)}) collective-permute-start(bf16[24,2304]{1,0:T(8,128)(2,1)S(1)} %get-tuple-element.72), channel_id=1, source_target_pairs={{0,6},{1,7},{2,4},{3,5},{4,2},{5,3},{6,0},{7,1},{8,14},{9,15},{10,... | collective-permute-start | bytes 331784 | tf_op jit(solution)/shard_map/ppermute | solution.py:80
  233.4 8.8 %collective-permute-start.24 = (bf16[24,896]{1,0:T(8,128)(2,1)S(1)}, bf16[24,896]{1,0:T(8,128)(2,1)S(1)}, u32[]{:S(2)}, u32[]{:S(2)}) collective-permute-start(bf16[24,896]{1,0:T(8,128)(2,1)S(1)} %get-tuple-element.82), channel_id=1, source_target_pairs={{0,16},{1,17},{2,18},{3,19},{4,20},{5,21},{6,22},{7,23},{8,24},{9,... | collective-permute-start | bytes 129032 | tf_op jit(solution)/shard_map/ppermute | solution.py:80
  (33 other events, 194.2 us)
